TPU v7x, 32 devices: a whole 2x2x4 slice. The times are simulated.
32 devices in a mesh: dp: 8 (over z, x), expert: 4 (over y, core).
Axes of the slice: x: 2, y: 2, z: 4, core: 2. Of those that a mesh axis runs over, the one named last changes fastest.
Arguments:
- tokens: bfloat16 [32768, 512], P(('dp', 'expert')), may hold values from -6 to 6
- doc_lengths: int32 [32, 4], P(('dp', 'expert')), may hold values from 1 to 512, 1024 in all within a row
- group_order: int32 [32, 1024], P(('dp', 'expert')), may hold values from 0 to 1023, each once within a row
- ln1_gain: float32 [512], replicated, may hold values from 0.5 to 1.5
- w_query: bfloat16 [512, 512], replicated, may hold values from -0.25 to 0.25
- w_key: bfloat16 [512, 512], replicated, may hold values from -0.25 to 0.25
- w_value: bfloat16 [512, 512], replicated, may hold values from -0.25 to 0.25
- w_out: bfloat16 [512, 512], replicated, may hold values from -1 to 1
- ln2_gain: float32 [512], replicated, may hold values from 0.5 to 1.5
- w_control: bfloat16 [512, 8], replicated, may hold values from -0.1875 to 0.1875
- w_up: bfloat16 [8, 512, 2048], P('expert'), may hold values from -1.5 to 1.5
- w_down: bfloat16 [8, 2048, 512], P('expert'), may hold values from -2 to 2
- cotangent: bfloat16 [32768, 512], P(('dp', 'expert')), may hold values from -6 to 6
Outputs:
- output: bfloat16 [32768, 512], P(('dp', 'expert'))
- grad_tokens: bfloat16 [32768, 512], P(('dp', 'expert'))
- grad_ln1_gain: float32 [512], replicated
- grad_w_query: float32 [512, 512], replicated
- grad_w_key: float32 [512, 512], replicated
- grad_w_value: float32 [512, 512], replicated
- grad_w_out: float32 [512, 512], replicated
- grad_ln2_gain: float32 [512], replicated
- grad_w_control: float32 [512, 8], replicated
- grad_w_up: float32 [8, 512, 2048], P('expert', 'dp')
- grad_w_down: float32 [8, 2048, 512], P('expert', 'dp')
Inputs may be any that keep to these rules, and one draw needn't show every extreme that they name: `doc_lengths`: each row holds the lengths of the 4 documents packed in order into one device's 1024 tokens; they sum to 1024 and the longest is exactly 512. `group_order`: each row is a permutation of one device's 1024 token places.
All inputs are finite; a program needn't handle non-finite values.
Results may differ from a plain program's by a relative error of at most 0.02.
Values may be sent and summed in bfloat16 or wider, within the bound.
No kernel may reach another device: no remote copies, remote signals or barrier semaphores. Data moves between devices by JAX's collectives and lax.ppermute only.
A program may use at most 256 MiB of HBM per device.

v0:
```python
import functools

import jax
import jax.numpy as jnp
from jax import lax
from jax.experimental import pallas as pl
from jax.experimental.pallas import tpu as pltpu
from jax.sharding import PartitionSpec as P

D = 512
HEADS = 8
HEAD_DIM = 64
PAIRS = 4
PAIR = 2 * HEAD_DIM
GROUP = 32
EXP_DEV = 2
LONGEST = 512
BLOCK = 256
FF_BLOCK = 512
EPSILON = 1e-05
NEGATIVE = -1e30
MIB = 1 << 20

F32 = jnp.float32
LOW = jnp.bfloat16


def product(left, right):
    return jnp.dot(left, right, preferred_element_type=F32)


def product_nt(left, right):
    return lax.dot_general(left, right, (((1,), (1,)), ((), ())), preferred_element_type=F32)


def product_tn(left, right):
    return lax.dot_general(left, right, (((0,), (0,)), ((), ())), preferred_element_type=F32)


def standard(values):
    center = values - jnp.mean(values, axis=-1, keepdims=True)
    inverse = lax.rsqrt(jnp.mean(center * center, axis=-1, keepdims=True) + EPSILON)
    return center * inverse, inverse


def standard_pull(norm, inverse, grad):
    return (
        grad
        - jnp.mean(grad, axis=-1, keepdims=True)
        - norm * jnp.mean(grad * norm, axis=-1, keepdims=True)
    ) * inverse


def gelu_parts(values):
    square = values * values
    tanh = jnp.tanh(0.7978845608028654 * values * (1.0 + 0.044715 * square))
    half = 0.5 + 0.5 * tanh
    slope = half + values * (0.5 - 0.5 * tanh * tanh) * (
        0.7978845608028654 + 0.10703222440890037 * square
    )
    return values * half, slope


def three_parts(values):
    high = values.astype(LOW).astype(F32)
    rest = values - high
    middle = rest.astype(LOW).astype(F32)
    return high, middle, rest - middle


def begin(copies):
    for copy in copies:
        copy.start()


def finish(copies):
    for copy in copies:
        copy.wait()


def loads(pairs, sems, first=0):
    return [
        pltpu.make_async_copy(source, target, sems.at[first + number])
        for number, (source, target) in enumerate(pairs)
    ]


def widened(w_control, width):
    experts = w_control.shape[0]
    lane = lax.broadcasted_iota(jnp.int32, (experts, width), 1) // (width // experts)
    row = lax.broadcasted_iota(jnp.int32, (experts, width), 0)
    return product_tn(jnp.where(lane == row, 1.0, 0.0).astype(LOW), w_control[...]).astype(LOW)


def forward_kernel(
    place,
    lengths_far,
    order_far,
    gain1_far,
    gain2_far,
    w_control_far,
    tok_far,
    cot_far,
    w_query_far,
    w_key_far,
    w_value_far,
    w_out_far,
    send0,
    send1,
    send2,
    send3,
    hidden_far,
    mix_far,
    normed_far,
    queries_far,
    keys_far,
    values_far,
    attended_far,
    lengths,
    order,
    gain1,
    gain2,
    w_control,
    tok,
    cot,
    w_query,
    w_key,
    w_value,
    w_out,
    hidden,
    mix,
    normed,
    queries,
    keys,
    values,
    attended,
    second,
    spread,
    mixed,
    pulled,
    marked,
    in_sems,
    out_sems,
):
    rows_all = tok.shape[0]
    groups = rows_all // GROUP
    width = mix.shape[1]
    ins = loads(
        [
            (tok_far, tok),
            (gain1_far, gain1),
            (lengths_far, lengths),
            (w_query_far, w_query),
            (w_key_far, w_key),
            (w_value_far, w_value),
            (w_out_far, w_out),
            (gain2_far, gain2),
            (w_control_far, w_control),
            (order_far, order),
            (cot_far, cot),
        ],
        in_sems,
    )
    begin(ins)
    blocks = [pl.ds(start, BLOCK) for start in range(0, rows_all, BLOCK)]
    outs = loads(
        [(normed, normed_far), (keys, keys_far), (values, values_far), (mix, mix_far)], out_sems
    )
    state_outs = loads([(hidden.at[rows], hidden_far.at[rows]) for rows in blocks], out_sems, 4)

    def pair_outs(pair):
        first = 4 + len(blocks)
        two = pl.ds(2 * pair, 2)
        return [
            pltpu.make_async_copy(marked.at[two], queries_far.at[two], out_sems.at[first + pair])
        ]

    attended_out = pltpu.make_async_copy(
        attended, attended_far, out_sems.at[4 + len(blocks) + PAIRS]
    )
    lane = lax.broadcasted_iota(jnp.int32, (BLOCK, PAIR), 1)
    upper = lane >= HEAD_DIM
    slot = lane % HEAD_DIM
    finish(ins[:3])
    end0 = lengths[0, 0]
    end1 = end0 + lengths[0, 1]
    end2 = end1 + lengths[0, 2]
    ones = (slot >= 4) & (slot < 7)
    for number, rows in enumerate(blocks):
        norm, _ = standard(tok[rows, :].astype(F32))
        low = (norm * gain1[...]).astype(LOW)
        normed[rows, :] = low
        places = number * BLOCK + lax.broadcasted_iota(jnp.int32, (BLOCK, PAIR), 0)
        document = (
            (places >= end0).astype(jnp.int32)
            + (places >= end1).astype(jnp.int32)
            + (places >= end2).astype(jnp.int32)
        )
        same = slot == document
        key_marks = jnp.where(same | ones, 1.0, 0.0)
        value_marks = jnp.where(ones, 1.0, 0.0)
        query_marks = jnp.where((slot < 4) & ~same, NEGATIVE, 0.0)
        if number == 0:
            finish(ins[3:6])
        query = product(low, w_query[...]) * (HEAD_DIM ** (-0.5))
        key = product(low, w_key[...])
        value = product(low, w_value[...])
        for pair in range(PAIRS):
            cols = slice(pair * PAIR, (pair + 1) * PAIR)
            for half in range(2):
                mine = upper if half else ~upper
                head = 2 * pair + half
                queries[head, rows, :] = jnp.where(mine, query[:, cols], query_marks).astype(LOW)
                keys[head, rows, :] = jnp.where(mine, key[:, cols], key_marks).astype(LOW)
                values[head, rows, :] = jnp.where(mine, value[:, cols], value_marks).astype(LOW)
    begin(outs[:3])

    triangle = lax.broadcasted_iota(jnp.int32, (BLOCK, BLOCK), 1) <= lax.broadcasted_iota(
        jnp.int32, (BLOCK, BLOCK), 0
    )

    def attend(pair, carry):
        work = [(number, half) for number in range(len(blocks)) for half in range(2)]
        results = {}

        def score(item):
            number, half = item
            start = number * BLOCK
            first = max(0, start - LONGEST)
            head = 2 * pair + half
            query = queries[head, blocks[number], :]
            near = jnp.where(triangle, product_nt(query, keys[head, blocks[number], :]), NEGATIVE)
            far = None
            if start > first:
                far = product_nt(query, keys[head, pl.ds(first, start - first), :])
            return query, near, far

        def weigh(item, scored):
            query, near, far = scored
            top = jnp.max(near, axis=1, keepdims=True)
            if far is not None:
                top = jnp.maximum(top, jnp.max(far, axis=1, keepdims=True))
                far = jnp.exp(far - top).astype(LOW)
            return query, jnp.exp(near - top).astype(LOW), far, top

        def gather(item, weighed):
            number, half = item
            query, near, far, top = weighed
            start = number * BLOCK
            first = max(0, start - LONGEST)
            head = 2 * pair + half
            rows = blocks[number]
            out = product(near, values[head, rows, :])
            if far is not None:
                out = out + product(far, values[head, pl.ds(first, start - first), :])
            mark = 4 + HEAD_DIM * (1 - half)
            total = out[:, mark : mark + 1]
            results[item] = out * (1.0 / total)
            high, middle, rest = three_parts(-(top + jnp.log(total)))
            marks = jnp.where(
                lane == mark, high, jnp.where(lane == mark + 1, middle, rest)
            ).astype(LOW)
            marked[head, rows, :] = jnp.where((lane >= mark) & (lane < mark + 3), marks, query)

        scored, weighed = {}, {}
        for index in range(len(work) + 2):
            if index < len(work):
                scored[index] = score(work[index])
            if 1 <= index <= len(work):
                weighed[index - 1] = weigh(work[index - 1], scored[index - 1])
            if index >= 2:
                gather(work[index - 2], weighed[index - 2])
        cols = pl.ds(pl.multiple_of(pair * PAIR, PAIR), PAIR)
        for number, rows in enumerate(blocks):
            attended[rows, cols] = jnp.where(upper, results[number, 1], results[number, 0]).astype(
                LOW
            )
        begin(pair_outs(pair))
        return carry

    lax.fori_loop(0, PAIRS, attend, 0)
    begin([attended_out])
    finish(ins[6:])

    place_group = lax.broadcasted_iota(jnp.int32, (rows_all, width), 0) // GROUP
    lane_group = lax.broadcasted_iota(jnp.int32, (rows_all, width), 1) % groups
    member = jnp.where(place_group == lane_group, 1.0, 0.0).astype(LOW)
    w_wide = widened(w_control, width)
    tops = []
    for number, rows in enumerate(blocks):
        state = tok[rows, :].astype(F32) + product(attended[rows, :], w_out[...])
        hidden[rows, :] = state
        begin(state_outs[number : number + 1])
        norm, _ = standard(state)
        low = (norm * gain2[...]).astype(LOW)
        second[rows, :] = low
        logits = product_nt(low, w_wide)
        places = number * BLOCK + lax.broadcasted_iota(jnp.int32, (BLOCK, rows_all), 0)
        hot = jnp.where(order[...] == places, 1.0, 0.0).astype(LOW)
        inside = product(hot, member)
        logits = jnp.where(inside > 0.5, logits, NEGATIVE)
        spread[rows, :] = logits
        tops.append(jnp.max(logits, axis=0, keepdims=True))
    top = functools.reduce(jnp.maximum, tops)
    total = 0.0
    for rows in blocks:
        expo = jnp.exp(spread[rows, :] - top)
        spread[rows, :] = expo
        total = total + jnp.sum(expo, axis=0, keepdims=True)
    scale = 1.0 / total
    mixed_sum = 0.0
    pulled_sum = 0.0
    for rows in blocks:
        full = spread[rows, :] * scale
        mix[rows, :] = full
        low = full.astype(LOW)
        mixed_sum = mixed_sum + product_tn(low, second[rows, :])
        pulled_sum = pulled_sum + product_tn(low, cot[rows, :])
    begin(outs[3:])
    mixed[...] = mixed_sum.astype(LOW)
    pulled[...] = pulled_sum.astype(LOW)
    share = EXP_DEV * groups
    for step, send in enumerate((send0, send1, send2, send3)):
        part = pl.ds(pl.multiple_of((place[0] ^ step) * share, share), share)
        send[:share, :] = mixed[part, :]
        send[share:, :] = pulled[part, :]
    finish(outs)
    finish(state_outs)
    for pair in range(PAIRS):
        finish(pair_outs(pair))
    finish([attended_out])


def expert_kernel(in0, in1, in2, in3, up_far, down_far, out0, out1, out2, out3, up, down, sems):
    groups = in0.shape[0] // (2 * EXP_DEV)
    ff = up.shape[2]
    ins = (in0, in1, in2, in3)
    outs = (out0, out1, out2, out3)
    steps = [(expert, first) for expert in range(EXP_DEV) for first in range(0, ff, FF_BLOCK)]
    copies = []
    for number, (expert, first) in enumerate(steps):
        part = pl.ds(first, FF_BLOCK)
        copies.append(
            loads(
                [
                    (up_far.at[expert, :, part], up.at[expert, :, part]),
                    (down_far.at[expert, part], down.at[expert, part]),
                ],
                sems,
                2 * number,
            )
        )
        begin(copies[-1])
    result = pull = 0.0
    for number, (expert, first) in enumerate(steps):
        part = pl.ds(first, FF_BLOCK)
        own = slice(expert * groups, (expert + 1) * groups)
        back = slice((EXP_DEV + expert) * groups, (EXP_DEV + expert + 1) * groups)
        taken = jnp.concatenate([ref[own, :] for ref in ins], axis=0)
        given = jnp.concatenate([ref[back, :] for ref in ins], axis=0)
        finish(copies[number])
        act, slope = gelu_parts(product(taken, up[expert, :, part]))
        grad = (product_nt(given, down[expert, part, :]) * slope).astype(LOW)
        result = result + product(act.astype(LOW), down[expert, part, :])
        pull = pull + product_nt(grad, up[expert, :, part])
        if first + FF_BLOCK == ff:
            for host, ref in enumerate(outs):
                rows = slice(host * groups, (host + 1) * groups)
                ref[own, :] = result[rows].astype(LOW)
                ref[back, :] = pull[rows].astype(LOW)
            result = pull = 0.0


def middle_kernel(
    place,
    near,
    ret0,
    ret1,
    ret2,
    ret3,
    gain2_far,
    w_control_far,
    hidden_far,
    cot_far,
    mix_far,
    attended_far,
    w_out_far,
    output_far,
    grad_hidden_far,
    pulls_far,
    mine_out,
    other_out,
    gain2,
    w_control,
    hidden,
    cot,
    mix,
    attended,
    w_out,
    output,
    grad_hidden,
    pulls,
    result,
    pull,
    second,
    inner,
    grad_attn,
    grad_out,
    in_sems,
    out_sems,
):
    rows_all = hidden.shape[0]
    groups = rows_all // GROUP
    share = EXP_DEV * groups
    blocks = [pl.ds(start, BLOCK) for start in range(0, rows_all, BLOCK)]
    ins = loads(
        [
            (gain2_far, gain2),
            (w_control_far, w_control),
            (mix_far, mix),
            (hidden_far, hidden),
            (cot_far, cot),
            (w_out_far, w_out),
            (attended_far, attended),
        ],
        in_sems,
    )
    begin(ins)
    outs = loads([(output.at[rows], output_far.at[rows]) for rows in blocks], out_sems)
    state_outs = loads(
        [(grad_hidden.at[rows], grad_hidden_far.at[rows]) for rows in blocks],
        out_sems,
        len(blocks),
    )
    pull_outs = loads(
        [(pulls.at[:, rows], pulls_far.at[:, rows]) for rows in blocks],
        out_sems,
        2 * len(blocks),
    )
    lane = lax.broadcasted_iota(jnp.int32, (BLOCK, PAIR), 1)
    upper = lane >= HEAD_DIM
    slot = lane % HEAD_DIM
    crossed = (lax.broadcasted_iota(jnp.int32, (PAIR, PAIR), 0) >= HEAD_DIM) != (
        lax.broadcasted_iota(jnp.int32, (PAIR, PAIR), 1) >= HEAD_DIM
    )
    crossing = jnp.where(crossed, -1.0, 0.0).astype(LOW)
    for step, ret in enumerate((ret0, ret1, ret2, ret3)):
        part = pl.ds(pl.multiple_of((place[0] ^ step) * share, share), share)
        result[part, :] = ret[:share, :]
        pull[part, :] = ret[share:, :]
    finish(ins[:5])
    total = 0.0
    for number, rows in enumerate(blocks):
        state = hidden[rows, :]
        norm, _ = standard(state)
        low = (norm * gain2[...]).astype(LOW)
        second[rows, :] = low
        full = mix[rows, :]
        output[rows, :] = (state + product(full.astype(LOW), result[...])).astype(LOW)
        begin(outs[number : number + 1])
        grad_mix = product_nt(cot[rows, :], result[...]) + product_nt(low, pull[...])
        weighted = full * grad_mix
        inner[rows, :] = weighted
        total = total + jnp.sum(weighted, axis=0, keepdims=True)
    finish(ins[5:])
    w_wide = widened(w_control, mix.shape[1])
    control = 0.0
    gain = 0.0
    for number, rows in enumerate(blocks):
        full = mix[rows, :]
        grad_logits = (inner[rows, :] - full * total).astype(LOW)
        grad_second = product(full.astype(LOW), pull[...]) + product(grad_logits, w_wide)
        control = control + product_tn(grad_logits, second[rows, :])
        norm, inverse = standard(hidden[rows, :])
        gain = gain + jnp.sum(grad_second * norm, axis=0, keepdims=True)
        grad_state = cot[rows, :].astype(F32) + standard_pull(
            norm, inverse, grad_second * gain2[...]
        )
        grad_hidden[rows, :] = grad_state
        begin(state_outs[number : number + 1])
        low = grad_state.astype(LOW)
        grad_attn[rows, :] = low
        grad_att = product_nt(low, w_out[...]).astype(LOW).astype(F32)
        shared = grad_att * attended[rows, :].astype(F32)
        for pair in range(PAIRS):
            cols = slice(pair * PAIR, (pair + 1) * PAIR)
            top = shared[:, cols].astype(LOW)
            rest = (shared[:, cols] - top.astype(F32)).astype(LOW)
            delta = product(top, crossing) + product(rest, crossing)
            high, middle, last = three_parts(delta)
            marks = jnp.where(
                slot == 4,
                high,
                jnp.where(slot == 5, middle, jnp.where(slot == 6, last, 0.0)),
            )
            for half in range(2):
                mine = upper if half else ~upper
                pulls[2 * pair + half, rows, :] = jnp.where(mine, grad_att[:, cols], marks).astype(
                    LOW
                )
        begin(pull_outs[number : number + 1])
    grad_out[:, :D] = product_tn(attended[...], grad_attn[...]).astype(LOW)
    experts = control.shape[0] // groups
    small = jnp.concatenate(
        (
            jnp.sum(control.reshape(experts, groups, D), axis=1),
            jnp.broadcast_to(gain, (PAIR - experts, D)),
        ),
        axis=0,
    )
    grad_out[:, D:] = small.T.astype(LOW)
    half = D // 2
    mine_out[...] = grad_out[pl.ds(pl.multiple_of(near[0] * half, half), half), :]
    other_out[...] = grad_out[pl.ds(pl.multiple_of((1 - near[0]) * half, half), half), :]
    finish(outs)
    finish(state_outs)
    finish(pull_outs)


def pair_kernel(
    near,
    queries_far,
    keys_far,
    values_far,
    pulls_far,
    normed_far,
    grads_far,
    mine_out,
    other_out,
    queries,
    keys,
    values,
    pulls,
    normed,
    grads,
    grad_query,
    weights,
    in_sems,
    out_sems,
):
    rows_all = normed.shape[0]
    lane = lax.broadcasted_iota(jnp.int32, (BLOCK, PAIR), 1)
    upper = lane >= HEAD_DIM
    triangle = lax.broadcasted_iota(jnp.int32, (BLOCK, BLOCK), 0) <= lax.broadcasted_iota(
        jnp.int32, (BLOCK, BLOCK), 1
    )

    def ins(pair):
        two = pl.ds(2 * pair, 2)
        return loads(
            [
                (keys_far.at[two], keys.at[two]),
                (queries_far.at[two], queries.at[two]),
                (values_far.at[two], values.at[two]),
                (pulls_far.at[two], pulls.at[two]),
            ],
            in_sems,
            4 * pair,
        )

    def outs(pair):
        return loads([(grads.at[pair], grads_far.at[pair])], out_sems, pair)

    begin(ins(0))
    norm_in = loads([(normed_far, normed)], in_sems, 4 * PAIRS)
    begin(ins(1))
    begin(norm_in)
    for pair in range(2, PAIRS):
        begin(ins(pair))

    def one_pair(pair, carry):
        finish(ins(pair))
        work = [(start, half) for start in range(0, rows_all, BLOCK) for half in range(2)]
        seen = set()
        halves = {}

        def score(item):
            start, half = item
            head = 2 * pair + half
            rows = pl.ds(start, BLOCK)
            key, value = keys[head, rows, :], values[head, rows, :]
            parts = [rows]
            if start + BLOCK < rows_all:
                after = min(rows_all, start + BLOCK + LONGEST) - (start + BLOCK)
                parts.append(pl.ds(start + BLOCK, after))
            made = []
            for number, part in enumerate(parts):
                scores = product_nt(key, queries[head, part, :])
                if number == 0:
                    scores = jnp.where(triangle, scores, NEGATIVE)
                made.append((part, scores, product_nt(value, pulls[head, part, :])))
            return key, made

        def weigh(scored):
            key, made = scored
            done = []
            for part, scores, grad_probs in made:
                probs = jnp.exp(scores)
                done.append((part, probs.astype(LOW), (probs * grad_probs).astype(LOW)))
            return key, done

        def gather(item, weighed):
            start, half = item
            head = 2 * pair + half
            key, done = weighed
            key = jnp.where(upper if half else ~upper, key, jnp.zeros_like(key))
            grad_key = 0.0
            grad_value = 0.0
            for part, probs, grad_scores in done:
                grad_value = grad_value + product(probs, pulls[head, part, :])
                grad_key = grad_key + product(grad_scores, queries[head, part, :])
                both = product_tn(grad_scores, key)
                for offset in range(0, part.size, BLOCK):
                    at = part.start + offset
                    piece = both[offset : offset + BLOCK]
                    if at in seen:
                        grad_query[pl.ds(at, BLOCK), :] += piece
                    else:
                        grad_query[pl.ds(at, BLOCK), :] = piece
                        seen.add(at)
            halves[start, half] = grad_key, grad_value
            if half == 1:
                rows = pl.ds(start, BLOCK)
                grads[pair, rows, PAIR : 2 * PAIR] = jnp.where(
                    upper, halves[start, 1][0], halves[start, 0][0]
                ).astype(LOW)
                grads[pair, rows, 2 * PAIR :] = jnp.where(
                    upper, halves[start, 1][1], halves[start, 0][1]
                ).astype(LOW)

        scored, weighed = {}, {}
        for index in range(len(work) + 2):
            if index < len(work):
                scored[index] = score(work[index])
            if 1 <= index <= len(work):
                weighed[index - 1] = weigh(scored[index - 1])
            if index >= 2:
                gather(work[index - 2], weighed[index - 2])
        grads[pair, :, :PAIR] = (grad_query[...] * (HEAD_DIM ** (-0.5))).astype(LOW)
        begin(outs(pair))

        @pl.when(pair == 0)
        def _():
            finish(norm_in)

        cols = pl.ds(pl.multiple_of(pair * 3 * PAIR, PAIR), 3 * PAIR)
        weights[:, cols] = product_tn(normed[...], grads[pair]).astype(LOW)
        return carry

    lax.fori_loop(0, PAIRS, one_pair, 0)
    half = D // 2
    mine_out[...] = weights[pl.ds(pl.multiple_of(near[0] * half, half), half), :]
    other_out[...] = weights[pl.ds(pl.multiple_of((1 - near[0]) * half, half), half), :]
    for pair in range(PAIRS):
        finish(outs(pair))


def last_kernel(grads, tok, grad_hidden, gain1, w_query, w_key, w_value, grad_tokens):
    parts = [grads[pair] for pair in range(PAIRS)]
    grad_normed = 0.0
    for number, weight in enumerate((w_query, w_key, w_value)):
        cols = slice(number * PAIR, (number + 1) * PAIR)
        joined = jnp.concatenate([part[:, cols] for part in parts], axis=1)
        grad_normed = grad_normed + product_nt(joined, weight[...])
    norm, inverse = standard(tok[...].astype(F32))
    grad_tokens[...] = (
        grad_hidden[...] + standard_pull(norm, inverse, grad_normed * gain1[...])
    ).astype(LOW)


def weight_kernel(expert, count, place, *refs):
    pieces = refs[:count]
    up, down = refs[count : count + 2]
    grad_up, grad_down, taken, given, held = refs[-5:]
    step = pl.program_id(0)
    share = PAIR
    groups = share // (2 * EXP_DEV)
    strip_rows, strip_ff = grad_up.shape[1], grad_down.shape[1]
    first = place[0] * strip_rows
    wide = pl.multiple_of(first // PAIR * PAIR, PAIR)
    inside = pl.ds(pl.multiple_of(first % PAIR, strip_rows), strip_rows)

    @pl.when(step == 0)
    def _():
        filled = 0
        for piece in pieces:
            for start in range(0, piece.shape[0], share):
                target = pl.ds(filled, groups)
                taken[target, :] = piece[
                    start + expert * groups : start + (expert + 1) * groups, :
                ]
                back = start + (EXP_DEV + expert) * groups
                given[target, :] = piece[back : back + groups, :]
                filled += groups

    rows_all = taken.shape[0]
    size = min(512, rows_all)
    ff_first = place[0] * strip_ff
    owner = step == ff_first // FF_BLOCK
    total = 0.0
    acts = []
    for start in range(0, rows_all, size):
        rows = pl.ds(start, size)
        act, slope = gelu_parts(product(taken[rows, :], up[0]))
        grad = (product_nt(given[rows, :], down[0]) * slope).astype(LOW)
        total = total + product_tn(taken[rows, pl.ds(wide, PAIR)], grad)
        acts.append(act.astype(LOW))
    held[:PAIR, :] = total
    grad_up[0] = held[inside, :]

    @pl.when(owner)
    def _():
        whole = 0.0
        for number, act in enumerate(acts):
            whole = whole + product_tn(act, given[pl.ds(number * size, size), :])
        held[...] = whole
        grad_down[0] = held[pl.ds(pl.multiple_of(ff_first % FF_BLOCK, strip_ff), strip_ff), :]


def join_kernel(mine_out, swapped_out, mine, swapped, sums):
    first = mine_out.shape[1]
    sums[:, :first] = (mine_out[...].astype(F32) + swapped_out[...].astype(F32)).astype(LOW)
    sums[:, first:] = (mine[...].astype(F32) + swapped[...].astype(F32)).astype(LOW)


def total_kernel(parts, spread):
    total = parts[0].astype(F32)
    for number in range(1, parts.shape[0]):
        total = total + parts[number].astype(F32)
    total = total.astype(LOW)
    for number in range(parts.shape[0]):
        spread[number] = total


def assemble_kernel(
    near,
    both_own,
    both_other,
    gain1_far,
    w_query_far,
    w_key_far,
    w_value_far,
    grad_query_far,
    grad_key_far,
    grad_value_far,
    grad_out_far,
    grad_control,
    grad_gain1,
    grad_gain2,
    gain1,
    weights,
    squares,
    columns,
    in_sems,
    out_sems,
):
    ins = loads(
        [
            (gain1_far, gain1),
            (w_query_far, weights.at[0]),
            (w_key_far, weights.at[1]),
            (w_value_far, weights.at[2]),
        ],
        in_sems,
    )
    begin(ins)
    half = D // 2
    experts = grad_control.shape[0]
    targets = (grad_query_far, grad_key_far, grad_value_far, grad_out_far)
    lane = lax.broadcasted_iota(jnp.int32, (half, PAIR), 1)
    outs = []
    for step, both in enumerate((both_own, both_other)):
        side = near[0] if step == 0 else 1 - near[0]
        rows = pl.ds(pl.multiple_of(side * half, half), half)
        outs.append(
            loads(
                [
                    (squares.at[number, rows], target.at[rows])
                    for number, target in enumerate(targets)
                ],
                out_sems,
                len(targets) * step,
            )
        )
        squares[3, rows, :] = both[:, :D].astype(F32)
        begin(outs[-1][3:])
        if step == 0:
            finish(ins)
        shared = 0.0
        for number in range(3):
            for pair in range(PAIRS):
                first = D + PAIR + (3 * pair + number) * PAIR
                part = both[:, first : first + PAIR].astype(F32)
                cols = slice(pair * PAIR, (pair + 1) * PAIR)
                squares[number, rows, cols] = part
                shared = shared + part * weights[number, rows, cols].astype(F32)
            begin(outs[-1][number : number + 1])
        columns[rows, :] = jnp.where(
            lane == experts + 1,
            jnp.sum(shared, axis=1, keepdims=True),
            both[:, D : D + PAIR].astype(F32),
        )
    turned = columns[...].T
    grad_control[...] = turned[:experts]
    grad_gain2[...] = turned[experts : experts + 1]
    grad_gain1[...] = turned[experts + 1 : experts + 2] / gain1[...]
    for one in outs:
        finish(one)


def vmem():
    return pl.BlockSpec(memory_space=pltpu.VMEM)


def smem():
    return pl.BlockSpec(memory_space=pltpu.SMEM)


def far():
    return pl.BlockSpec(memory_space=pltpu.HBM)


def shape(*sizes, kind=LOW):
    return jax.ShapeDtypeStruct(sizes, kind)


def params(mib):
    return pltpu.CompilerParams(vmem_limit_bytes=mib * MIB)


def cost(flops, moved):
    return pl.CostEstimate(flops=int(flops), bytes_accessed=int(moved), transcendentals=0)


def ring_of(count):
    order = list(range(0, count, 2)) + list(range(count - 1, 0, -2))
    ahead = [(order[i], order[(i + 1) % count]) for i in range(count)]
    return ahead, [(target, source) for source, target in ahead]


def dma(count):
    return pltpu.SemaphoreType.DMA((count,))


def forward_call(lengths, place, order, gain1, gain2, tokens, cot, weights, w_control, experts):
    rows = tokens.shape[0]
    groups = rows // GROUP
    wide = experts * groups
    blocks = rows // BLOCK
    heads = (HEADS, rows, PAIR)
    kept = [
        ((rows, D), F32),
        ((rows, wide), F32),
        ((rows, D), LOW),
        (heads, LOW),
        (heads, LOW),
        (heads, LOW),
        ((rows, D), LOW),
    ]
    results = pl.pallas_call(
        forward_kernel,
        in_specs=[smem()] + [far()] * 11,
        out_specs=[vmem()] * 4 + [far()] * 7,
        out_shape=[shape(2 * EXP_DEV * groups, D)] * 4
        + [shape(*size, kind=kind) for size, kind in kept],
        scratch_shapes=[
            pltpu.SMEM(lengths.shape, jnp.int32),
            pltpu.VMEM(order.shape, jnp.int32),
            pltpu.VMEM((1, D), F32),
            pltpu.VMEM((1, D), F32),
            pltpu.VMEM((experts, D), LOW),
        ]
        + [pltpu.VMEM((rows, D), LOW)] * 2
        + [pltpu.VMEM((D, D), LOW)] * 4
        + [pltpu.VMEM(*one) for one in kept]
        + [
            pltpu.VMEM((rows, D), LOW),
            pltpu.VMEM((rows, wide), F32),
            pltpu.VMEM((wide, D), LOW),
            pltpu.VMEM((wide, D), LOW),
            pltpu.VMEM(heads, LOW),
            dma(11),
            dma(4 + blocks + PAIRS + 1),
        ],
        compiler_params=params(56),
        cost_estimate=cost(2e10, 2e7),
    )(place, lengths, order, gain1, gain2, w_control, tokens, cot, *weights)
    return results[:4], results[4:]


def expert_call(arrived, w_up, w_down):
    size, _ = arrived[0].shape
    steps = EXP_DEV * w_up.shape[2] // FF_BLOCK
    return pl.pallas_call(
        expert_kernel,
        in_specs=[vmem()] * len(arrived) + [far()] * 2,
        out_specs=[vmem()] * len(arrived),
        out_shape=[shape(size, D)] * len(arrived),
        scratch_shapes=[
            pltpu.VMEM(w_up.shape, LOW),
            pltpu.VMEM(w_down.shape, LOW),
            dma(2 * steps),
        ],
        compiler_params=params(56),
        cost_estimate=cost(5e9, 1e7),
    )(*arrived, w_up, w_down)


def middle_call(place, near, returned, gain2, w_control, hidden, cot, mix, attended, w_out):
    rows, wide = mix.shape
    blocks = rows // BLOCK
    taken = [
        ((rows, D), F32),
        ((rows, D), LOW),
        ((rows, wide), F32),
        ((rows, D), LOW),
        ((D, D), LOW),
    ]
    made = [((rows, D), LOW), ((rows, D), F32), ((HEADS, rows, PAIR), LOW)]
    part = shape(D // 2, D + PAIR)
    return pl.pallas_call(
        middle_kernel,
        in_specs=[smem()] * 2 + [vmem()] * 4 + [far()] * 7,
        out_specs=[far()] * 3 + [vmem()] * 2,
        out_shape=[shape(*size, kind=kind) for size, kind in made] + [part, part],
        scratch_shapes=[pltpu.VMEM((1, D), F32), pltpu.VMEM(w_control.shape, LOW)]
        + [pltpu.VMEM(*one) for one in taken + made]
        + [
            pltpu.VMEM((wide, D), LOW),
            pltpu.VMEM((wide, D), LOW),
            pltpu.VMEM((rows, D), LOW),
            pltpu.VMEM((rows, wide), F32),
            pltpu.VMEM((rows, D), LOW),
            pltpu.VMEM((D, D + PAIR), LOW),
            dma(7),
            dma(3 * blocks),
        ],
        compiler_params=params(52),
        cost_estimate=cost(8e9, 1.5e7),
    )(place, near, *returned, gain2, w_control, hidden, cot, mix, attended, w_out)


def pair_call(near, queries, keys, values, pulls, normed):
    rows = normed.shape[0]
    half = shape(D // 2, 3 * PAIRS * PAIR)
    return pl.pallas_call(
        pair_kernel,
        in_specs=[smem()] + [far()] * 5,
        out_specs=[far()] + [vmem()] * 2,
        out_shape=[shape(PAIRS, rows, 3 * PAIR), half, half],
        scratch_shapes=[pltpu.VMEM((HEADS, rows, PAIR), LOW)] * 4
        + [
            pltpu.VMEM((rows, D), LOW),
            pltpu.VMEM((PAIRS, rows, 3 * PAIR), LOW),
            pltpu.VMEM((rows, PAIR), F32),
            pltpu.VMEM((D, 3 * PAIRS * PAIR), LOW),
            dma(4 * PAIRS + 1),
            dma(PAIRS),
        ],
        compiler_params=params(56),
        cost_estimate=cost(2e10, 1.2e7),
    )(near, queries, keys, values, pulls, normed)


def weight_call(expert, copy, pieces, w_up, w_down, copies, earlier):
    ff = w_up.shape[2]
    held = sum(piece.shape[0] for piece in pieces)
    every = held // (2 * EXP_DEV)
    whole = [pl.BlockSpec(one.shape, lambda f: (0, 0)) for one in pieces]
    return pl.pallas_call(
        functools.partial(weight_kernel, expert, len(pieces)),
        grid=(ff // FF_BLOCK,),
        in_specs=[smem()]
        + whole
        + [
            pl.BlockSpec((1, D, FF_BLOCK), lambda f: (expert, 0, f)),
            pl.BlockSpec((1, FF_BLOCK, D), lambda f: (expert, f, 0)),
        ]
        + [far()] * len(earlier),
        out_specs=[
            pl.BlockSpec((1, D // copies, FF_BLOCK), lambda f: (expert, 0, f)),
            pl.BlockSpec((1, ff // copies, D), lambda f: (expert, 0, 0)),
        ],
        out_shape=[
            shape(EXP_DEV, D // copies, ff, kind=F32),
            shape(EXP_DEV, ff // copies, D, kind=F32),
        ],
        scratch_shapes=[
            pltpu.VMEM((every, D), LOW),
            pltpu.VMEM((every, D), LOW),
            pltpu.VMEM((FF_BLOCK, D), F32),
        ],
        input_output_aliases={3 + len(pieces) + i: i for i in range(len(earlier))},
        compiler_params=params(52),
        cost_estimate=cost(1e10, 8e6),
    )(copy, *pieces, w_up, w_down, *earlier)


def last_call(grads, tokens, grad_hidden, gain1, weights):
    rows = tokens.shape[0]
    row_block = lambda i: (i, 0)
    fixed = lambda i: (0, 0)
    return pl.pallas_call(
        last_kernel,
        grid=(rows // BLOCK,),
        in_specs=[pl.BlockSpec((PAIRS, BLOCK, 3 * PAIR), lambda i: (0, i, 0))]
        + [pl.BlockSpec((BLOCK, D), row_block)] * 2
        + [pl.BlockSpec((1, D), fixed)]
        + [pl.BlockSpec((D, D), fixed)] * 3,
        out_specs=pl.BlockSpec((BLOCK, D), row_block),
        out_shape=shape(rows, D),
        compiler_params=params(52),
        cost_estimate=cost(2e9, 8e6),
    )(grads, tokens, grad_hidden, gain1, *weights)


def join_call(*parts):
    rows = parts[0].shape[0]
    return pl.pallas_call(
        join_kernel,
        in_specs=[vmem()] * 4,
        out_specs=vmem(),
        out_shape=shape(rows, parts[0].shape[1] + parts[2].shape[1]),
        compiler_params=params(16),
        cost_estimate=cost(1e6, 3e6),
    )(*parts)


def total_call(parts):
    return pl.pallas_call(
        total_kernel,
        in_specs=[vmem()],
        out_specs=vmem(),
        out_shape=shape(*parts.shape),
        compiler_params=params(16),
        cost_estimate=cost(1e6, 3e6),
    )(parts)


def assemble_call(near, both_own, both_other, gain1, weights, experts):
    square = shape(D, D, kind=F32)
    return pl.pallas_call(
        assemble_kernel,
        in_specs=[smem()] + [vmem()] * 2 + [far()] * 4,
        out_specs=[far()] * 4 + [vmem()] * 3,
        out_shape=[square] * 4 + [shape(experts, D, kind=F32)] + [shape(1, D, kind=F32)] * 2,
        scratch_shapes=[
            pltpu.VMEM((1, D), F32),
            pltpu.VMEM((3, D, D), LOW),
            pltpu.VMEM((4, D, D), F32),
            pltpu.VMEM((D, PAIR), F32),
            dma(4),
            dma(8),
        ],
        compiler_params=params(40),
        cost_estimate=cost(1e8, 6e6),
    )(near, both_own, both_other, gain1, *weights)


def in_order(*values):
    return lax.optimization_barrier(values)


def shards(
    tokens,
    doc_lengths,
    group_order,
    ln1_gain,
    w_query,
    w_key,
    w_value,
    w_out,
    ln2_gain,
    w_control,
    w_up,
    w_down,
    cotangent,
):
    copies, far_hosts, near_hosts = (lax.axis_size(name) for name in ("dp", "far", "near"))
    hosts = far_hosts * near_hosts
    hosts_axes = ("far", "near")
    axes = ("dp", "far")
    count = copies * far_hosts
    experts = hosts * EXP_DEV
    place = lax.axis_index(hosts_axes).astype(jnp.int32).reshape(1)
    near = lax.axis_index("near").astype(jnp.int32).reshape(1)
    copy = lax.axis_index("dp").astype(jnp.int32).reshape(1)
    gain1 = ln1_gain.reshape(1, D)
    gain2 = ln2_gain.reshape(1, D)
    weights = (w_query, w_key, w_value)
    w_control = w_control.T
    ahead, behind = ring_of(copies)
    steps_left = copies // 2 - 1
    pieces = []

    def exchange(parts):
        return [parts[0]] + [
            lax.ppermute(parts[step], hosts_axes, [(i, i ^ step) for i in range(hosts)])
            for step in range(1, hosts)
        ]

    def pass_on(ahead_part, behind_part):
        return lax.ppermute(ahead_part, "dp", ahead), lax.ppermute(behind_part, "dp", behind)

    def next_step(moving):
        nonlocal steps_left
        pieces.extend(moving)
        steps_left -= 1
        if steps_left > 0:
            return pass_on(*moving)
        half = moving[0].shape[0] // 2
        return pass_on(moving[0][:half], moving[1][half:])

    def near_swap(values):
        return lax.ppermute(values, "near", [(i, i ^ 1) for i in range(near_hosts)])

    def scatter(half):
        rows, cols = half.shape
        return lax.all_to_all(half.reshape(count, rows // count, cols), axes, 0, 0, tiled=True)

    def spread(own):
        return lax.all_to_all(own, axes, 0, 0, tiled=True).reshape(-1, own.shape[-1])

    with jax.named_scope("attention_and_mixing"):
        sends, kept = forward_call(
            doc_lengths,
            place,
            group_order,
            gain1,
            gain2,
            tokens,
            cotangent,
            (*weights, w_out),
            w_control,
            experts,
        )
        hidden, mix, normed, queries, keys, values, attended = kept
    with jax.named_scope("to_experts"):
        arrived = exchange(sends)
    with jax.named_scope("gather_for_weights"):
        own = jnp.concatenate(arrived, axis=0)
        pieces.append(own)
        moving = pass_on(own, own)
    with jax.named_scope("experts"):
        results = expert_call(arrived, w_up, w_down)
    with jax.named_scope("from_experts"):
        returned = exchange(results)
    with jax.named_scope("gather_for_weights"):
        moving = next_step(moving)
    with jax.named_scope("mixing_backward"):
        output, grad_hidden, pulls, mine_out, other_out = middle_call(
            place, near, returned, gain2, w_control, hidden, cotangent, mix, attended, w_out
        )
    with jax.named_scope("gather_for_weights"):
        pulls, other_out, moving = in_order(pulls, other_out, moving)
        moving = next_step(moving)
    with jax.named_scope("reduce"):
        swapped_out = near_swap(other_out)
    with jax.named_scope("attention_backward"):
        grads, mine, other = pair_call(near, queries, keys, values, pulls, normed)
        mine, other, moving, swapped_out = in_order(mine, other, moving, swapped_out)
    with jax.named_scope("gather_for_weights"):
        while steps_left > 0:
            moving = next_step(moving)
    with jax.named_scope("reduce"):
        sums = join_call(mine_out, swapped_out, mine, near_swap(other))
        sums, grads, moving = in_order(sums, grads, moving)
        pieces.extend(moving)
        sums = scatter(sums)
    with jax.named_scope("norm_backward"):
        grad_tokens = last_call(grads, tokens, grad_hidden, gain1, weights)
    with jax.named_scope("expert_weights"):
        grads_expert = weight_call(0, copy, pieces, w_up, w_down, copies, ())
        sums, grads_expert, grad_tokens = in_order(sums, grads_expert, grad_tokens)
    with jax.named_scope("reduce"):
        sums = total_call(sums)
        sums, grads_expert = in_order(sums, grads_expert)
        sums = spread(sums)
    with jax.named_scope("expert_weights"):
        grad_up, grad_down = weight_call(1, copy, pieces, w_up, w_down, copies, grads_expert)
        sums, grad_up, grad_down = in_order(sums, grad_up, grad_down)
    with jax.named_scope("reduce"):
        sums_other = near_swap(sums)
    with jax.named_scope("assemble"):
        grad_query, grad_key, grad_value, grad_out, grad_control, grad_gain1, grad_gain2 = (
            assemble_call(near, sums, sums_other, gain1, weights, experts)
        )
    return (
        output,
        grad_tokens,
        grad_gain1.reshape(D),
        grad_query,
        grad_key,
        grad_value,
        grad_out,
        grad_gain2.reshape(D),
        grad_control.T,
        grad_up,
        grad_down,
    )


def solution(mesh):
    copies, hosts = mesh.shape["dp"], mesh.shape["expert"]
    finer = jax.sharding.Mesh(mesh.devices.reshape(copies, hosts // 2, 2), ("dp", "far", "near"))
    every = P(("dp", "far", "near"), None)
    expert = P(("far", "near"), None, None)
    sliced = P(("far", "near"), "dp", None)
    return jax.shard_map(
        shards,
        mesh=finer,
        in_specs=(every,) * 3 + (P(),) * 7 + (expert,) * 2 + (every,),
        out_specs=(every,) * 2 + (P(),) * 7 + (sliced,) * 2,
        check_vma=False,
    )
```

profile of v0, /device:TPU:11, one launch (start us, length us, event | category | flops | bytes accessed | tf_op | source)
XLA Modules:
  0.0 158.6 jit_solution(8771420942158506134)
XLA Ops:
  0.7 18.4 %attention_and_mixing.1 = (bf16[128,512]{1,0:T(8,128)(2,1)}, bf16[128,512]{1,0:T(8,128)(2,1)}, bf16[128,512]{1,0:T(8,128)(2,1)}, bf16[128,512]{1,0:T(8,128)(2,1)...) custom-call(s32[1]{0:T(128)} %bitcast.place, ...), custom_call_target="tpu_custom_call" | custom-call | flops 20000000000 | bytes 20000000 | tf_op jit(solution)/shard_map/attention_and_mixing/pallas_call | solution.py:860
  19.1 0.7 collective-permute-start
  19.8 1.3 collective-permute-start.1
  21.0 0.5 collective-permute-start.2
  21.5 0.9 constant_dynamic-update-slice_fusion.3
  22.4 0.0 collective-permute-done.in1
  22.4 0.0 copy-start.17
  22.5 2.6 %collective-permute-done.1.in2 = bf16[128,512]{1,0:T(8,128)(2,1)S(1)} collective-permute-done((bf16[128,512]{1,0:T(8,128)(2,1)}, bf16[128,512]{1,0:T(8,128)(2,1)S(1)}, u32[]{:S(2)}, u32[]{:S(2)}) %collective-permute-start.1) | collective-permute-done | bytes 131104 | tf_op jit(solution)/shard_map/to_experts/ppermute | solution.py:1098
  25.1 3.0 %collective-permute-done.2.in3 = bf16[128,512]{1,0:T(8,128)(2,1)S(1)} collective-permute-done((bf16[128,512]{1,0:T(8,128)(2,1)}, bf16[128,512]{1,0:T(8,128)(2,1)S(1)}, u32[]{:S(2)}, u32[]{:S(2)}) %collective-permute-start.2) | collective-permute-done | bytes 131104 | tf_op jit(solution)/shard_map/to_experts/ppermute | solution.py:1098
  28.1 0.0 copy-start.5
  28.1 0.0 copy-start.12
  28.1 0.0 copy-start.13
  28.1 0.2 collective-permute-start.6
  28.3 1.4 collective-permute-start.8
  29.7 0.0 copy-done.19
  29.7 8.5 %experts.1 = (bf16[128,512]{1,0:T(8,128)(2,1)}, bf16[128,512]{1,0:T(8,128)(2,1)}, bf16[128,512]{1,0:T(8,128)(2,1)}, bf16[128,512]{1,0:T(8,128)(2,1)}) custom-call(bf16[128,512]{1,0:T(8,128)(2,1)} %get-tuple-element.68.in0, bf16[128,512]{1,0:T(8,128)(2,1)} %copy-done.17, bf16[128,512]{1,0:T(8,128)(2,1)} %copy-done.18, bf16[128,512]{1,0:T(8,128)(2,1)} %copy-done.19, ...), custom_call_target="tpu_custom_call" | custom-call | flops 5000000000 | bytes 10000000 | tf_op jit(solution)/shard_map/experts/pallas_call | solution.py:894
  38.2 0.8 collective-permute-start.3
  39.0 1.3 collective-permute-start.4
  40.3 0.5 collective-permute-start.5
  40.7 0.7 collective-permute-done.6.refs_1_
  41.4 0.2 collective-permute-start.7
  41.6 0.0 collective-permute-done.8.refs_2_
  41.6 1.3 collective-permute-start.9
  42.9 0.0 collective-permute-done.3.ret1
  42.9 1.4 collective-permute-done.4.ret2
  44.3 3.3 %collective-permute-done.5.ret3 = bf16[128,512]{1,0:T(8,128)(2,1)S(1)} collective-permute-done((bf16[128,512]{1,0:T(8,128)(2,1)}, bf16[128,512]{1,0:T(8,128)(2,1)S(1)}, u32[]{:S(2)}, u32[]{:S(2)}) %collective-permute-start.5) | collective-permute-done | bytes 131104 | tf_op jit(solution)/shard_map/from_experts/ppermute | solution.py:1098
  47.6 0.0 copy-done.13
  47.6 0.0 copy-start.14
  47.6 0.9 copy-done.14
  48.5 8.4 %mixing_backward.1 = (bf16[1024,512]{1,0:T(8,128)(2,1)}, f32[1024,512]{1,0:T(8,128)}, bf16[8,1024,128]{2,1,0:T(8,128)(2,1)}, bf16[256,640]{1,0:T(8,128)(2,1)S(1)}, bf16[256,640]{1,0:T(8,128)(2,1)S(1)}) custom-call(s32[1]{0:T(128)} %bitcast.place, s32[1]{0:T(128)} %bitcast.1.near, bf16[128,512]{1,0:T(8,128)(2,1)S(1)} %copy-done.14, ...), custom_call_target="tpu_custom_call" | custom-call | flops 8000000000 | bytes 15000000 | tf_op jit(solution)/shard_map/mixing_backward/pallas_call | solution.py:921
  56.9 0.0 collective-permute-done.7.refs_3_
  56.9 0.0 copy-start.21
  56.9 0.0 collective-permute-done.9.refs_4_
  56.9 0.2 collective-permute-start.10
  57.1 1.4 collective-permute-start.11
  58.6 0.4 collective-permute-start.12
  58.9 19.0 %attention_backward.1 = (bf16[4,1024,384]{2,1,0:T(8,128)(2,1)}, bf16[256,1536]{1,0:T(8,128)(2,1)}, bf16[256,1536]{1,0:T(8,128)(2,1)}) custom-call(s32[1]{0:T(128)} %bitcast.1.near, bf16[8,1024,128]{2,1,0:T(8,128)(2,1)} %get-tuple-element.81.queries_far, bf16[8,1024,128]{2,1,0:T(8,128)(2,1)} %get-tuple-element.82.keys_far, ...), custom_call_target="tpu_custom_call" | custom-call | flops 20000000000 | bytes 12000000 | tf_op jit(solution)/shard_map/attention_backward/pallas_call | solution.py:946
  78.0 0.0 collective-permute-done.12.swapped_out
  78.0 0.0 collective-permute-done.10.refs_5_
  78.0 0.0 collective-permute-done.11.refs_6_
  78.0 0.2 collective-permute-start.13
  78.2 0.2 collective-permute-start.14
  78.5 1.4 collective-permute-start.15
  79.8 0.7 collective-permute-done.13.swapped
  80.6 1.1 copy-done.3
  81.7 1.3 reduce.2
  83.0 2.8 %collective-permute-done.14.refs_7_ = bf16[256,512]{1,0:T(8,128)(2,1)S(1)} collective-permute-done((bf16[256,512]{1,0:T(8,128)(2,1)S(1)}, bf16[256,512]{1,0:T(8,128)(2,1)S(1)}, u32[]{:S(2)}, u32[]{:S(2)}) %collective-permute-start.14) | collective-permute-done | bytes 262176 | tf_op jit(solution)/shard_map/gather_for_weights/ppermute | solution.py:1103
  85.8 0.0 collective-permute-done.15.refs_8_
  85.8 0.7 copy-done.9
  86.5 6.6 %all-to-all-start = ((bf16[16,16,2176]{2,1,0:T(8,128)(2,1)}), bf16[16,16,2176]{2,1,0:T(8,128)(2,1)S(1)}, u32[]{:S(2)}, u32[]{:S(2)}) async-start(bf16[16,16,2176]{2,1,0:T(8,128)(2,1)} %bitcast.5), calls=%async_computation | async-start | bytes 2228224 | tf_op jit(solution)/shard_map/reduce/all_to_all | solution.py:1119
  93.1 0.0 copy-start.7
  93.1 0.0 copy-start.10
  93.1 6.0 %norm_backward.1 = bf16[1024,512]{1,0:T(8,128)(2,1)} custom-call(bf16[4,1024,384]{2,1,0:T(8,128)(2,1)} %get-tuple-element.104.grads, bf16[1024,512]{1,0:T(8,128)(2,1)} %tok.1, f32[1024,512]{1,0:T(8,128)} %get-tuple-element.105.grad_hidden, f32[1,512]{1,0:T(1,128)S(1)} %bitcast.14, bf16[512,512]{1,0:T(8,128)(2,1)S(1)} %copy-done, ...), custom_call_target="tpu_custom_call" | custom-call | flops 2000000000 | bytes 8000000 | tf_op jit(solution)/shard_map/norm_backward/pallas_call | solution.py:1003
  99.1 11.9 %expert_weights.2 = (f32[2,64,2048]{2,1,0:T(8,128)}, f32[2,256,512]{2,1,0:T(8,128)}) custom-call(s32[1]{0:T(128)} %bitcast.6.place, bf16[512,512]{1,0:T(8,128)(2,1)S(1)} %constant_dynamic-update-slice_fusion.refs_0_, bf16[512,512]{1,0:T(8,128)(2,1)S(1)} %copy-done.7, bf16[512,512]{1,0:T(8,128)(2,1)} %copy-done.20, bf16[512,512]{1,0:T(8,128)(2,1)} %copy-done.21, ...), custom_call_target="tpu_custom_call" | custom-call | flops 10000000000 | bytes 8000000 | tf_op jit(solution)/shard_map/expert_weights/pallas_call | solution.py:970
  111.0 8.2 %all-to-all-done.parts = bf16[16,16,2176]{2,1,0:T(8,128)(2,1)S(1)} async-done(((bf16[16,16,2176]{2,1,0:T(8,128)(2,1)}), bf16[16,16,2176]{2,1,0:T(8,128)(2,1)S(1)}, u32[]{:S(2)}, u32[]{:S(2)}) %all-to-all-start) | async-done | bytes 1114144 | tf_op jit(solution)/shard_map/reduce/all_to_all | solution.py:1119
  119.2 1.2 reduce.3
  120.4 4.0 %all-to-all-start.1 = ((bf16[16,16,2176]{2,1,0:T(8,128)(2,1)}), bf16[16,16,2176]{2,1,0:T(8,128)(2,1)S(1)}, u32[]{:S(2)}, u32[]{:S(2)}) async-start(bf16[16,16,2176]{2,1,0:T(8,128)(2,1)} %reduce.3), calls=%async_computation.1 | async-start | bytes 2228224 | tf_op jit(solution)/shard_map/reduce/all_to_all | solution.py:1122
  124.4 1.0 copy-done.8
  125.4 0.9 copy-done.11
  126.3 11.9 %expert_weights.3 = (f32[2,64,2048]{2,1,0:T(8,128)}, f32[2,256,512]{2,1,0:T(8,128)}) custom-call(s32[1]{0:T(128)} %bitcast.6.place, bf16[512,512]{1,0:T(8,128)(2,1)S(1)} %constant_dynamic-update-slice_fusion.refs_0_, bf16[512,512]{1,0:T(8,128)(2,1)S(1)} %copy-done.8, bf16[512,512]{1,0:T(8,128)(2,1)} %copy-done.20, ...), custom_call_target="tpu_custom_call", output_to_operand_aliasing={{0}: (12, {}), {1}: (13, {})} | custom-call | flops 10000000000 | bytes 8000000 | tf_op jit(solution)/shard_map/expert_weights/pallas_call | solution.py:970
  138.3 12.2 %all-to-all-done.1 = bf16[16,16,2176]{2,1,0:T(8,128)(2,1)S(1)} async-done(((bf16[16,16,2176]{2,1,0:T(8,128)(2,1)}), bf16[16,16,2176]{2,1,0:T(8,128)(2,1)S(1)}, u32[]{:S(2)}, u32[]{:S(2)}) %all-to-all-start.1) | async-done | bytes 1114144 | tf_op jit(solution)/shard_map/reduce/all_to_all | solution.py:1122
  150.5 2.5 %collective-permute-start.16 = (bf16[256,2176]{1,0:T(8,128)(2,1)S(1)}, bf16[256,2176]{1,0:T(8,128)(2,1)S(1)}, u32[]{:S(2)}, u32[]{:S(2)}) collective-permute-start(bf16[256,2176]{1,0:T(8,128)(2,1)S(1)} %bitcast.11), channel_id=1, source_target_pairs={{0,1},{1,0},{2,3},{3,2},{4,5},{5,4},{6,7},{7,6},{8,9},{9,8},{10,11... | collective-permute-start | bytes 3342344 | tf_op jit(solution)/shard_map/reduce/ppermute | solution.py:1115
  153.0 2.4 %collective-permute-done.16.both_other = bf16[256,2176]{1,0:T(8,128)(2,1)S(1)} collective-permute-done((bf16[256,2176]{1,0:T(8,128)(2,1)S(1)}, bf16[256,2176]{1,0:T(8,128)(2,1)S(1)}, u32[]{:S(2)}, u32[]{:S(2)}) %collective-permute-start.16) | collective-permute-done | bytes 1114144 | tf_op jit(solution)/shard_map/reduce/ppermute | solution.py:1115
  155.4 3.1 %assemble.1 = (f32[512,512]{1,0:T(8,128)}, f32[512,512]{1,0:T(8,128)}, f32[512,512]{1,0:T(8,128)}, f32[512,512]{1,0:T(8,128)}, f32[8,512]{1,0:T(8,128)}, /*index=5*/f32[1,512]{1,0:T(1,128)}, f32[1,512]{1,0:T(1,128)}) custom-call(s32[1]{0:T(128)} %bitcast.1.near, bf16[256,2176]{1,0:T(8,128)(2,1)S(1)} %bitcast.12, ...), custom_call_target="tpu_custom_call" | custom-call | flops 100000000 | bytes 6000000 | tf_op jit(solution)/shard_map/assemble/pallas_call | solution.py:1042
  (36 shorter events, 0.1 us)
Async XLA Ops:
  19.1 3.4 %collective-permute-start = (bf16[128,512]{1,0:T(8,128)(2,1)}, bf16[128,512]{1,0:T(8,128)(2,1)S(1)}, u32[]{:S(2)}, u32[]{:S(2)}) collective-permute-start(bf16[128,512]{1,0:T(8,128)(2,1)} %get-tuple-element.69), channel_id=1, source_target_pairs={{0,1},{1,0},{2,3},{3,2},{4,5},{5,4},{6,7},{7,6},{8,9},{9,8},{10,11... | collective-permute-start | bytes 393224 | tf_op jit(solution)/shard_map/to_experts/ppermute | solution.py:1098
  19.8 5.3 %collective-permute-start.1 = (bf16[128,512]{1,0:T(8,128)(2,1)}, bf16[128,512]{1,0:T(8,128)(2,1)S(1)}, u32[]{:S(2)}, u32[]{:S(2)}) collective-permute-start(bf16[128,512]{1,0:T(8,128)(2,1)} %get-tuple-element.70), channel_id=1, source_target_pairs={{0,2},{1,3},{2,0},{3,1},{4,6},{5,7},{6,4},{7,5},{8,10},{9,11},{10,... | collective-permute-start | bytes 393224 | tf_op jit(solution)/shard_map/to_experts/ppermute | solution.py:1098
  21.0 7.0 %collective-permute-start.2 = (bf16[128,512]{1,0:T(8,128)(2,1)}, bf16[128,512]{1,0:T(8,128)(2,1)S(1)}, u32[]{:S(2)}, u32[]{:S(2)}) collective-permute-start(bf16[128,512]{1,0:T(8,128)(2,1)} %get-tuple-element.71), channel_id=1, source_target_pairs={{0,3},{1,2},{2,1},{3,0},{4,7},{5,6},{6,5},{7,4},{8,11},{9,10},{10,... | collective-permute-start | bytes 393224 | tf_op jit(solution)/shard_map/to_experts/ppermute | solution.py:1098
  22.4 7.3 %copy-start.17 = (bf16[128,512]{1,0:T(8,128)(2,1)}, bf16[128,512]{1,0:T(8,128)(2,1)S(1)}, u32[]{:S(2)}) copy-start(bf16[128,512]{1,0:T(8,128)(2,1)S(1)} %collective-permute-done.in1) | copy-start | bytes 393220
  25.1 4.6 %copy-start.18 = (bf16[128,512]{1,0:T(8,128)(2,1)}, bf16[128,512]{1,0:T(8,128)(2,1)S(1)}, u32[]{:S(2)}) copy-start(bf16[128,512]{1,0:T(8,128)(2,1)S(1)} %collective-permute-done.1.in2) | copy-start | bytes 393220
  28.0 1.7 %copy-start.19 = (bf16[128,512]{1,0:T(8,128)(2,1)}, bf16[128,512]{1,0:T(8,128)(2,1)S(1)}, u32[]{:S(2)}) copy-start(bf16[128,512]{1,0:T(8,128)(2,1)S(1)} %collective-permute-done.2.in3) | copy-start | bytes 393220
  28.1 19.5 %copy-start.5 = (bf16[512,512]{1,0:T(8,128)(2,1)S(1)}, bf16[512,512]{1,0:T(8,128)(2,1)}, u32[]{:S(2)}) copy-start(bf16[512,512]{1,0:T(8,128)(2,1)} %w_out_far.3) | copy-start | bytes 1572868
  28.1 19.5 %copy-start.12 = (bf16[512,8]{0,1:T(8,128)(2,1)S(1)}, bf16[512,8]{0,1:T(8,128)(2,1)}, u32[]{:S(2)}) copy-start(bf16[512,8]{0,1:T(8,128)(2,1)} %param.22) | copy-start | bytes 24580
  28.1 19.5 %copy-start.13 = (f32[512]{0:T(512)S(1)}, f32[512]{0:T(512)}, u32[]{:S(2)}) copy-start(f32[512]{0:T(512)} %param.21) | copy-start | bytes 6148
  28.1 13.3 %collective-permute-start.6 = (bf16[512,512]{1,0:T(8,128)(2,1)S(1)}, bf16[512,512]{1,0:T(8,128)(2,1)S(1)}, u32[]{:S(2)}, u32[]{:S(2)}) collective-permute-start(bf16[512,512]{1,0:T(8,128)(2,1)S(1)} %constant_dynamic-update-slice_fusion.refs_0_), channel_id=1, source_target_pairs={{0,8},{8,16},{16,24},{24,28},{28,20},{20,12},{12,4},{4,0},{1,9},{9... | collective-permute-start | bytes 1572872 | tf_op jit(solution)/shard_map/gather_for_weights/ppermute | solution.py:1103
  28.3 13.3 %collective-permute-start.8 = (bf16[512,512]{1,0:T(8,128)(2,1)S(1)}, bf16[512,512]{1,0:T(8,128)(2,1)S(1)}, u32[]{:S(2)}, u32[]{:S(2)}) collective-permute-start(bf16[512,512]{1,0:T(8,128)(2,1)S(1)} %constant_dynamic-update-slice_fusion.refs_0_), channel_id=1, source_target_pairs={{8,0},{16,8},{24,16},{28,24},{20,28},{12,20},{4,12},{0,4},{9,1},{1... | collective-permute-start | bytes 1572872 | tf_op jit(solution)/shard_map/gather_for_weights/ppermute | solution.py:1103
  38.2 4.7 %collective-permute-start.3 = (bf16[128,512]{1,0:T(8,128)(2,1)}, bf16[128,512]{1,0:T(8,128)(2,1)S(1)}, u32[]{:S(2)}, u32[]{:S(2)}) collective-permute-start(bf16[128,512]{1,0:T(8,128)(2,1)} %get-tuple-element.73), channel_id=1, source_target_pairs={{0,1},{1,0},{2,3},{3,2},{4,5},{5,4},{6,7},{7,6},{8,9},{9,8},{10,11... | collective-permute-start | bytes 393224 | tf_op jit(solution)/shard_map/from_experts/ppermute | solution.py:1098
  39.0 5.3 %collective-permute-start.4 = (bf16[128,512]{1,0:T(8,128)(2,1)}, bf16[128,512]{1,0:T(8,128)(2,1)S(1)}, u32[]{:S(2)}, u32[]{:S(2)}) collective-permute-start(bf16[128,512]{1,0:T(8,128)(2,1)} %get-tuple-element.74), channel_id=1, source_target_pairs={{0,2},{1,3},{2,0},{3,1},{4,6},{5,7},{6,4},{7,5},{8,10},{9,11},{10,... | collective-permute-start | bytes 393224 | tf_op jit(solution)/shard_map/from_experts/ppermute | solution.py:1098
  40.3 7.3 %collective-permute-start.5 = (bf16[128,512]{1,0:T(8,128)(2,1)}, bf16[128,512]{1,0:T(8,128)(2,1)S(1)}, u32[]{:S(2)}, u32[]{:S(2)}) collective-permute-start(bf16[128,512]{1,0:T(8,128)(2,1)} %get-tuple-element.75), channel_id=1, source_target_pairs={{0,3},{1,2},{2,1},{3,0},{4,7},{5,6},{6,5},{7,4},{8,11},{9,10},{10,... | collective-permute-start | bytes 393224 | tf_op jit(solution)/shard_map/from_experts/ppermute | solution.py:1098
  41.4 15.4 %copy-start.6 = (bf16[512,512]{1,0:T(8,128)(2,1)}, bf16[512,512]{1,0:T(8,128)(2,1)S(1)}, u32[]{:S(2)}) copy-start(bf16[512,512]{1,0:T(8,128)(2,1)S(1)} %collective-permute-done.6.refs_1_) | copy-start | bytes 1572868
  41.4 15.4 %collective-permute-start.7 = (bf16[512,512]{1,0:T(8,128)(2,1)S(1)}, bf16[512,512]{1,0:T(8,128)(2,1)S(1)}, u32[]{:S(2)}, u32[]{:S(2)}) collective-permute-start(bf16[512,512]{1,0:T(8,128)(2,1)S(1)} %collective-permute-done.6.refs_1_), channel_id=1, source_target_pairs={{0,8},{8,16},{16,24},{24,28},{28,20},{20,12},{12,4},{4,0},{1,9},{9... | collective-permute-start | bytes 1572872 | tf_op jit(solution)/shard_map/gather_for_weights/ppermute | solution.py:1103
  41.6 15.2 %copy-start.20 = (bf16[512,512]{1,0:T(8,128)(2,1)}, bf16[512,512]{1,0:T(8,128)(2,1)S(1)}, u32[]{:S(2)}) copy-start(bf16[512,512]{1,0:T(8,128)(2,1)S(1)} %collective-permute-done.8.refs_2_) | copy-start | bytes 1572868
  41.6 15.3 %collective-permute-start.9 = (bf16[512,512]{1,0:T(8,128)(2,1)S(1)}, bf16[512,512]{1,0:T(8,128)(2,1)S(1)}, u32[]{:S(2)}, u32[]{:S(2)}) collective-permute-start(bf16[512,512]{1,0:T(8,128)(2,1)S(1)} %collective-permute-done.8.refs_2_), channel_id=1, source_target_pairs={{8,0},{16,8},{24,16},{28,24},{20,28},{12,20},{4,12},{0,4},{9,1},{1... | collective-permute-start | bytes 1572872 | tf_op jit(solution)/shard_map/gather_for_weights/ppermute | solution.py:1103
  47.6 0.9 copy-start.14
  56.9 21.1 %copy-start.21 = (bf16[512,512]{1,0:T(8,128)(2,1)}, bf16[512,512]{1,0:T(8,128)(2,1)S(1)}, u32[]{:S(2)}) copy-start(bf16[512,512]{1,0:T(8,128)(2,1)S(1)} %collective-permute-done.7.refs_3_) | copy-start | bytes 1572868
  56.9 21.1 %copy-start.22 = (bf16[512,512]{1,0:T(8,128)(2,1)}, bf16[512,512]{1,0:T(8,128)(2,1)S(1)}, u32[]{:S(2)}) copy-start(bf16[512,512]{1,0:T(8,128)(2,1)S(1)} %collective-permute-done.9.refs_4_) | copy-start | bytes 1572868
  56.9 21.1 %collective-permute-start.10 = (bf16[512,512]{1,0:T(8,128)(2,1)S(1)}, bf16[512,512]{1,0:T(8,128)(2,1)S(1)}, u32[]{:S(2)}, u32[]{:S(2)}) collective-permute-start(bf16[512,512]{1,0:T(8,128)(2,1)S(1)} %collective-permute-done.7.refs_3_), channel_id=1, source_target_pairs={{0,8},{8,16},{16,24},{24,28},{28,20},{20,12},{12,4},{4,0},{1,9},{9... | collective-permute-start | bytes 1572872 | tf_op jit(solution)/shard_map/gather_for_weights/ppermute | solution.py:1103
  57.1 20.9 %collective-permute-start.11 = (bf16[512,512]{1,0:T(8,128)(2,1)S(1)}, bf16[512,512]{1,0:T(8,128)(2,1)S(1)}, u32[]{:S(2)}, u32[]{:S(2)}) collective-permute-start(bf16[512,512]{1,0:T(8,128)(2,1)S(1)} %collective-permute-done.9.refs_4_), channel_id=1, source_target_pairs={{8,0},{16,8},{24,16},{28,24},{20,28},{12,20},{4,12},{0,4},{9,1},{1... | collective-permute-start | bytes 1572872 | tf_op jit(solution)/shard_map/gather_for_weights/ppermute | solution.py:1103
  58.6 19.4 %collective-permute-start.12 = (bf16[256,640]{1,0:T(8,128)(2,1)S(1)}, bf16[256,640]{1,0:T(8,128)(2,1)S(1)}, u32[]{:S(2)}, u32[]{:S(2)}) collective-permute-start(bf16[256,640]{1,0:T(8,128)(2,1)S(1)} %get-tuple-element.92), channel_id=1, source_target_pairs={{0,1},{1,0},{2,3},{3,2},{4,5},{5,4},{6,7},{7,6},{8,9},{9,8},{10,11... | collective-permute-start | bytes 983048 | tf_op jit(solution)/shard_map/reduce/ppermute | solution.py:1115
  78.0 5.0 %copy-start.15 = (bf16[512,512]{1,0:T(8,128)(2,1)}, bf16[512,512]{1,0:T(8,128)(2,1)S(1)}, u32[]{:S(2)}) copy-start(bf16[512,512]{1,0:T(8,128)(2,1)S(1)} %collective-permute-done.10.refs_5_) | copy-start | bytes 1572868
  78.0 5.0 %copy-start.16 = (bf16[512,512]{1,0:T(8,128)(2,1)}, bf16[512,512]{1,0:T(8,128)(2,1)S(1)}, u32[]{:S(2)}) copy-start(bf16[512,512]{1,0:T(8,128)(2,1)S(1)} %collective-permute-done.11.refs_6_) | copy-start | bytes 1572868
  78.0 2.6 %collective-permute-start.13 = (bf16[256,1536]{1,0:T(8,128)(2,1)}, bf16[256,1536]{1,0:T(8,128)(2,1)S(1)}, u32[]{:S(2)}, u32[]{:S(2)}) collective-permute-start(bf16[256,1536]{1,0:T(8,128)(2,1)} %get-tuple-element.95), channel_id=1, source_target_pairs={{0,1},{1,0},{2,3},{3,2},{4,5},{5,4},{6,7},{7,6},{8,9},{9,8},{10,11... | collective-permute-start | bytes 2359304 | tf_op jit(solution)/shard_map/reduce/ppermute | solution.py:1115
  78.2 7.6 %collective-permute-start.14 = (bf16[256,512]{1,0:T(8,128)(2,1)S(1)}, bf16[256,512]{1,0:T(8,128)(2,1)S(1)}, u32[]{:S(2)}, u32[]{:S(2)}) collective-permute-start(bf16[256,512]{1,0:T(8,128)(2,1)S(1)} %slice.6), channel_id=1, source_target_pairs={{0,8},{8,16},{16,24},{24,28},{28,20},{20,12},{12,4},{4,0},{1,9},{9... | collective-permute-start | bytes 786440 | tf_op jit(solution)/shard_map/gather_for_weights/ppermute | solution.py:1103
  78.5 7.3 %collective-permute-start.15 = (bf16[256,512]{1,0:T(8,128)(2,1)S(1)}, bf16[256,512]{1,0:T(8,128)(2,1)S(1)}, u32[]{:S(2)}, u32[]{:S(2)}) collective-permute-start(bf16[256,512]{1,0:T(8,128)(2,1)S(1)} %slice.7), channel_id=1, source_target_pairs={{8,0},{16,8},{24,16},{28,24},{20,28},{12,20},{4,12},{0,4},{9,1},{1... | collective-permute-start | bytes 786440 | tf_op jit(solution)/shard_map/gather_for_weights/ppermute | solution.py:1103
  80.6 1.1 copy-start.3
  81.7 11.4 %copy-start = (bf16[512,512]{1,0:T(8,128)(2,1)S(1)}, bf16[512,512]{1,0:T(8,128)(2,1)}, u32[]{:S(2)}) copy-start(bf16[512,512]{1,0:T(8,128)(2,1)} %w_query_far.3) | copy-start | bytes 1572868
  81.7 11.4 %copy-start.1 = (bf16[512,512]{1,0:T(8,128)(2,1)S(1)}, bf16[512,512]{1,0:T(8,128)(2,1)}, u32[]{:S(2)}) copy-start(bf16[512,512]{1,0:T(8,128)(2,1)} %w_key_far.3) | copy-start | bytes 1572868
  81.7 11.4 %copy-start.2 = (bf16[512,512]{1,0:T(8,128)(2,1)S(1)}, bf16[512,512]{1,0:T(8,128)(2,1)}, u32[]{:S(2)}) copy-start(bf16[512,512]{1,0:T(8,128)(2,1)} %w_value_far.3) | copy-start | bytes 1572868
  81.7 11.4 %copy-start.4 = (f32[512]{0:T(512)S(1)}, f32[512]{0:T(512)}, u32[]{:S(2)}) copy-start(f32[512]{0:T(512)} %param.16) | copy-start | bytes 6148
  85.8 0.7 copy-start.9
  86.5 32.7 %all-to-all-start = ((bf16[16,16,2176]{2,1,0:T(8,128)(2,1)}), bf16[16,16,2176]{2,1,0:T(8,128)(2,1)S(1)}, u32[]{:S(2)}, u32[]{:S(2)}) async-start(bf16[16,16,2176]{2,1,0:T(8,128)(2,1)} %bitcast.5), calls=%async_computation | async-start | bytes 2228224 | tf_op jit(solution)/shard_map/reduce/all_to_all | solution.py:1119
  93.1 6.0 %copy-start.7 = (bf16[512,512]{1,0:T(8,128)(2,1)S(1)}, bf16[512,512]{1,0:T(8,128)(2,1)}, u32[]{:S(2)}) copy-start(bf16[512,512]{1,0:T(8,128)(2,1)} %copy-done.6) | copy-start | bytes 1572868
  93.1 6.0 %copy-start.10 = (bf16[256,512]{1,0:T(8,128)(2,1)S(1)}, bf16[256,512]{1,0:T(8,128)(2,1)}, u32[]{:S(2)}) copy-start(bf16[256,512]{1,0:T(8,128)(2,1)} %copy-done.9) | copy-start | bytes 786436
  120.4 30.1 %all-to-all-start.1 = ((bf16[16,16,2176]{2,1,0:T(8,128)(2,1)}), bf16[16,16,2176]{2,1,0:T(8,128)(2,1)S(1)}, u32[]{:S(2)}, u32[]{:S(2)}) async-start(bf16[16,16,2176]{2,1,0:T(8,128)(2,1)} %reduce.3), calls=%async_computation.1 | async-start | bytes 2228224 | tf_op jit(solution)/shard_map/reduce/all_to_all | solution.py:1122
  124.4 1.0 copy-start.8
  125.4 0.9 copy-start.11
  150.5 4.9 %collective-permute-start.16 = (bf16[256,2176]{1,0:T(8,128)(2,1)S(1)}, bf16[256,2176]{1,0:T(8,128)(2,1)S(1)}, u32[]{:S(2)}, u32[]{:S(2)}) collective-permute-start(bf16[256,2176]{1,0:T(8,128)(2,1)S(1)} %bitcast.11), channel_id=1, source_target_pairs={{0,1},{1,0},{2,3},{3,2},{4,5},{5,4},{6,7},{7,6},{8,9},{9,8},{10,11... | collective-permute-start | bytes 3342344 | tf_op jit(solution)/shard_map/reduce/ppermute | solution.py:1115
where the time goes:
time: 159 us
  Pallas kernels  89.6 us (56%)
  waiting for transfers between devices  37.3 us (23%)
  starting transfers between devices  24.8 us (16%)
  local copies, waits for them, and re-layouts  5.79 us (4%)
    pallas_call x2, Pallas kernels, weight_call(): pl.pallas_call(functools.partial(weight_kernel, expert, len(pieces)), gri...  23.8 us
    pallas_call x1, Pallas kernels, pair_call(): pl.pallas_call(pair_kernel, in_specs=[smem()] + [far()] * 5, out_specs=[f...  19 us
    pallas_call x1, Pallas kernels, forward_call(): pl.pallas_call(forward_kernel, in_specs=[smem()] + [far()] * 11, out_spec...  18.4 us
    all_to_all x1, waiting for transfers between devices, spread(): lax.all_to_all(own, axes, 0, 0, tiled=True).reshape(-1, own.shape[-1])  12.2 us
    ppermute x6, waiting for transfers between devices, exchange(): lax.ppermute(parts[step], hosts_axes, [(i, i ^ step) for i in range(hosts)])  10.2 us
    pallas_call x1, Pallas kernels, expert_call(): pl.pallas_call(expert_kernel, in_specs=[vmem()] * len(arrived) + [far()]...  8.52 us
    pallas_call x1, Pallas kernels, middle_call(): pl.pallas_call(middle_kernel, in_specs=[smem()] * 2 + [vmem()] * 4 + [far...  8.36 us
    all_to_all x1, waiting for transfers between devices, scatter(): lax.all_to_all(half.reshape(count, rows // count, cols), axes, 0, 0, tile...  8.19 us
  transfers between devices with their start and end apart: 19, of which 10 were waited for; matrix products, arithmetic and copies ran while one was open for 1% of the time, Pallas kernels for 42%

commit v1 on v0

--- a/solution.py
+++ b/solution.py
@@ -331,34 +331,19 @@
     finish([attended_out])
 
 
-def expert_kernel(in0, in1, in2, in3, up_far, down_far, out0, out1, out2, out3, up, down, sems):
+def expert_kernel(in0, in1, in2, in3, up, down, out0, out1, out2, out3):
     groups = in0.shape[0] // (2 * EXP_DEV)
     ff = up.shape[2]
     ins = (in0, in1, in2, in3)
     outs = (out0, out1, out2, out3)
     steps = [(expert, first) for expert in range(EXP_DEV) for first in range(0, ff, FF_BLOCK)]
-    copies = []
-    for number, (expert, first) in enumerate(steps):
-        part = pl.ds(first, FF_BLOCK)
-        copies.append(
-            loads(
-                [
-                    (up_far.at[expert, :, part], up.at[expert, :, part]),
-                    (down_far.at[expert, part], down.at[expert, part]),
-                ],
-                sems,
-                2 * number,
-            )
-        )
-        begin(copies[-1])
     result = pull = 0.0
-    for number, (expert, first) in enumerate(steps):
+    for expert, first in steps:
         part = pl.ds(first, FF_BLOCK)
         own = slice(expert * groups, (expert + 1) * groups)
         back = slice((EXP_DEV + expert) * groups, (EXP_DEV + expert + 1) * groups)
         taken = jnp.concatenate([ref[own, :] for ref in ins], axis=0)
         given = jnp.concatenate([ref[back, :] for ref in ins], axis=0)
-        finish(copies[number])
         act, slope = gelu_parts(product(taken, up[expert, :, part]))
         grad = (product_nt(given, down[expert, part, :]) * slope).astype(LOW)
         result = result + product(act.astype(LOW), down[expert, part, :])
@@ -882,7 +867,7 @@
             dma(11),
             dma(4 + blocks + PAIRS + 1),
         ],
-        compiler_params=params(56),
+        compiler_params=pltpu.CompilerParams(vmem_limit_bytes=56623104),
         cost_estimate=cost(2e10, 2e7),
     )(place, lengths, order, gain1, gain2, w_control, tokens, cot, *weights)
     return results[:4], results[4:]
@@ -890,18 +875,12 @@
 
 def expert_call(arrived, w_up, w_down):
     size, _ = arrived[0].shape
-    steps = EXP_DEV * w_up.shape[2] // FF_BLOCK
     return pl.pallas_call(
         expert_kernel,
-        in_specs=[vmem()] * len(arrived) + [far()] * 2,
+        in_specs=[vmem()] * (len(arrived) + 2),
         out_specs=[vmem()] * len(arrived),
         out_shape=[shape(size, D)] * len(arrived),
-        scratch_shapes=[
-            pltpu.VMEM(w_up.shape, LOW),
-            pltpu.VMEM(w_down.shape, LOW),
-            dma(2 * steps),
-        ],
-        compiler_params=params(56),
+        compiler_params=params(16),
         cost_estimate=cost(5e9, 1e7),
     )(*arrived, w_up, w_down)
 

time: 159 us -> 158 us (level)
  Pallas kernels: 89.6 us -> 85.6 us
  starting transfers between devices: 24.8 us -> 27.1 us
    ppermute x4, waiting for transfers between devices: 3.56 us -> 8.01 us  [pass_on(): lax.ppermute(ahead_part, 'dp', ahead)]
    pallas_call x1, Pallas kernels: 8.52 us -> 4.44 us  [expert_call(): pl.pallas_call(expert_kernel, in_specs=[vmem()] * (len(arrived) + 2), out...]
    ppermute x6, waiting for transfers between devices: 10.2 us -> 6.55 us  [exchange(): lax.ppermute(parts[step], hosts_axes, [(i, i ^ step) for i in range(hosts)])]
    ppermute x3, starting transfers between devices: 3.06 us -> 5.22 us  [near_swap(): return lax.ppermute(values, 'near', [(i, i ^ 1) for i in range(near_hosts)])]
    unnamed x49 -> x47, local copies, waits for them, and re-layouts: 5.74 us -> 5.73 us
  transfers between devices with their start and end apart: 19 -> 19, of which waited for: 10 -> 10; matrix products, arithmetic and copies ran while one was open for 1% -> 1% of each run, Pallas kernels for 42% -> 40%
where the time goes in v1:
time: 158 us
  Pallas kernels  85.6 us (54%)
  waiting for transfers between devices  38.2 us (24%)
  starting transfers between devices  27.1 us (17%)
  local copies, waits for them, and re-layouts  5.78 us (4%)
    pallas_call x2, Pallas kernels, weight_call(): pl.pallas_call(functools.partial(weight_kernel, expert, len(pieces)), gri...  23.8 us
    pallas_call x1, Pallas kernels, pair_call(): pl.pallas_call(pair_kernel, in_specs=[smem()] + [far()] * 5, out_specs=[f...  19 us
    pallas_call x1, Pallas kernels, forward_call(): pl.pallas_call(forward_kernel, in_specs=[smem()] + [far()] * 11, out_spec...  18.5 us
    all_to_all x1, waiting for transfers between devices, spread(): lax.all_to_all(own, axes, 0, 0, tiled=True).reshape(-1, own.shape[-1])  12.2 us
    pallas_call x1, Pallas kernels, middle_call(): pl.pallas_call(middle_kernel, in_specs=[smem()] * 2 + [vmem()] * 4 + [far...  8.33 us
    all_to_all x1, waiting for transfers between devices, scatter(): lax.all_to_all(half.reshape(count, rows // count, cols), axes, 0, 0, tile...  8.17 us
    ppermute x4, waiting for transfers between devices, pass_on(): lax.ppermute(ahead_part, 'dp', ahead)  8.01 us
    all_to_all x1, starting transfers between devices, scatter(): lax.all_to_all(half.reshape(count, rows // count, cols), axes, 0, 0, tile...  6.79 us
  transfers between devices with their start and end apart: 19, of which 10 were waited for; matrix products, arithmetic and copies ran while one was open for 1% of the time, Pallas kernels for 40%

profile of v1, /device:TPU:11, one launch (start us, length us, event | category | flops | bytes accessed | tf_op | source)
XLA Modules:
  0.0 157.8 jit_solution(6478650330053776046)
XLA Ops:
  0.7 0.0 copy-start.6
  0.7 0.0 copy-start.7
  0.7 18.5 %attention_and_mixing.1 = (bf16[128,512]{1,0:T(8,128)(2,1)}, bf16[128,512]{1,0:T(8,128)(2,1)}, bf16[128,512]{1,0:T(8,128)(2,1)}, bf16[128,512]{1,0:T(8,128)(2,1)...) custom-call(s32[1]{0:T(128)} %bitcast.place, ...), custom_call_target="tpu_custom_call" | custom-call | flops 20000000000 | bytes 20000000 | tf_op jit(solution)/shard_map/attention_and_mixing/pallas_call | solution.py:845
  19.2 0.7 collective-permute-start
  20.0 1.2 collective-permute-start.1
  21.2 0.5 collective-permute-start.2
  21.7 0.9 constant_dynamic-update-slice_fusion.3
  22.6 0.0 collective-permute-done.in1
  22.6 2.6 %collective-permute-done.1.in2 = bf16[128,512]{1,0:T(8,128)(2,1)S(1)} collective-permute-done((bf16[128,512]{1,0:T(8,128)(2,1)}, bf16[128,512]{1,0:T(8,128)(2,1)S(1)}, u32[]{:S(2)}, u32[]{:S(2)}) %collective-permute-start.1) | collective-permute-done | bytes 131104 | tf_op jit(solution)/shard_map/to_experts/ppermute | solution.py:1077
  25.3 3.0 %collective-permute-done.2.in3 = bf16[128,512]{1,0:T(8,128)(2,1)S(1)} collective-permute-done((bf16[128,512]{1,0:T(8,128)(2,1)}, bf16[128,512]{1,0:T(8,128)(2,1)S(1)}, u32[]{:S(2)}, u32[]{:S(2)}) %collective-permute-start.2) | collective-permute-done | bytes 131104 | tf_op jit(solution)/shard_map/to_experts/ppermute | solution.py:1077
  28.2 0.2 collective-permute-start.6
  28.5 1.3 collective-permute-start.8
  29.8 0.0 copy-done.6
  29.8 0.0 copy-done.7
  29.8 0.9 copy-done.4
  30.7 4.4 %experts.1 = (bf16[128,512]{1,0:T(8,128)(2,1)S(1)}, bf16[128,512]{1,0:T(8,128)(2,1)S(1)}, bf16[128,512]{1,0:T(8,128)(2,1)S(1)}, bf16[128,512]{1,0:T(8,128)(2,1)S(1)}) custom-call(bf16[128,512]{1,0:T(8,128)(2,1)S(1)} %copy-done.4, bf16[128,512]{1,0:T(8,128)(2,1)S(1)} %collective-permute-done.in1, bf16[128,512]{1,0:T(8,128)(2,1)S(1)} %collective-permute-done.1.in2, ...), custom_call_target="tpu_custom_call" | custom-call | flops 5000000000 | bytes 10000000 | tf_op jit(solution)/shard_map/experts/pallas_call | solution.py:878
  35.1 0.9 collective-permute-start.3
  36.0 1.3 collective-permute-start.4
  37.2 0.5 collective-permute-start.5
  37.7 3.9 %collective-permute-done.6.refs_1_ = bf16[512,512]{1,0:T(8,128)(2,1)S(1)} collective-permute-done((bf16[512,512]{1,0:T(8,128)(2,1)S(1)}, bf16[512,512]{1,0:T(8,128)(2,1)S(1)}, u32[]{:S(2)}, u32[]{:S(2)}) %collective-permute-start.6) | collective-permute-done | bytes 524320 | tf_op jit(solution)/shard_map/gather_for_weights/ppermute | solution.py:1082
  41.6 0.2 collective-permute-start.7
  41.8 0.0 collective-permute-done.8.refs_2_
  41.8 1.3 collective-permute-start.9
  43.1 0.0 collective-permute-done.3.ret1
  43.1 0.0 collective-permute-done.4.ret2
  43.1 1.0 collective-permute-done.5.ret3
  44.0 0.0 copy-done.15
  44.0 8.3 %mixing_backward.1 = (bf16[1024,512]{1,0:T(8,128)(2,1)}, f32[1024,512]{1,0:T(8,128)}, bf16[8,1024,128]{2,1,0:T(8,128)(2,1)}, bf16[256,640]{1,0:T(8,128)(2,1)S(1)}, bf16[256,640]{1,0:T(8,128)(2,1)S(1)}) custom-call(s32[1]{0:T(128)} %bitcast.place, s32[1]{0:T(128)} %bitcast.1.near, bf16[128,512]{1,0:T(8,128)(2,1)S(1)} %get-tuple-element.72.ret0, ...), custom_call_target="tpu_custom_call" | custom-call | flops 8000000000 | bytes 15000000 | tf_op jit(solution)/shard_map/mixing_backward/pallas_call | solution.py:900
  52.4 1.6 collective-permute-done.7.refs_3_
  54.0 0.0 collective-permute-done.9.refs_4_
  54.0 0.2 collective-permute-start.10
  54.2 1.3 collective-permute-start.11
  55.5 2.6 %collective-permute-start.12 = (bf16[256,640]{1,0:T(8,128)(2,1)S(1)}, bf16[256,640]{1,0:T(8,128)(2,1)S(1)}, u32[]{:S(2)}, u32[]{:S(2)}) collective-permute-start(bf16[256,640]{1,0:T(8,128)(2,1)S(1)} %get-tuple-element.92), channel_id=1, source_target_pairs={{0,1},{1,0},{2,3},{3,2},{4,5},{5,4},{6,7},{7,6},{8,9},{9,8},{10,11... | collective-permute-start | bytes 983048 | tf_op jit(solution)/shard_map/reduce/ppermute | solution.py:1094
  58.1 19.0 %attention_backward.1 = (bf16[4,1024,384]{2,1,0:T(8,128)(2,1)}, bf16[256,1536]{1,0:T(8,128)(2,1)}, bf16[256,1536]{1,0:T(8,128)(2,1)}) custom-call(s32[1]{0:T(128)} %bitcast.1.near, bf16[8,1024,128]{2,1,0:T(8,128)(2,1)} %get-tuple-element.81.queries_far, bf16[8,1024,128]{2,1,0:T(8,128)(2,1)} %get-tuple-element.82.keys_far, ...), custom_call_target="tpu_custom_call" | custom-call | flops 20000000000 | bytes 12000000 | tf_op jit(solution)/shard_map/attention_backward/pallas_call | solution.py:925
  77.1 0.0 collective-permute-done.12.swapped_out
  77.2 0.0 collective-permute-done.10.refs_5_
  77.2 0.0 collective-permute-done.11.refs_6_
  77.2 0.0 copy-start.18
  77.2 0.1 collective-permute-start.13
  77.3 0.1 collective-permute-start.14
  77.5 1.4 collective-permute-start.15
  78.9 0.9 collective-permute-done.13.swapped
  79.8 1.1 copy-done.3
  80.9 1.3 reduce.2
  82.2 2.6 %collective-permute-done.14.refs_7_ = bf16[256,512]{1,0:T(8,128)(2,1)S(1)} collective-permute-done((bf16[256,512]{1,0:T(8,128)(2,1)S(1)}, bf16[256,512]{1,0:T(8,128)(2,1)S(1)}, u32[]{:S(2)}, u32[]{:S(2)}) %collective-permute-start.14) | collective-permute-done | bytes 262176 | tf_op jit(solution)/shard_map/gather_for_weights/ppermute | solution.py:1082
  84.7 0.0 collective-permute-done.15.refs_8_
  84.7 0.7 copy-done.12
  85.4 6.8 %all-to-all-start = ((bf16[16,16,2176]{2,1,0:T(8,128)(2,1)}), bf16[16,16,2176]{2,1,0:T(8,128)(2,1)S(1)}, u32[]{:S(2)}, u32[]{:S(2)}) async-start(bf16[16,16,2176]{2,1,0:T(8,128)(2,1)} %bitcast.5), calls=%async_computation | async-start | bytes 2228224 | tf_op jit(solution)/shard_map/reduce/all_to_all | solution.py:1098
  92.2 0.0 copy-done
  92.3 0.0 copy-start.10
  92.3 0.0 copy-start.13
  92.3 6.0 %norm_backward.1 = bf16[1024,512]{1,0:T(8,128)(2,1)} custom-call(bf16[4,1024,384]{2,1,0:T(8,128)(2,1)} %get-tuple-element.104.grads, bf16[1024,512]{1,0:T(8,128)(2,1)} %tok.1, f32[1024,512]{1,0:T(8,128)} %get-tuple-element.105.grad_hidden, f32[1,512]{1,0:T(1,128)S(1)} %bitcast.14, bf16[512,512]{1,0:T(8,128)(2,1)S(1)} %copy-done, ...), custom_call_target="tpu_custom_call" | custom-call | flops 2000000000 | bytes 8000000 | tf_op jit(solution)/shard_map/norm_backward/pallas_call | solution.py:982
  98.3 0.0 copy-done.10
  98.3 11.9 %expert_weights.2 = (f32[2,64,2048]{2,1,0:T(8,128)}, f32[2,256,512]{2,1,0:T(8,128)}) custom-call(s32[1]{0:T(128)} %bitcast.6.place, bf16[512,512]{1,0:T(8,128)(2,1)S(1)} %constant_dynamic-update-slice_fusion.refs_0_, bf16[512,512]{1,0:T(8,128)(2,1)S(1)} %copy-done.10, bf16[512,512]{1,0:T(8,128)(2,1)} %copy-done.19, bf16[512,512]{1,0:T(8,128)(2,1)} %copy-done.20, ...), custom_call_target="tpu_custom_call" | custom-call | flops 10000000000 | bytes 8000000 | tf_op jit(solution)/shard_map/expert_weights/pallas_call | solution.py:949
  110.2 8.2 %all-to-all-done.parts = bf16[16,16,2176]{2,1,0:T(8,128)(2,1)S(1)} async-done(((bf16[16,16,2176]{2,1,0:T(8,128)(2,1)}), bf16[16,16,2176]{2,1,0:T(8,128)(2,1)S(1)}, u32[]{:S(2)}, u32[]{:S(2)}) %all-to-all-start) | async-done | bytes 1114144 | tf_op jit(solution)/shard_map/reduce/all_to_all | solution.py:1098
  118.4 1.2 reduce.3
  119.6 4.0 %all-to-all-start.1 = ((bf16[16,16,2176]{2,1,0:T(8,128)(2,1)}), bf16[16,16,2176]{2,1,0:T(8,128)(2,1)S(1)}, u32[]{:S(2)}, u32[]{:S(2)}) async-start(bf16[16,16,2176]{2,1,0:T(8,128)(2,1)} %reduce.3), calls=%async_computation.1 | async-start | bytes 2228224 | tf_op jit(solution)/shard_map/reduce/all_to_all | solution.py:1101
  123.6 1.0 copy-done.11
  124.6 0.9 copy-done.14
  125.5 11.9 %expert_weights.3 = (f32[2,64,2048]{2,1,0:T(8,128)}, f32[2,256,512]{2,1,0:T(8,128)}) custom-call(s32[1]{0:T(128)} %bitcast.6.place, bf16[512,512]{1,0:T(8,128)(2,1)S(1)} %constant_dynamic-update-slice_fusion.refs_0_, bf16[512,512]{1,0:T(8,128)(2,1)S(1)} %copy-done.11, bf16[512,512]{1,0:T(8,128)(2,1)} %copy-done.19, ...), custom_call_target="tpu_custom_call", output_to_operand_aliasing={{0}: (12, {}), {1}: (13, {})} | custom-call | flops 10000000000 | bytes 8000000 | tf_op jit(solution)/shard_map/expert_weights/pallas_call | solution.py:949
  137.4 12.2 %all-to-all-done.1 = bf16[16,16,2176]{2,1,0:T(8,128)(2,1)S(1)} async-done(((bf16[16,16,2176]{2,1,0:T(8,128)(2,1)}), bf16[16,16,2176]{2,1,0:T(8,128)(2,1)S(1)}, u32[]{:S(2)}, u32[]{:S(2)}) %all-to-all-start.1) | async-done | bytes 1114144 | tf_op jit(solution)/shard_map/reduce/all_to_all | solution.py:1101
  149.7 2.5 %collective-permute-start.16 = (bf16[256,2176]{1,0:T(8,128)(2,1)S(1)}, bf16[256,2176]{1,0:T(8,128)(2,1)S(1)}, u32[]{:S(2)}, u32[]{:S(2)}) collective-permute-start(bf16[256,2176]{1,0:T(8,128)(2,1)S(1)} %bitcast.11), channel_id=1, source_target_pairs={{0,1},{1,0},{2,3},{3,2},{4,5},{5,4},{6,7},{7,6},{8,9},{9,8},{10,11... | collective-permute-start | bytes 3342344 | tf_op jit(solution)/shard_map/reduce/ppermute | solution.py:1094
  152.2 2.4 %collective-permute-done.16.both_other = bf16[256,2176]{1,0:T(8,128)(2,1)S(1)} collective-permute-done((bf16[256,2176]{1,0:T(8,128)(2,1)S(1)}, bf16[256,2176]{1,0:T(8,128)(2,1)S(1)}, u32[]{:S(2)}, u32[]{:S(2)}) %collective-permute-start.16) | collective-permute-done | bytes 1114144 | tf_op jit(solution)/shard_map/reduce/ppermute | solution.py:1094
  154.6 3.1 %assemble.1 = (f32[512,512]{1,0:T(8,128)}, f32[512,512]{1,0:T(8,128)}, f32[512,512]{1,0:T(8,128)}, f32[512,512]{1,0:T(8,128)}, f32[8,512]{1,0:T(8,128)}, /*index=5*/f32[1,512]{1,0:T(1,128)}, f32[1,512]{1,0:T(1,128)}) custom-call(s32[1]{0:T(128)} %bitcast.1.near, bf16[256,2176]{1,0:T(8,128)(2,1)S(1)} %bitcast.12, ...), custom_call_target="tpu_custom_call" | custom-call | flops 100000000 | bytes 6000000 | tf_op jit(solution)/shard_map/assemble/pallas_call | solution.py:1021
  (34 shorter events, 0.1 us)
Async XLA Ops:
  0.7 29.1 %copy-start.6 = (bf16[2,512,2048]{2,1,0:T(8,128)(2,1)S(1)}, bf16[2,512,2048]{2,1,0:T(8,128)(2,1)}, u32[]{:S(2)}) copy-start(bf16[2,512,2048]{2,1,0:T(8,128)(2,1)} %refs_9_.3) | copy-start | bytes 12582916
  0.7 29.1 %copy-start.7 = (bf16[2,2048,512]{2,1,0:T(8,128)(2,1)S(1)}, bf16[2,2048,512]{2,1,0:T(8,128)(2,1)}, u32[]{:S(2)}) copy-start(bf16[2,2048,512]{2,1,0:T(8,128)(2,1)} %refs_10_.3) | copy-start | bytes 12582916
  19.2 3.4 %collective-permute-start = (bf16[128,512]{1,0:T(8,128)(2,1)}, bf16[128,512]{1,0:T(8,128)(2,1)S(1)}, u32[]{:S(2)}, u32[]{:S(2)}) collective-permute-start(bf16[128,512]{1,0:T(8,128)(2,1)} %get-tuple-element.69), channel_id=1, source_target_pairs={{0,1},{1,0},{2,3},{3,2},{4,5},{5,4},{6,7},{7,6},{8,9},{9,8},{10,11... | collective-permute-start | bytes 393224 | tf_op jit(solution)/shard_map/to_experts/ppermute | solution.py:1077
  20.0 5.3 %collective-permute-start.1 = (bf16[128,512]{1,0:T(8,128)(2,1)}, bf16[128,512]{1,0:T(8,128)(2,1)S(1)}, u32[]{:S(2)}, u32[]{:S(2)}) collective-permute-start(bf16[128,512]{1,0:T(8,128)(2,1)} %get-tuple-element.70), channel_id=1, source_target_pairs={{0,2},{1,3},{2,0},{3,1},{4,6},{5,7},{6,4},{7,5},{8,10},{9,11},{10,... | collective-permute-start | bytes 393224 | tf_op jit(solution)/shard_map/to_experts/ppermute | solution.py:1077
  21.2 7.0 %collective-permute-start.2 = (bf16[128,512]{1,0:T(8,128)(2,1)}, bf16[128,512]{1,0:T(8,128)(2,1)S(1)}, u32[]{:S(2)}, u32[]{:S(2)}) collective-permute-start(bf16[128,512]{1,0:T(8,128)(2,1)} %get-tuple-element.71), channel_id=1, source_target_pairs={{0,3},{1,2},{2,1},{3,0},{4,7},{5,6},{6,5},{7,4},{8,11},{9,10},{10,... | collective-permute-start | bytes 393224 | tf_op jit(solution)/shard_map/to_experts/ppermute | solution.py:1077
  28.2 15.8 %copy-start.15 = (bf16[512,8]{0,1:T(8,128)(2,1)S(1)}, bf16[512,8]{0,1:T(8,128)(2,1)}, u32[]{:S(2)}) copy-start(bf16[512,8]{0,1:T(8,128)(2,1)} %param.22) | copy-start | bytes 24580
  28.2 15.8 %copy-start.16 = (f32[512]{0:T(512)S(1)}, f32[512]{0:T(512)}, u32[]{:S(2)}) copy-start(f32[512]{0:T(512)} %param.21) | copy-start | bytes 6148
  28.2 13.3 %collective-permute-start.6 = (bf16[512,512]{1,0:T(8,128)(2,1)S(1)}, bf16[512,512]{1,0:T(8,128)(2,1)S(1)}, u32[]{:S(2)}, u32[]{:S(2)}) collective-permute-start(bf16[512,512]{1,0:T(8,128)(2,1)S(1)} %constant_dynamic-update-slice_fusion.refs_0_), channel_id=1, source_target_pairs={{0,8},{8,16},{16,24},{24,28},{28,20},{20,12},{12,4},{4,0},{1,9},{9... | collective-permute-start | bytes 1572872 | tf_op jit(solution)/shard_map/gather_for_weights/ppermute | solution.py:1082
  28.5 13.3 %collective-permute-start.8 = (bf16[512,512]{1,0:T(8,128)(2,1)S(1)}, bf16[512,512]{1,0:T(8,128)(2,1)S(1)}, u32[]{:S(2)}, u32[]{:S(2)}) collective-permute-start(bf16[512,512]{1,0:T(8,128)(2,1)S(1)} %constant_dynamic-update-slice_fusion.refs_0_), channel_id=1, source_target_pairs={{8,0},{16,8},{24,16},{28,24},{20,28},{12,20},{4,12},{0,4},{9,1},{1... | collective-permute-start | bytes 1572872 | tf_op jit(solution)/shard_map/gather_for_weights/ppermute | solution.py:1082
  29.8 0.9 copy-start.4
  30.7 13.4 %copy-start.8 = (bf16[512,512]{1,0:T(8,128)(2,1)S(1)}, bf16[512,512]{1,0:T(8,128)(2,1)}, u32[]{:S(2)}) copy-start(bf16[512,512]{1,0:T(8,128)(2,1)} %w_out_far.3) | copy-start | bytes 1572868
  35.1 7.9 %collective-permute-start.3 = (bf16[128,512]{1,0:T(8,128)(2,1)S(1)}, bf16[128,512]{1,0:T(8,128)(2,1)S(1)}, u32[]{:S(2)}, u32[]{:S(2)}) collective-permute-start(bf16[128,512]{1,0:T(8,128)(2,1)S(1)} %get-tuple-element.73), channel_id=1, source_target_pairs={{0,1},{1,0},{2,3},{3,2},{4,5},{5,4},{6,7},{7,6},{8,9},{9,8},{10,11... | collective-permute-start | bytes 393224 | tf_op jit(solution)/shard_map/from_experts/ppermute | solution.py:1077
  36.0 7.1 %collective-permute-start.4 = (bf16[128,512]{1,0:T(8,128)(2,1)S(1)}, bf16[128,512]{1,0:T(8,128)(2,1)S(1)}, u32[]{:S(2)}, u32[]{:S(2)}) collective-permute-start(bf16[128,512]{1,0:T(8,128)(2,1)S(1)} %get-tuple-element.74), channel_id=1, source_target_pairs={{0,2},{1,3},{2,0},{3,1},{4,6},{5,7},{6,4},{7,5},{8,10},{9,11},{10,... | collective-permute-start | bytes 393224 | tf_op jit(solution)/shard_map/from_experts/ppermute | solution.py:1077
  37.2 6.8 %collective-permute-start.5 = (bf16[128,512]{1,0:T(8,128)(2,1)S(1)}, bf16[128,512]{1,0:T(8,128)(2,1)S(1)}, u32[]{:S(2)}, u32[]{:S(2)}) collective-permute-start(bf16[128,512]{1,0:T(8,128)(2,1)S(1)} %get-tuple-element.75), channel_id=1, source_target_pairs={{0,3},{1,2},{2,1},{3,0},{4,7},{5,6},{6,5},{7,4},{8,11},{9,10},{10,... | collective-permute-start | bytes 393224 | tf_op jit(solution)/shard_map/from_experts/ppermute | solution.py:1077
  41.6 10.8 %copy-start.9 = (bf16[512,512]{1,0:T(8,128)(2,1)}, bf16[512,512]{1,0:T(8,128)(2,1)S(1)}, u32[]{:S(2)}) copy-start(bf16[512,512]{1,0:T(8,128)(2,1)S(1)} %collective-permute-done.6.refs_1_) | copy-start | bytes 1572868
  41.6 12.4 %collective-permute-start.7 = (bf16[512,512]{1,0:T(8,128)(2,1)S(1)}, bf16[512,512]{1,0:T(8,128)(2,1)S(1)}, u32[]{:S(2)}, u32[]{:S(2)}) collective-permute-start(bf16[512,512]{1,0:T(8,128)(2,1)S(1)} %collective-permute-done.6.refs_1_), channel_id=1, source_target_pairs={{0,8},{8,16},{16,24},{24,28},{28,20},{20,12},{12,4},{4,0},{1,9},{9... | collective-permute-start | bytes 1572872 | tf_op jit(solution)/shard_map/gather_for_weights/ppermute | solution.py:1082
  41.8 10.6 %copy-start.19 = (bf16[512,512]{1,0:T(8,128)(2,1)}, bf16[512,512]{1,0:T(8,128)(2,1)S(1)}, u32[]{:S(2)}) copy-start(bf16[512,512]{1,0:T(8,128)(2,1)S(1)} %collective-permute-done.8.refs_2_) | copy-start | bytes 1572868
  41.8 12.2 %collective-permute-start.9 = (bf16[512,512]{1,0:T(8,128)(2,1)S(1)}, bf16[512,512]{1,0:T(8,128)(2,1)S(1)}, u32[]{:S(2)}, u32[]{:S(2)}) collective-permute-start(bf16[512,512]{1,0:T(8,128)(2,1)S(1)} %collective-permute-done.8.refs_2_), channel_id=1, source_target_pairs={{8,0},{16,8},{24,16},{28,24},{20,28},{12,20},{4,12},{0,4},{9,1},{1... | collective-permute-start | bytes 1572872 | tf_op jit(solution)/shard_map/gather_for_weights/ppermute | solution.py:1082
  54.0 23.2 %copy-start.20 = (bf16[512,512]{1,0:T(8,128)(2,1)}, bf16[512,512]{1,0:T(8,128)(2,1)S(1)}, u32[]{:S(2)}) copy-start(bf16[512,512]{1,0:T(8,128)(2,1)S(1)} %collective-permute-done.7.refs_3_) | copy-start | bytes 1572868
  54.0 23.2 %copy-start.21 = (bf16[512,512]{1,0:T(8,128)(2,1)}, bf16[512,512]{1,0:T(8,128)(2,1)S(1)}, u32[]{:S(2)}) copy-start(bf16[512,512]{1,0:T(8,128)(2,1)S(1)} %collective-permute-done.9.refs_4_) | copy-start | bytes 1572868
  54.0 23.2 %collective-permute-start.10 = (bf16[512,512]{1,0:T(8,128)(2,1)S(1)}, bf16[512,512]{1,0:T(8,128)(2,1)S(1)}, u32[]{:S(2)}, u32[]{:S(2)}) collective-permute-start(bf16[512,512]{1,0:T(8,128)(2,1)S(1)} %collective-permute-done.7.refs_3_), channel_id=1, source_target_pairs={{0,8},{8,16},{16,24},{24,28},{28,20},{20,12},{12,4},{4,0},{1,9},{9... | collective-permute-start | bytes 1572872 | tf_op jit(solution)/shard_map/gather_for_weights/ppermute | solution.py:1082
  54.2 23.0 %collective-permute-start.11 = (bf16[512,512]{1,0:T(8,128)(2,1)S(1)}, bf16[512,512]{1,0:T(8,128)(2,1)S(1)}, u32[]{:S(2)}, u32[]{:S(2)}) collective-permute-start(bf16[512,512]{1,0:T(8,128)(2,1)S(1)} %collective-permute-done.9.refs_4_), channel_id=1, source_target_pairs={{8,0},{16,8},{24,16},{28,24},{20,28},{12,20},{4,12},{0,4},{9,1},{1... | collective-permute-start | bytes 1572872 | tf_op jit(solution)/shard_map/gather_for_weights/ppermute | solution.py:1082
  55.5 21.7 %collective-permute-start.12 = (bf16[256,640]{1,0:T(8,128)(2,1)S(1)}, bf16[256,640]{1,0:T(8,128)(2,1)S(1)}, u32[]{:S(2)}, u32[]{:S(2)}) collective-permute-start(bf16[256,640]{1,0:T(8,128)(2,1)S(1)} %get-tuple-element.92), channel_id=1, source_target_pairs={{0,1},{1,0},{2,3},{3,2},{4,5},{5,4},{6,7},{7,6},{8,9},{9,8},{10,11... | collective-permute-start | bytes 983048 | tf_op jit(solution)/shard_map/reduce/ppermute | solution.py:1094
  77.2 5.0 %copy-start.17 = (bf16[512,512]{1,0:T(8,128)(2,1)}, bf16[512,512]{1,0:T(8,128)(2,1)S(1)}, u32[]{:S(2)}) copy-start(bf16[512,512]{1,0:T(8,128)(2,1)S(1)} %collective-permute-done.10.refs_5_) | copy-start | bytes 1572868
  77.2 5.0 %copy-start.18 = (bf16[512,512]{1,0:T(8,128)(2,1)}, bf16[512,512]{1,0:T(8,128)(2,1)S(1)}, u32[]{:S(2)}) copy-start(bf16[512,512]{1,0:T(8,128)(2,1)S(1)} %collective-permute-done.11.refs_6_) | copy-start | bytes 1572868
  77.2 2.6 %collective-permute-start.13 = (bf16[256,1536]{1,0:T(8,128)(2,1)}, bf16[256,1536]{1,0:T(8,128)(2,1)S(1)}, u32[]{:S(2)}, u32[]{:S(2)}) collective-permute-start(bf16[256,1536]{1,0:T(8,128)(2,1)} %get-tuple-element.95), channel_id=1, source_target_pairs={{0,1},{1,0},{2,3},{3,2},{4,5},{5,4},{6,7},{7,6},{8,9},{9,8},{10,11... | collective-permute-start | bytes 2359304 | tf_op jit(solution)/shard_map/reduce/ppermute | solution.py:1094
  77.3 7.4 %collective-permute-start.14 = (bf16[256,512]{1,0:T(8,128)(2,1)S(1)}, bf16[256,512]{1,0:T(8,128)(2,1)S(1)}, u32[]{:S(2)}, u32[]{:S(2)}) collective-permute-start(bf16[256,512]{1,0:T(8,128)(2,1)S(1)} %slice.6), channel_id=1, source_target_pairs={{0,8},{8,16},{16,24},{24,28},{28,20},{20,12},{12,4},{4,0},{1,9},{9... | collective-permute-start | bytes 786440 | tf_op jit(solution)/shard_map/gather_for_weights/ppermute | solution.py:1082
  77.5 7.3 %collective-permute-start.15 = (bf16[256,512]{1,0:T(8,128)(2,1)S(1)}, bf16[256,512]{1,0:T(8,128)(2,1)S(1)}, u32[]{:S(2)}, u32[]{:S(2)}) collective-permute-start(bf16[256,512]{1,0:T(8,128)(2,1)S(1)} %slice.7), channel_id=1, source_target_pairs={{8,0},{16,8},{24,16},{28,24},{20,28},{12,20},{4,12},{0,4},{9,1},{1... | collective-permute-start | bytes 786440 | tf_op jit(solution)/shard_map/gather_for_weights/ppermute | solution.py:1082
  79.8 1.1 copy-start.3
  80.9 11.3 %copy-start = (bf16[512,512]{1,0:T(8,128)(2,1)S(1)}, bf16[512,512]{1,0:T(8,128)(2,1)}, u32[]{:S(2)}) copy-start(bf16[512,512]{1,0:T(8,128)(2,1)} %w_query_far.3) | copy-start | bytes 1572868
  80.9 11.4 %copy-start.1 = (bf16[512,512]{1,0:T(8,128)(2,1)S(1)}, bf16[512,512]{1,0:T(8,128)(2,1)}, u32[]{:S(2)}) copy-start(bf16[512,512]{1,0:T(8,128)(2,1)} %w_key_far.3) | copy-start | bytes 1572868
  80.9 11.4 %copy-start.2 = (bf16[512,512]{1,0:T(8,128)(2,1)S(1)}, bf16[512,512]{1,0:T(8,128)(2,1)}, u32[]{:S(2)}) copy-start(bf16[512,512]{1,0:T(8,128)(2,1)} %w_value_far.3) | copy-start | bytes 1572868
  80.9 11.4 %copy-start.5 = (f32[512]{0:T(512)S(1)}, f32[512]{0:T(512)}, u32[]{:S(2)}) copy-start(f32[512]{0:T(512)} %param.16) | copy-start | bytes 6148
  84.7 0.7 copy-start.12
  85.4 32.9 %all-to-all-start = ((bf16[16,16,2176]{2,1,0:T(8,128)(2,1)}), bf16[16,16,2176]{2,1,0:T(8,128)(2,1)S(1)}, u32[]{:S(2)}, u32[]{:S(2)}) async-start(bf16[16,16,2176]{2,1,0:T(8,128)(2,1)} %bitcast.5), calls=%async_computation | async-start | bytes 2228224 | tf_op jit(solution)/shard_map/reduce/all_to_all | solution.py:1098
  92.3 6.0 %copy-start.10 = (bf16[512,512]{1,0:T(8,128)(2,1)S(1)}, bf16[512,512]{1,0:T(8,128)(2,1)}, u32[]{:S(2)}) copy-start(bf16[512,512]{1,0:T(8,128)(2,1)} %copy-done.9) | copy-start | bytes 1572868
  92.3 6.0 %copy-start.13 = (bf16[256,512]{1,0:T(8,128)(2,1)S(1)}, bf16[256,512]{1,0:T(8,128)(2,1)}, u32[]{:S(2)}) copy-start(bf16[256,512]{1,0:T(8,128)(2,1)} %copy-done.12) | copy-start | bytes 786436
  119.6 30.1 %all-to-all-start.1 = ((bf16[16,16,2176]{2,1,0:T(8,128)(2,1)}), bf16[16,16,2176]{2,1,0:T(8,128)(2,1)S(1)}, u32[]{:S(2)}, u32[]{:S(2)}) async-start(bf16[16,16,2176]{2,1,0:T(8,128)(2,1)} %reduce.3), calls=%async_computation.1 | async-start | bytes 2228224 | tf_op jit(solution)/shard_map/reduce/all_to_all | solution.py:1101
  123.5 1.0 copy-start.11
  124.6 0.9 copy-start.14
  149.7 4.9 %collective-permute-start.16 = (bf16[256,2176]{1,0:T(8,128)(2,1)S(1)}, bf16[256,2176]{1,0:T(8,128)(2,1)S(1)}, u32[]{:S(2)}, u32[]{:S(2)}) collective-permute-start(bf16[256,2176]{1,0:T(8,128)(2,1)S(1)} %bitcast.11), channel_id=1, source_target_pairs={{0,1},{1,0},{2,3},{3,2},{4,5},{5,4},{6,7},{7,6},{8,9},{9,8},{10,11... | collective-permute-start | bytes 3342344 | tf_op jit(solution)/shard_map/reduce/ppermute | solution.py:1094

commit v2 on v1

--- a/solution.py
+++ b/solution.py
@@ -914,7 +914,7 @@
             dma(7),
             dma(3 * blocks),
         ],
-        compiler_params=params(52),
+        compiler_params=params(28),
         cost_estimate=cost(8e9, 1.5e7),
     )(place, near, *returned, gain2, w_control, hidden, cot, mix, attended, w_out)
 
@@ -936,7 +936,7 @@
             dma(4 * PAIRS + 1),
             dma(PAIRS),
         ],
-        compiler_params=params(56),
+        compiler_params=params(32),
         cost_estimate=cost(2e10, 1.2e7),
     )(near, queries, keys, values, pulls, normed)
 
@@ -970,7 +970,7 @@
             pltpu.VMEM((FF_BLOCK, D), F32),
         ],
         input_output_aliases={3 + len(pieces) + i: i for i in range(len(earlier))},
-        compiler_params=params(52),
+        compiler_params=params(40),
         cost_estimate=cost(1e10, 8e6),
     )(copy, *pieces, w_up, w_down, *earlier)
 
@@ -988,7 +988,7 @@
         + [pl.BlockSpec((D, D), fixed)] * 3,
         out_specs=pl.BlockSpec((BLOCK, D), row_block),
         out_shape=shape(rows, D),
-        compiler_params=params(52),
+        compiler_params=params(32),
         cost_estimate=cost(2e9, 8e6),
     )(grads, tokens, grad_hidden, gain1, *weights)
 

time: 158 us -> 157 us (level)
  local copies, waits for them, and re-layouts: 5.78 us -> 22.7 us
  waiting for transfers between devices: 38.2 us -> 27.2 us
  Pallas kernels: 85.6 us -> 77.8 us
    unnamed x47 -> x107, local copies, waits for them, and re-layouts: 5.73 us -> 22.7 us
    all_to_all x1, waiting for transfers between devices: 12.2 us -> 4.52 us  [spread(): lax.all_to_all(own, axes, 0, 0, tiled=True).reshape(-1, own.shape[-1])]
    all_to_all x1, waiting for transfers between devices: 8.17 us -> 3.45 us  [scatter(): lax.all_to_all(half.reshape(count, rows // count, cols), axes, 0, 0, tile...]
    pallas_call x2, Pallas kernels: 23.8 us -> 20 us  [weight_call(): pl.pallas_call(functools.partial(weight_kernel, expert, len(pieces)), gri...]
    pallas_call x1, Pallas kernels: 5.96 us -> 4.09 us  [last_call(): pl.pallas_call(last_kernel, grid=(rows // BLOCK,), in_specs=[pl.BlockSpec...]
    pallas_call x1, Pallas kernels: 19 us -> 17.2 us  [pair_call(): pl.pallas_call(pair_kernel, in_specs=[smem()] + [far()] * 5, out_specs=[f...]
    ppermute x4, waiting for transfers between devices: 8.01 us -> 9.61 us  [pass_on(): lax.ppermute(ahead_part, 'dp', ahead)]
  transfers between devices with their start and end apart: 19 -> 19, of which waited for: 10 -> 10; matrix products, arithmetic and copies ran while one was open for 1% -> 1% of each run, Pallas kernels for 40% -> 35%
where the time goes in v2:
time: 157 us; the launch traced here: 156 us
  Pallas kernels  77.8 us (50%)
  waiting for transfers between devices  27.2 us (17%)
  starting transfers between devices  27.1 us (17%)
  local copies, waits for them, and re-layouts  22.7 us (14%)
    unnamed x107, local copies, waits for them, and re-layouts  22.7 us
    pallas_call x2, Pallas kernels, weight_call(): pl.pallas_call(functools.partial(weight_kernel, expert, len(pieces)), gri...  20 us
    pallas_call x1, Pallas kernels, forward_call(): pl.pallas_call(forward_kernel, in_specs=[smem()] + [far()] * 11, out_spec...  18.5 us
    pallas_call x1, Pallas kernels, pair_call(): pl.pallas_call(pair_kernel, in_specs=[smem()] + [far()] * 5, out_specs=[f...  17.2 us
    ppermute x4, waiting for transfers between devices, pass_on(): lax.ppermute(ahead_part, 'dp', ahead)  9.61 us
    pallas_call x1, Pallas kernels, middle_call(): pl.pallas_call(middle_kernel, in_specs=[smem()] * 2 + [vmem()] * 4 + [far...  7.96 us
    all_to_all x1, starting transfers between devices, scatter(): lax.all_to_all(half.reshape(count, rows // count, cols), axes, 0, 0, tile...  6.79 us
    ppermute x6, waiting for transfers between devices, exchange(): lax.ppermute(parts[step], hosts_axes, [(i, i ^ step) for i in range(hosts)])  6.59 us
  transfers between devices with their start and end apart: 19, of which 10 were waited for; matrix products, arithmetic and copies ran while one was open for 1% of the time, Pallas kernels for 35%

profile of v2, /device:TPU:11, one launch (start us, length us, event | category | flops | bytes accessed | tf_op | source)
XLA Modules:
  0.0 156.1 jit_solution(8378882760081051614)
XLA Ops:
  0.7 0.0 copy-start.20
  0.7 0.0 copy-start.23
  0.7 18.5 %attention_and_mixing.1 = (bf16[128,512]{1,0:T(8,128)(2,1)}, bf16[128,512]{1,0:T(8,128)(2,1)}, bf16[128,512]{1,0:T(8,128)(2,1)}, bf16[128,512]{1,0:T(8,128)(2,1)...) custom-call(s32[1]{0:T(128)} %bitcast.place, ...), custom_call_target="tpu_custom_call" | custom-call | flops 20000000000 | bytes 20000000 | tf_op jit(solution)/shard_map/attention_and_mixing/pallas_call | solution.py:845
  19.2 0.7 collective-permute-start
  20.0 1.3 collective-permute-start.1
  21.2 0.5 collective-permute-start.2
  21.7 0.9 constant_dynamic-update-slice_fusion.3
  22.6 2.6 %collective-permute-done.1.in2 = bf16[128,512]{1,0:T(8,128)(2,1)S(1)} collective-permute-done((bf16[128,512]{1,0:T(8,128)(2,1)}, bf16[128,512]{1,0:T(8,128)(2,1)S(1)}, u32[]{:S(2)}, u32[]{:S(2)}) %collective-permute-start.1) | collective-permute-done | bytes 131104 | tf_op jit(solution)/shard_map/to_experts/ppermute | solution.py:1077
  25.3 3.0 %collective-permute-done.2.in3 = bf16[128,512]{1,0:T(8,128)(2,1)S(1)} collective-permute-done((bf16[128,512]{1,0:T(8,128)(2,1)}, bf16[128,512]{1,0:T(8,128)(2,1)S(1)}, u32[]{:S(2)}, u32[]{:S(2)}) %collective-permute-start.2) | collective-permute-done | bytes 131104 | tf_op jit(solution)/shard_map/to_experts/ppermute | solution.py:1077
  28.2 0.0 copy-start.16
  28.3 0.2 collective-permute-start.6
  28.5 1.3 collective-permute-start.8
  29.8 0.9 copy-done.15
  30.7 0.0 copy-start.47
  30.7 4.4 %experts.1 = (bf16[128,512]{1,0:T(8,128)(2,1)S(1)}, bf16[128,512]{1,0:T(8,128)(2,1)S(1)}, bf16[128,512]{1,0:T(8,128)(2,1)S(1)}, bf16[128,512]{1,0:T(8,128)(2,1)S(1)}) custom-call(bf16[128,512]{1,0:T(8,128)(2,1)S(1)} %copy-done.15, bf16[128,512]{1,0:T(8,128)(2,1)S(1)} %collective-permute-done.in1, bf16[128,512]{1,0:T(8,128)(2,1)S(1)} %collective-permute-done.1.in2, ...), custom_call_target="tpu_custom_call" | custom-call | flops 5000000000 | bytes 10000000 | tf_op jit(solution)/shard_map/experts/pallas_call | solution.py:878
  35.2 0.9 collective-permute-start.3
  36.0 1.3 collective-permute-start.4
  37.3 0.5 collective-permute-start.5
  37.7 3.9 %collective-permute-done.6.refs_1_ = bf16[512,512]{1,0:T(8,128)(2,1)S(1)} collective-permute-done((bf16[512,512]{1,0:T(8,128)(2,1)S(1)}, bf16[512,512]{1,0:T(8,128)(2,1)S(1)}, u32[]{:S(2)}, u32[]{:S(2)}) %collective-permute-start.6) | collective-permute-done | bytes 524320 | tf_op jit(solution)/shard_map/gather_for_weights/ppermute | solution.py:1082
  41.6 0.2 collective-permute-start.7
  41.8 1.3 collective-permute-start.9
  43.1 1.0 collective-permute-done.5.ret3
  44.2 0.0 copy-start.51
  44.2 8.0 %mixing_backward.1 = (bf16[1024,512]{1,0:T(8,128)(2,1)}, f32[1024,512]{1,0:T(8,128)S(1)}, bf16[8,1024,128]{2,1,0:T(8,128)(2,1)S(1)}, bf16[256,640]{1,0:T(8,128)(2,1)S(1)}, bf16[256,640]{1,0:T(8,128)(2,1)S(1)}) custom-call(s32[1]{0:T(128)} %bitcast.place, s32[1]{0:T(128)} %bitcast.1.near, bf16[128,512]{1,0:T(8,128)(2,1)S(1)} %get-tuple-element.72.ret0, ...), custom_call_target="tpu_custom_call" | custom-call | flops 8000000000 | bytes 15000000 | tf_op jit(solution)/shard_map/mixing_backward/pallas_call | solution.py:900
  52.2 1.8 %collective-permute-done.7.refs_3_ = bf16[512,512]{1,0:T(8,128)(2,1)S(1)} collective-permute-done((bf16[512,512]{1,0:T(8,128)(2,1)S(1)}, bf16[512,512]{1,0:T(8,128)(2,1)S(1)}, u32[]{:S(2)}, u32[]{:S(2)}) %collective-permute-start.7) | collective-permute-done | bytes 524320 | tf_op jit(solution)/shard_map/gather_for_weights/ppermute | solution.py:1082
  54.0 0.2 collective-permute-start.10
  54.2 1.3 collective-permute-start.11
  55.5 2.7 %collective-permute-start.12 = (bf16[256,640]{1,0:T(8,128)(2,1)S(1)}, bf16[256,640]{1,0:T(8,128)(2,1)S(1)}, u32[]{:S(2)}, u32[]{:S(2)}) collective-permute-start(bf16[256,640]{1,0:T(8,128)(2,1)S(1)} %get-tuple-element.92), channel_id=1, source_target_pairs={{0,1},{1,0},{2,3},{3,2},{4,5},{5,4},{6,7},{7,6},{8,9},{9,8},{10,11... | collective-permute-start | bytes 983048 | tf_op jit(solution)/shard_map/reduce/ppermute | solution.py:1094
  58.2 17.2 %attention_backward.1 = (bf16[4,1024,384]{2,1,0:T(8,128)(2,1)S(1)}, bf16[256,1536]{1,0:T(8,128)(2,1)S(1)}, bf16[256,1536]{1,0:T(8,128)(2,1)S(1)}) custom-call(s32[1]{0:T(128)} %bitcast.1.near, bf16[8,1024,128]{2,1,0:T(8,128)(2,1)S(1)} %copy-done.48, bf16[8,1024,128]{2,1,0:T(8,128)(2,1)S(1)} %copy-done.49, bf16[8,1024,128]{2,1,0:T(8,128)(2,1)S(1)} %copy-done.50, ...), custom_call_target="tpu_custom_call" | custom-call | flops 20000000000 | bytes 12000000 | tf_op jit(solution)/shard_map/attention_backward/pallas_call | solution.py:925
  75.5 0.1 collective-permute-start.13
  75.6 0.1 collective-permute-start.14
  75.7 1.4 collective-permute-start.15
  77.2 0.7 collective-permute-done.13.swapped
  77.8 1.2 reduce.2
  79.1 3.9 %collective-permute-done.14.refs_7_ = bf16[256,512]{1,0:T(8,128)(2,1)S(1)} collective-permute-done((bf16[256,512]{1,0:T(8,128)(2,1)S(1)}, bf16[256,512]{1,0:T(8,128)(2,1)S(1)}, u32[]{:S(2)}, u32[]{:S(2)}) %collective-permute-start.14) | collective-permute-done | bytes 262176 | tf_op jit(solution)/shard_map/gather_for_weights/ppermute | solution.py:1082
  83.0 0.7 copy-done.40
  83.7 6.8 %all-to-all-start = ((bf16[16,16,2176]{2,1,0:T(8,128)(2,1)}), bf16[16,16,2176]{2,1,0:T(8,128)(2,1)S(1)}, u32[]{:S(2)}, u32[]{:S(2)}) async-start(bf16[16,16,2176]{2,1,0:T(8,128)(2,1)} %bitcast.5), calls=%async_computation | async-start | bytes 2228224 | tf_op jit(solution)/shard_map/reduce/all_to_all | solution.py:1098
  90.5 1.9 %copy-done.1 = bf16[4,1024,384]{2,1,0:T(8,128)(2,1)S(1)} copy-done((bf16[4,1024,384]{2,1,0:T(8,128)(2,1)S(1)}, bf16[4,1024,384]{2,1,0:T(8,128)(2,1)}, u32[]{:S(2)}) %copy-start.1) | copy-done | bytes 3145752
  92.4 1.0 copy-done.2
  93.4 1.0 copy-done.4
  94.5 1.0 copy-done.6
  95.5 1.2 copy-done.8
  96.8 0.0 copy-start.29
  96.8 0.0 copy-start.35
  96.8 4.1 %norm_backward.1 = bf16[1024,512]{1,0:T(8,128)(2,1)} custom-call(bf16[4,1024,384]{2,1,0:T(8,128)(2,1)S(1)} %copy-done.1, bf16[1024,512]{1,0:T(8,128)(2,1)S(1)} %copy-done.8, f32[1024,512]{1,0:T(8,128)S(1)} %get-tuple-element.105.grad_hidden, f32[1,512]{1,0:T(1,128)S(1)} %bitcast.14, bf16[512,512]{1,0:T(8,128)(2,1)S(1)} %copy-done.2, ...), custom_call_target="tpu_custom_call" | custom-call | flops 2000000000 | bytes 8000000 | tf_op jit(solution)/shard_map/norm_backward/pallas_call | solution.py:982
  101.0 2.2 %copy-done.24 = bf16[2,2048,512]{2,1,0:T(8,128)(2,1)S(1)} copy-done((bf16[2,2048,512]{2,1,0:T(8,128)(2,1)S(1)}, bf16[2,2048,512]{2,1,0:T(8,128)(2,1)}, u32[]{:S(2)}) %copy-start.24) | copy-done | bytes 4194328
  103.2 10.0 %expert_weights.2 = (f32[2,64,2048]{2,1,0:T(8,128)}, f32[2,256,512]{2,1,0:T(8,128)}) custom-call(s32[1]{0:T(128)} %bitcast.6.place, bf16[512,512]{1,0:T(8,128)(2,1)S(1)} %copy-done.17, bf16[512,512]{1,0:T(8,128)(2,1)S(1)} %copy-done.29, bf16[512,512]{1,0:T(8,128)(2,1)S(1)} %copy-done.32, bf16[512,512]{1,0:T(8,128)(2,1)S(1)} %copy-done.35, ...), custom_call_target="tpu_custom_call" | custom-call | flops 10000000000 | bytes 8000000 | tf_op jit(solution)/shard_map/expert_weights/pallas_call | solution.py:949
  113.2 3.4 %all-to-all-done.parts = bf16[16,16,2176]{2,1,0:T(8,128)(2,1)S(1)} async-done(((bf16[16,16,2176]{2,1,0:T(8,128)(2,1)}), bf16[16,16,2176]{2,1,0:T(8,128)(2,1)S(1)}, u32[]{:S(2)}, u32[]{:S(2)}) %all-to-all-start) | async-done | bytes 1114144 | tf_op jit(solution)/shard_map/reduce/all_to_all | solution.py:1098
  116.6 1.2 reduce.3
  117.8 4.0 %all-to-all-start.1 = ((bf16[16,16,2176]{2,1,0:T(8,128)(2,1)}), bf16[16,16,2176]{2,1,0:T(8,128)(2,1)S(1)}, u32[]{:S(2)}, u32[]{:S(2)}) async-start(bf16[16,16,2176]{2,1,0:T(8,128)(2,1)} %reduce.3), calls=%async_computation.1 | async-start | bytes 2228224 | tf_op jit(solution)/shard_map/reduce/all_to_all | solution.py:1101
  121.8 1.0 copy-done.14
  122.8 1.0 copy-done.18
  123.9 2.2 %copy-done.22 = bf16[2,512,2048]{2,1,0:T(8,128)(2,1)S(1)} copy-done((bf16[2,512,2048]{2,1,0:T(8,128)(2,1)S(1)}, bf16[2,512,2048]{2,1,0:T(8,128)(2,1)}, u32[]{:S(2)}) %copy-start.22) | copy-done | bytes 4194328
  126.1 2.2 %copy-done.25 = bf16[2,2048,512]{2,1,0:T(8,128)(2,1)S(1)} copy-done((bf16[2,2048,512]{2,1,0:T(8,128)(2,1)S(1)}, bf16[2,2048,512]{2,1,0:T(8,128)(2,1)}, u32[]{:S(2)}) %copy-start.25) | copy-done | bytes 4194328
  128.3 1.0 copy-done.30
  129.3 1.0 copy-done.33
  130.4 1.0 copy-done.36
  131.4 1.0 copy-done.39
  132.4 0.9 copy-done.42
  133.4 10.0 %expert_weights.3 = (f32[2,64,2048]{2,1,0:T(8,128)}, f32[2,256,512]{2,1,0:T(8,128)}) custom-call(s32[1]{0:T(128)} %bitcast.6.place, bf16[512,512]{1,0:T(8,128)(2,1)S(1)} %copy-done.18, bf16[512,512]{1,0:T(8,128)(2,1)S(1)} %copy-done.30, bf16[512,512]{1,0:T(8,128)(2,1)S(1)} %copy-done.33, ...), custom_call_target="tpu_custom_call", output_to_operand_aliasing={{0}: (12, {}), {1}: (13, {})} | custom-call | flops 10000000000 | bytes 8000000 | tf_op jit(solution)/shard_map/expert_weights/pallas_call | solution.py:949
  143.4 4.5 %all-to-all-done.1 = bf16[16,16,2176]{2,1,0:T(8,128)(2,1)S(1)} async-done(((bf16[16,16,2176]{2,1,0:T(8,128)(2,1)}), bf16[16,16,2176]{2,1,0:T(8,128)(2,1)S(1)}, u32[]{:S(2)}, u32[]{:S(2)}) %all-to-all-start.1) | async-done | bytes 1114144 | tf_op jit(solution)/shard_map/reduce/all_to_all | solution.py:1101
  147.9 2.5 %collective-permute-start.16 = (bf16[256,2176]{1,0:T(8,128)(2,1)S(1)}, bf16[256,2176]{1,0:T(8,128)(2,1)S(1)}, u32[]{:S(2)}, u32[]{:S(2)}) collective-permute-start(bf16[256,2176]{1,0:T(8,128)(2,1)S(1)} %bitcast.11), channel_id=1, source_target_pairs={{0,1},{1,0},{2,3},{3,2},{4,5},{5,4},{6,7},{7,6},{8,9},{9,8},{10,11... | collective-permute-start | bytes 3342344 | tf_op jit(solution)/shard_map/reduce/ppermute | solution.py:1094
  150.4 2.4 %collective-permute-done.16.both_other = bf16[256,2176]{1,0:T(8,128)(2,1)S(1)} collective-permute-done((bf16[256,2176]{1,0:T(8,128)(2,1)S(1)}, bf16[256,2176]{1,0:T(8,128)(2,1)S(1)}, u32[]{:S(2)}, u32[]{:S(2)}) %collective-permute-start.16) | collective-permute-done | bytes 1114144 | tf_op jit(solution)/shard_map/reduce/ppermute | solution.py:1094
  152.8 3.1 %assemble.1 = (f32[512,512]{1,0:T(8,128)}, f32[512,512]{1,0:T(8,128)}, f32[512,512]{1,0:T(8,128)}, f32[512,512]{1,0:T(8,128)}, f32[8,512]{1,0:T(8,128)}, /*index=5*/f32[1,512]{1,0:T(1,128)}, f32[1,512]{1,0:T(1,128)}) custom-call(s32[1]{0:T(128)} %bitcast.1.near, bf16[256,2176]{1,0:T(8,128)(2,1)S(1)} %bitcast.12, ...), custom_call_target="tpu_custom_call" | custom-call | flops 100000000 | bytes 6000000 | tf_op jit(solution)/shard_map/assemble/pallas_call | solution.py:1021
  (94 shorter events, 0.2 us)
Async XLA Ops:
  0.7 29.1 %copy-start.20 = (bf16[2,512,2048]{2,1,0:T(8,128)(2,1)S(1)}, bf16[2,512,2048]{2,1,0:T(8,128)(2,1)}, u32[]{:S(2)}) copy-start(bf16[2,512,2048]{2,1,0:T(8,128)(2,1)} %refs_9_.3) | copy-start | bytes 12582916
  0.7 29.1 %copy-start.23 = (bf16[2,2048,512]{2,1,0:T(8,128)(2,1)S(1)}, bf16[2,2048,512]{2,1,0:T(8,128)(2,1)}, u32[]{:S(2)}) copy-start(bf16[2,2048,512]{2,1,0:T(8,128)(2,1)} %refs_10_.3) | copy-start | bytes 12582916
  19.2 3.4 %collective-permute-start = (bf16[128,512]{1,0:T(8,128)(2,1)}, bf16[128,512]{1,0:T(8,128)(2,1)S(1)}, u32[]{:S(2)}, u32[]{:S(2)}) collective-permute-start(bf16[128,512]{1,0:T(8,128)(2,1)} %get-tuple-element.69), channel_id=1, source_target_pairs={{0,1},{1,0},{2,3},{3,2},{4,5},{5,4},{6,7},{7,6},{8,9},{9,8},{10,11... | collective-permute-start | bytes 393224 | tf_op jit(solution)/shard_map/to_experts/ppermute | solution.py:1077
  20.0 5.3 %collective-permute-start.1 = (bf16[128,512]{1,0:T(8,128)(2,1)}, bf16[128,512]{1,0:T(8,128)(2,1)S(1)}, u32[]{:S(2)}, u32[]{:S(2)}) collective-permute-start(bf16[128,512]{1,0:T(8,128)(2,1)} %get-tuple-element.70), channel_id=1, source_target_pairs={{0,2},{1,3},{2,0},{3,1},{4,6},{5,7},{6,4},{7,5},{8,10},{9,11},{10,... | collective-permute-start | bytes 393224 | tf_op jit(solution)/shard_map/to_experts/ppermute | solution.py:1077
  21.2 7.0 %collective-permute-start.2 = (bf16[128,512]{1,0:T(8,128)(2,1)}, bf16[128,512]{1,0:T(8,128)(2,1)S(1)}, u32[]{:S(2)}, u32[]{:S(2)}) collective-permute-start(bf16[128,512]{1,0:T(8,128)(2,1)} %get-tuple-element.71), channel_id=1, source_target_pairs={{0,3},{1,2},{2,1},{3,0},{4,7},{5,6},{6,5},{7,4},{8,11},{9,10},{10,... | collective-permute-start | bytes 393224 | tf_op jit(solution)/shard_map/to_experts/ppermute | solution.py:1077
  28.2 15.9 %copy-start.43 = (bf16[512,8]{0,1:T(8,128)(2,1)S(1)}, bf16[512,8]{0,1:T(8,128)(2,1)}, u32[]{:S(2)}) copy-start(bf16[512,8]{0,1:T(8,128)(2,1)} %param.22) | copy-start | bytes 24580
  28.2 15.9 %copy-start.44 = (f32[512]{0:T(512)S(1)}, f32[512]{0:T(512)}, u32[]{:S(2)}) copy-start(f32[512]{0:T(512)} %param.21) | copy-start | bytes 6148
  28.2 6.9 %copy-start.16 = (bf16[512,512]{1,0:T(8,128)(2,1)}, bf16[512,512]{1,0:T(8,128)(2,1)S(1)}, u32[]{:S(2)}) copy-start(bf16[512,512]{1,0:T(8,128)(2,1)S(1)} %constant_dynamic-update-slice_fusion.refs_0_) | copy-start | bytes 1572868
  28.3 13.3 %collective-permute-start.6 = (bf16[512,512]{1,0:T(8,128)(2,1)S(1)}, bf16[512,512]{1,0:T(8,128)(2,1)S(1)}, u32[]{:S(2)}, u32[]{:S(2)}) collective-permute-start(bf16[512,512]{1,0:T(8,128)(2,1)S(1)} %constant_dynamic-update-slice_fusion.refs_0_), channel_id=1, source_target_pairs={{0,8},{8,16},{16,24},{24,28},{28,20},{20,12},{12,4},{4,0},{1,9},{9... | collective-permute-start | bytes 1572872 | tf_op jit(solution)/shard_map/gather_for_weights/ppermute | solution.py:1082
  28.5 13.3 %collective-permute-start.8 = (bf16[512,512]{1,0:T(8,128)(2,1)S(1)}, bf16[512,512]{1,0:T(8,128)(2,1)S(1)}, u32[]{:S(2)}, u32[]{:S(2)}) collective-permute-start(bf16[512,512]{1,0:T(8,128)(2,1)S(1)} %constant_dynamic-update-slice_fusion.refs_0_), channel_id=1, source_target_pairs={{8,0},{16,8},{24,16},{28,24},{20,28},{12,20},{4,12},{0,4},{9,1},{1... | collective-permute-start | bytes 1572872 | tf_op jit(solution)/shard_map/gather_for_weights/ppermute | solution.py:1082
  30.7 13.4 %copy-start.26 = (bf16[1024,512]{1,0:T(8,128)(2,1)S(1)}, bf16[1024,512]{1,0:T(8,128)(2,1)}, u32[]{:S(2)}) copy-start(bf16[1024,512]{1,0:T(8,128)(2,1)} %cot_far.3) | copy-start | bytes 3145732
  30.7 13.4 %copy-start.27 = (bf16[512,512]{1,0:T(8,128)(2,1)S(1)}, bf16[512,512]{1,0:T(8,128)(2,1)}, u32[]{:S(2)}) copy-start(bf16[512,512]{1,0:T(8,128)(2,1)} %w_out_far.3) | copy-start | bytes 1572868
  30.7 13.4 %copy-start.45 = (f32[1024,512]{1,0:T(8,128)S(1)}, f32[1024,512]{1,0:T(8,128)}, u32[]{:S(2)}) copy-start(f32[1024,512]{1,0:T(8,128)} %get-tuple-element.76.hidden_far) | copy-start | bytes 6291460
  30.7 13.4 %copy-start.46 = (f32[1024,256]{1,0:T(8,128)S(1)}, f32[1024,256]{1,0:T(8,128)}, u32[]{:S(2)}) copy-start(f32[1024,256]{1,0:T(8,128)} %get-tuple-element.77.mix_far) | copy-start | bytes 3145732
  30.7 13.4 %copy-start.47 = (bf16[1024,512]{1,0:T(8,128)(2,1)S(1)}, bf16[1024,512]{1,0:T(8,128)(2,1)}, u32[]{:S(2)}) copy-start(bf16[1024,512]{1,0:T(8,128)(2,1)} %get-tuple-element.78.attended_far) | copy-start | bytes 3145732
  35.2 7.9 %collective-permute-start.3 = (bf16[128,512]{1,0:T(8,128)(2,1)S(1)}, bf16[128,512]{1,0:T(8,128)(2,1)S(1)}, u32[]{:S(2)}, u32[]{:S(2)}) collective-permute-start(bf16[128,512]{1,0:T(8,128)(2,1)S(1)} %get-tuple-element.73), channel_id=1, source_target_pairs={{0,1},{1,0},{2,3},{3,2},{4,5},{5,4},{6,7},{7,6},{8,9},{9,8},{10,11... | collective-permute-start | bytes 393224 | tf_op jit(solution)/shard_map/from_experts/ppermute | solution.py:1077
  36.0 7.1 %collective-permute-start.4 = (bf16[128,512]{1,0:T(8,128)(2,1)S(1)}, bf16[128,512]{1,0:T(8,128)(2,1)S(1)}, u32[]{:S(2)}, u32[]{:S(2)}) collective-permute-start(bf16[128,512]{1,0:T(8,128)(2,1)S(1)} %get-tuple-element.74), channel_id=1, source_target_pairs={{0,2},{1,3},{2,0},{3,1},{4,6},{5,7},{6,4},{7,5},{8,10},{9,11},{10,... | collective-permute-start | bytes 393224 | tf_op jit(solution)/shard_map/from_experts/ppermute | solution.py:1077
  37.3 6.8 %collective-permute-start.5 = (bf16[128,512]{1,0:T(8,128)(2,1)S(1)}, bf16[128,512]{1,0:T(8,128)(2,1)S(1)}, u32[]{:S(2)}, u32[]{:S(2)}) collective-permute-start(bf16[128,512]{1,0:T(8,128)(2,1)S(1)} %get-tuple-element.75), channel_id=1, source_target_pairs={{0,3},{1,2},{2,1},{3,0},{4,7},{5,6},{6,5},{7,4},{8,11},{9,10},{10,... | collective-permute-start | bytes 393224 | tf_op jit(solution)/shard_map/from_experts/ppermute | solution.py:1077
  41.6 10.5 %copy-start.28 = (bf16[512,512]{1,0:T(8,128)(2,1)}, bf16[512,512]{1,0:T(8,128)(2,1)S(1)}, u32[]{:S(2)}) copy-start(bf16[512,512]{1,0:T(8,128)(2,1)S(1)} %collective-permute-done.6.refs_1_) | copy-start | bytes 1572868
  41.6 12.4 %collective-permute-start.7 = (bf16[512,512]{1,0:T(8,128)(2,1)S(1)}, bf16[512,512]{1,0:T(8,128)(2,1)S(1)}, u32[]{:S(2)}, u32[]{:S(2)}) collective-permute-start(bf16[512,512]{1,0:T(8,128)(2,1)S(1)} %collective-permute-done.6.refs_1_), channel_id=1, source_target_pairs={{0,8},{8,16},{16,24},{24,28},{28,20},{20,12},{12,4},{4,0},{1,9},{9... | collective-permute-start | bytes 1572872 | tf_op jit(solution)/shard_map/gather_for_weights/ppermute | solution.py:1082
  41.8 10.4 %copy-start.31 = (bf16[512,512]{1,0:T(8,128)(2,1)}, bf16[512,512]{1,0:T(8,128)(2,1)S(1)}, u32[]{:S(2)}) copy-start(bf16[512,512]{1,0:T(8,128)(2,1)S(1)} %collective-permute-done.8.refs_2_) | copy-start | bytes 1572868
  41.8 12.2 %collective-permute-start.9 = (bf16[512,512]{1,0:T(8,128)(2,1)S(1)}, bf16[512,512]{1,0:T(8,128)(2,1)S(1)}, u32[]{:S(2)}, u32[]{:S(2)}) collective-permute-start(bf16[512,512]{1,0:T(8,128)(2,1)S(1)} %collective-permute-done.8.refs_2_), channel_id=1, source_target_pairs={{8,0},{16,8},{24,16},{28,24},{20,28},{12,20},{4,12},{0,4},{9,1},{1... | collective-permute-start | bytes 1572872 | tf_op jit(solution)/shard_map/gather_for_weights/ppermute | solution.py:1082
  44.1 14.0 %copy-start.48 = (bf16[8,1024,128]{2,1,0:T(8,128)(2,1)S(1)}, bf16[8,1024,128]{2,1,0:T(8,128)(2,1)}, u32[]{:S(2)}) copy-start(bf16[8,1024,128]{2,1,0:T(8,128)(2,1)} %get-tuple-element.81.queries_far) | copy-start | bytes 6291460
  44.1 14.0 %copy-start.49 = (bf16[8,1024,128]{2,1,0:T(8,128)(2,1)S(1)}, bf16[8,1024,128]{2,1,0:T(8,128)(2,1)}, u32[]{:S(2)}) copy-start(bf16[8,1024,128]{2,1,0:T(8,128)(2,1)} %get-tuple-element.82.keys_far) | copy-start | bytes 6291460
  44.1 14.0 %copy-start.50 = (bf16[8,1024,128]{2,1,0:T(8,128)(2,1)S(1)}, bf16[8,1024,128]{2,1,0:T(8,128)(2,1)}, u32[]{:S(2)}) copy-start(bf16[8,1024,128]{2,1,0:T(8,128)(2,1)} %get-tuple-element.83.values_far) | copy-start | bytes 6291460
  44.2 14.0 %copy-start.51 = (bf16[1024,512]{1,0:T(8,128)(2,1)S(1)}, bf16[1024,512]{1,0:T(8,128)(2,1)}, u32[]{:S(2)}) copy-start(bf16[1024,512]{1,0:T(8,128)(2,1)} %get-tuple-element.87.normed_far) | copy-start | bytes 3145732
  54.0 21.4 %copy-start.34 = (bf16[512,512]{1,0:T(8,128)(2,1)}, bf16[512,512]{1,0:T(8,128)(2,1)S(1)}, u32[]{:S(2)}) copy-start(bf16[512,512]{1,0:T(8,128)(2,1)S(1)} %collective-permute-done.7.refs_3_) | copy-start | bytes 1572868
  54.0 21.4 %copy-start.37 = (bf16[512,512]{1,0:T(8,128)(2,1)}, bf16[512,512]{1,0:T(8,128)(2,1)S(1)}, u32[]{:S(2)}) copy-start(bf16[512,512]{1,0:T(8,128)(2,1)S(1)} %collective-permute-done.9.refs_4_) | copy-start | bytes 1572868
  54.0 21.4 %collective-permute-start.10 = (bf16[512,512]{1,0:T(8,128)(2,1)S(1)}, bf16[512,512]{1,0:T(8,128)(2,1)S(1)}, u32[]{:S(2)}, u32[]{:S(2)}) collective-permute-start(bf16[512,512]{1,0:T(8,128)(2,1)S(1)} %collective-permute-done.7.refs_3_), channel_id=1, source_target_pairs={{0,8},{8,16},{16,24},{24,28},{28,20},{20,12},{12,4},{4,0},{1,9},{9... | collective-permute-start | bytes 1572872 | tf_op jit(solution)/shard_map/gather_for_weights/ppermute | solution.py:1082
  54.2 21.2 %collective-permute-start.11 = (bf16[512,512]{1,0:T(8,128)(2,1)S(1)}, bf16[512,512]{1,0:T(8,128)(2,1)S(1)}, u32[]{:S(2)}, u32[]{:S(2)}) collective-permute-start(bf16[512,512]{1,0:T(8,128)(2,1)S(1)} %collective-permute-done.9.refs_4_), channel_id=1, source_target_pairs={{8,0},{16,8},{24,16},{28,24},{20,28},{12,20},{4,12},{0,4},{9,1},{1... | collective-permute-start | bytes 1572872 | tf_op jit(solution)/shard_map/gather_for_weights/ppermute | solution.py:1082
  55.5 19.9 %collective-permute-start.12 = (bf16[256,640]{1,0:T(8,128)(2,1)S(1)}, bf16[256,640]{1,0:T(8,128)(2,1)S(1)}, u32[]{:S(2)}, u32[]{:S(2)}) collective-permute-start(bf16[256,640]{1,0:T(8,128)(2,1)S(1)} %get-tuple-element.92), channel_id=1, source_target_pairs={{0,1},{1,0},{2,3},{3,2},{4,5},{5,4},{6,7},{7,6},{8,9},{9,8},{10,11... | collective-permute-start | bytes 983048 | tf_op jit(solution)/shard_map/reduce/ppermute | solution.py:1094
  75.4 3.7 %copy-start = (bf16[4,1024,384]{2,1,0:T(8,128)(2,1)}, bf16[4,1024,384]{2,1,0:T(8,128)(2,1)S(1)}, u32[]{:S(2)}) copy-start(bf16[4,1024,384]{2,1,0:T(8,128)(2,1)S(1)} %get-tuple-element.104.grads) | copy-start | bytes 9437188
  75.4 3.6 %copy-start.9 = (bf16[512,512]{1,0:T(8,128)(2,1)}, bf16[512,512]{1,0:T(8,128)(2,1)S(1)}, u32[]{:S(2)}) copy-start(bf16[512,512]{1,0:T(8,128)(2,1)S(1)} %collective-permute-done.10.refs_5_) | copy-start | bytes 1572868
  75.4 3.6 %copy-start.12 = (bf16[512,512]{1,0:T(8,128)(2,1)}, bf16[512,512]{1,0:T(8,128)(2,1)S(1)}, u32[]{:S(2)}) copy-start(bf16[512,512]{1,0:T(8,128)(2,1)S(1)} %collective-permute-done.11.refs_6_) | copy-start | bytes 1572868
  75.5 2.4 %collective-permute-start.13 = (bf16[256,1536]{1,0:T(8,128)(2,1)S(1)}, bf16[256,1536]{1,0:T(8,128)(2,1)S(1)}, u32[]{:S(2)}, u32[]{:S(2)}) collective-permute-start(bf16[256,1536]{1,0:T(8,128)(2,1)S(1)} %get-tuple-element.95), channel_id=1, source_target_pairs={{0,1},{1,0},{2,3},{3,2},{4,5},{5,4},{6,7},{7,6},{8,9},{9,8},{10,11... | collective-permute-start | bytes 2359304 | tf_op jit(solution)/shard_map/reduce/ppermute | solution.py:1094
  75.6 7.4 %collective-permute-start.14 = (bf16[256,512]{1,0:T(8,128)(2,1)S(1)}, bf16[256,512]{1,0:T(8,128)(2,1)S(1)}, u32[]{:S(2)}, u32[]{:S(2)}) collective-permute-start(bf16[256,512]{1,0:T(8,128)(2,1)S(1)} %slice.6), channel_id=1, source_target_pairs={{0,8},{8,16},{16,24},{24,28},{28,20},{20,12},{12,4},{4,0},{1,9},{9... | collective-permute-start | bytes 786440 | tf_op jit(solution)/shard_map/gather_for_weights/ppermute | solution.py:1082
  75.7 7.3 %collective-permute-start.15 = (bf16[256,512]{1,0:T(8,128)(2,1)S(1)}, bf16[256,512]{1,0:T(8,128)(2,1)S(1)}, u32[]{:S(2)}, u32[]{:S(2)}) collective-permute-start(bf16[256,512]{1,0:T(8,128)(2,1)S(1)} %slice.7), channel_id=1, source_target_pairs={{8,0},{16,8},{24,16},{28,24},{20,28},{12,20},{4,12},{0,4},{9,1},{1... | collective-permute-start | bytes 786440 | tf_op jit(solution)/shard_map/gather_for_weights/ppermute | solution.py:1082
  77.8 12.7 %copy-start.19 = (f32[512]{0:T(512)S(1)}, f32[512]{0:T(512)}, u32[]{:S(2)}) copy-start(f32[512]{0:T(512)} %param.16) | copy-start | bytes 6148
  83.7 32.9 %all-to-all-start = ((bf16[16,16,2176]{2,1,0:T(8,128)(2,1)}), bf16[16,16,2176]{2,1,0:T(8,128)(2,1)S(1)}, u32[]{:S(2)}, u32[]{:S(2)}) async-start(bf16[16,16,2176]{2,1,0:T(8,128)(2,1)} %bitcast.5), calls=%async_computation | async-start | bytes 2228224 | tf_op jit(solution)/shard_map/reduce/all_to_all | solution.py:1098
  90.5 1.9 %copy-start.1 = (bf16[4,1024,384]{2,1,0:T(8,128)(2,1)S(1)}, bf16[4,1024,384]{2,1,0:T(8,128)(2,1)}, u32[]{:S(2)}) copy-start(bf16[4,1024,384]{2,1,0:T(8,128)(2,1)} %copy-done) | copy-start | bytes 9437188
  92.4 1.0 copy-start.2
  93.4 1.0 copy-start.4
  95.5 1.2 copy-start.8
  96.7 4.2 %copy-start.10 = (bf16[512,512]{1,0:T(8,128)(2,1)S(1)}, bf16[512,512]{1,0:T(8,128)(2,1)}, u32[]{:S(2)}) copy-start(bf16[512,512]{1,0:T(8,128)(2,1)} %copy-done.9) | copy-start | bytes 1572868
  96.7 4.2 %copy-start.13 = (bf16[512,512]{1,0:T(8,128)(2,1)S(1)}, bf16[512,512]{1,0:T(8,128)(2,1)}, u32[]{:S(2)}) copy-start(bf16[512,512]{1,0:T(8,128)(2,1)} %copy-done.12) | copy-start | bytes 1572868
  96.8 4.2 %copy-start.17 = (bf16[512,512]{1,0:T(8,128)(2,1)S(1)}, bf16[512,512]{1,0:T(8,128)(2,1)}, u32[]{:S(2)}) copy-start(bf16[512,512]{1,0:T(8,128)(2,1)} %copy-done.16) | copy-start | bytes 1572868
  96.8 4.2 %copy-start.21 = (bf16[2,512,2048]{2,1,0:T(8,128)(2,1)S(1)}, bf16[2,512,2048]{2,1,0:T(8,128)(2,1)}, u32[]{:S(2)}) copy-start(bf16[2,512,2048]{2,1,0:T(8,128)(2,1)} %refs_9_.3) | copy-start | bytes 12582916
  96.8 4.2 %copy-start.29 = (bf16[512,512]{1,0:T(8,128)(2,1)S(1)}, bf16[512,512]{1,0:T(8,128)(2,1)}, u32[]{:S(2)}) copy-start(bf16[512,512]{1,0:T(8,128)(2,1)} %copy-done.28) | copy-start | bytes 1572868
  96.8 4.2 %copy-start.32 = (bf16[512,512]{1,0:T(8,128)(2,1)S(1)}, bf16[512,512]{1,0:T(8,128)(2,1)}, u32[]{:S(2)}) copy-start(bf16[512,512]{1,0:T(8,128)(2,1)} %copy-done.31) | copy-start | bytes 1572868
  96.8 4.2 %copy-start.35 = (bf16[512,512]{1,0:T(8,128)(2,1)S(1)}, bf16[512,512]{1,0:T(8,128)(2,1)}, u32[]{:S(2)}) copy-start(bf16[512,512]{1,0:T(8,128)(2,1)} %copy-done.34) | copy-start | bytes 1572868
  96.8 4.2 %copy-start.38 = (bf16[512,512]{1,0:T(8,128)(2,1)S(1)}, bf16[512,512]{1,0:T(8,128)(2,1)}, u32[]{:S(2)}) copy-start(bf16[512,512]{1,0:T(8,128)(2,1)} %copy-done.37) | copy-start | bytes 1572868
  96.8 4.2 %copy-start.41 = (bf16[256,512]{1,0:T(8,128)(2,1)S(1)}, bf16[256,512]{1,0:T(8,128)(2,1)}, u32[]{:S(2)}) copy-start(bf16[256,512]{1,0:T(8,128)(2,1)} %copy-done.40) | copy-start | bytes 786436
  101.0 2.2 %copy-start.24 = (bf16[2,2048,512]{2,1,0:T(8,128)(2,1)S(1)}, bf16[2,2048,512]{2,1,0:T(8,128)(2,1)}, u32[]{:S(2)}) copy-start(bf16[2,2048,512]{2,1,0:T(8,128)(2,1)} %refs_10_.3) | copy-start | bytes 12582916
  116.6 5.2 %copy-start.11 = (bf16[512,512]{1,0:T(8,128)(2,1)S(1)}, bf16[512,512]{1,0:T(8,128)(2,1)}, u32[]{:S(2)}) copy-start(bf16[512,512]{1,0:T(8,128)(2,1)} %copy-done.9) | copy-start | bytes 1572868
  117.8 30.1 %all-to-all-start.1 = ((bf16[16,16,2176]{2,1,0:T(8,128)(2,1)}), bf16[16,16,2176]{2,1,0:T(8,128)(2,1)S(1)}, u32[]{:S(2)}, u32[]{:S(2)}) async-start(bf16[16,16,2176]{2,1,0:T(8,128)(2,1)} %reduce.3), calls=%async_computation.1 | async-start | bytes 2228224 | tf_op jit(solution)/shard_map/reduce/all_to_all | solution.py:1101
  121.8 1.0 copy-start.14
  122.8 1.0 copy-start.18
  123.9 2.2 %copy-start.22 = (bf16[2,512,2048]{2,1,0:T(8,128)(2,1)S(1)}, bf16[2,512,2048]{2,1,0:T(8,128)(2,1)}, u32[]{:S(2)}) copy-start(bf16[2,512,2048]{2,1,0:T(8,128)(2,1)} %refs_9_.3) | copy-start | bytes 12582916
  126.1 2.2 %copy-start.25 = (bf16[2,2048,512]{2,1,0:T(8,128)(2,1)S(1)}, bf16[2,2048,512]{2,1,0:T(8,128)(2,1)}, u32[]{:S(2)}) copy-start(bf16[2,2048,512]{2,1,0:T(8,128)(2,1)} %refs_10_.3) | copy-start | bytes 12582916
  128.3 1.0 copy-start.30
  133.4 19.4 %copy-start.3 = (bf16[512,512]{1,0:T(8,128)(2,1)S(1)}, bf16[512,512]{1,0:T(8,128)(2,1)}, u32[]{:S(2)}) copy-start(bf16[512,512]{1,0:T(8,128)(2,1)} %w_query_far.3) | copy-start | bytes 1572868
  133.4 19.4 %copy-start.5 = (bf16[512,512]{1,0:T(8,128)(2,1)S(1)}, bf16[512,512]{1,0:T(8,128)(2,1)}, u32[]{:S(2)}) copy-start(bf16[512,512]{1,0:T(8,128)(2,1)} %w_key_far.3) | copy-start | bytes 1572868
  133.4 19.4 %copy-start.7 = (bf16[512,512]{1,0:T(8,128)(2,1)S(1)}, bf16[512,512]{1,0:T(8,128)(2,1)}, u32[]{:S(2)}) copy-start(bf16[512,512]{1,0:T(8,128)(2,1)} %w_value_far.3) | copy-start | bytes 1572868
  147.9 4.9 %collective-permute-start.16 = (bf16[256,2176]{1,0:T(8,128)(2,1)S(1)}, bf16[256,2176]{1,0:T(8,128)(2,1)S(1)}, u32[]{:S(2)}, u32[]{:S(2)}) collective-permute-start(bf16[256,2176]{1,0:T(8,128)(2,1)S(1)} %bitcast.11), channel_id=1, source_target_pairs={{0,1},{1,0},{2,3},{3,2},{4,5},{5,4},{6,7},{7,6},{8,9},{9,8},{10,11... | collective-permute-start | bytes 3342344 | tf_op jit(solution)/shard_map/reduce/ppermute | solution.py:1094
  (7 other events, 6.7 us)

commit v3 on v2

--- a/solution.py
+++ b/solution.py
@@ -717,80 +717,54 @@
         spread[number] = total
 
 
-def assemble_kernel(
-    near,
-    both_own,
-    both_other,
-    gain1_far,
-    w_query_far,
-    w_key_far,
-    w_value_far,
-    grad_query_far,
-    grad_key_far,
-    grad_value_far,
-    grad_out_far,
-    grad_control,
-    grad_gain1,
-    grad_gain2,
-    gain1,
-    weights,
-    squares,
-    columns,
-    in_sems,
-    out_sems,
-):
+def half_kernel(step, near, both, w_query_far, w_key_far, w_value_far, *refs):
+    grad_query_far, grad_key_far, grad_value_far, grad_out_far, columns = refs[-9:-4]
+    squares, weights, in_sems, out_sems = refs[-4:]
+    half = D // 2
+    side = near[0] if step == 0 else 1 - near[0]
+    rows = pl.ds(pl.multiple_of(side * half, half), half)
     ins = loads(
         [
-            (gain1_far, gain1),
-            (w_query_far, weights.at[0]),
-            (w_key_far, weights.at[1]),
-            (w_value_far, weights.at[2]),
+            (far_weight.at[rows], weights.at[number])
+            for number, far_weight in enumerate((w_query_far, w_key_far, w_value_far))
         ],
         in_sems,
     )
     begin(ins)
+    targets = (grad_query_far, grad_key_far, grad_value_far, grad_out_far)
+    outs = loads(
+        [(squares.at[number], target.at[rows]) for number, target in enumerate(targets)], out_sems
+    )
+    squares[3] = both[:, :D].astype(F32)
+    begin(outs[3:])
+    finish(ins)
+    shared = 0.0
+    for number in range(3):
+        for pair in range(PAIRS):
+            first = D + PAIR + (3 * pair + number) * PAIR
+            part = both[:, first : first + PAIR].astype(F32)
+            cols = slice(pair * PAIR, (pair + 1) * PAIR)
+            squares[number, :, cols] = part
+            shared = shared + part * weights[number, :, cols].astype(F32)
+        begin(outs[number : number + 1])
+    lane = lax.broadcasted_iota(jnp.int32, (half, PAIR), 1)
+    columns[...] = jnp.where(
+        lane == PAIR - 1,
+        jnp.sum(shared, axis=1, keepdims=True),
+        both[:, D : D + PAIR].astype(F32),
+    )
+    finish(outs)
+
+
+def small_kernel(near, own, other, gain1, grad_control, grad_gain1, grad_gain2, columns):
     half = D // 2
     experts = grad_control.shape[0]
-    targets = (grad_query_far, grad_key_far, grad_value_far, grad_out_far)
-    lane = lax.broadcasted_iota(jnp.int32, (half, PAIR), 1)
-    outs = []
-    for step, both in enumerate((both_own, both_other)):
-        side = near[0] if step == 0 else 1 - near[0]
-        rows = pl.ds(pl.multiple_of(side * half, half), half)
-        outs.append(
-            loads(
-                [
-                    (squares.at[number, rows], target.at[rows])
-                    for number, target in enumerate(targets)
-                ],
-                out_sems,
-                len(targets) * step,
-            )
-        )
-        squares[3, rows, :] = both[:, :D].astype(F32)
-        begin(outs[-1][3:])
-        if step == 0:
-            finish(ins)
-        shared = 0.0
-        for number in range(3):
-            for pair in range(PAIRS):
-                first = D + PAIR + (3 * pair + number) * PAIR
-                part = both[:, first : first + PAIR].astype(F32)
-                cols = slice(pair * PAIR, (pair + 1) * PAIR)
-                squares[number, rows, cols] = part
-                shared = shared + part * weights[number, rows, cols].astype(F32)
-            begin(outs[-1][number : number + 1])
-        columns[rows, :] = jnp.where(
-            lane == experts + 1,
-            jnp.sum(shared, axis=1, keepdims=True),
-            both[:, D : D + PAIR].astype(F32),
-        )
+    for side, part in ((near[0], own), (1 - near[0], other)):
+        columns[pl.ds(pl.multiple_of(side * half, half), half), :] = part[...]
     turned = columns[...].T
     grad_control[...] = turned[:experts]
     grad_gain2[...] = turned[experts : experts + 1]
-    grad_gain1[...] = turned[experts + 1 : experts + 2] / gain1[...]
-    for one in outs:
-        finish(one)
+    grad_gain1[...] = turned[PAIR - 1 :] / gain1[...]
 
 
 def vmem():
@@ -1016,24 +990,36 @@
     )(parts)
 
 
-def assemble_call(near, both_own, both_other, gain1, weights, experts):
+def half_call(step, near, both, weights, earlier):
     square = shape(D, D, kind=F32)
+    half = D // 2
     return pl.pallas_call(
-        assemble_kernel,
-        in_specs=[smem()] + [vmem()] * 2 + [far()] * 4,
-        out_specs=[far()] * 4 + [vmem()] * 3,
-        out_shape=[square] * 4 + [shape(experts, D, kind=F32)] + [shape(1, D, kind=F32)] * 2,
+        functools.partial(half_kernel, step),
+        in_specs=[smem(), vmem()] + [far()] * (3 + len(earlier)),
+        out_specs=[far()] * 4 + [vmem()],
+        out_shape=[square] * 4 + [shape(half, PAIR, kind=F32)],
         scratch_shapes=[
-            pltpu.VMEM((1, D), F32),
-            pltpu.VMEM((3, D, D), LOW),
-            pltpu.VMEM((4, D, D), F32),
-            pltpu.VMEM((D, PAIR), F32),
+            pltpu.VMEM((4, half, D), F32),
+            pltpu.VMEM((3, half, D), LOW),
+            dma(3),
             dma(4),
-            dma(8),
         ],
+        input_output_aliases={5 + i: i for i in range(len(earlier))},
         compiler_params=params(40),
         cost_estimate=cost(1e8, 6e6),
-    )(near, both_own, both_other, gain1, *weights)
+    )(near, both, *weights, *earlier)
+
+
+def small_call(near, own, other, gain1, experts):
+    return pl.pallas_call(
+        small_kernel,
+        in_specs=[smem()] + [vmem()] * 3,
+        out_specs=[vmem()] * 3,
+        out_shape=[shape(experts, D, kind=F32)] + [shape(1, D, kind=F32)] * 2,
+        scratch_shapes=[pltpu.VMEM((D, PAIR), F32)],
+        compiler_params=params(16),
+        cost_estimate=cost(1e6, 1e6),
+    )(near, own, other, gain1)
 
 
 def in_order(*values):
@@ -1161,8 +1147,11 @@
     with jax.named_scope("reduce"):
         sums_other = near_swap(sums)
     with jax.named_scope("assemble"):
-        grad_query, grad_key, grad_value, grad_out, grad_control, grad_gain1, grad_gain2 = (
-            assemble_call(near, sums, sums_other, gain1, weights, experts)
+        *squares, own_columns = half_call(0, near, sums, weights, ())
+        *squares, other_columns = half_call(1, near, sums_other, weights, squares)
+        grad_query, grad_key, grad_value, grad_out = squares
+        grad_control, grad_gain1, grad_gain2 = small_call(
+            near, own_columns, other_columns, gain1, experts
         )
     return (
         output,

time: 157 us -> 156 us (level)
    all_to_all x1, waiting for transfers between devices: 3.45 us -> 5.04 us  [scatter(): lax.all_to_all(half.reshape(count, rows // count, cols), axes, 0, 0, tile...]
    unnamed x107 -> x101, local copies, waits for them, and re-layouts: 22.7 us -> 23.4 us
    pallas_call x1 -> x3, Pallas kernels: 3.09 us -> 3.75 us  [the longest x2 3 us: half_call(): pl.pallas_call(functools.partial(half_kernel, step), in_specs=[smem(), vm...]
  transfers between devices with their start and end apart: 19 -> 19, of which waited for: 10 -> 10; matrix products, arithmetic and copies ran while one was open for 1% -> 1% of each run, Pallas kernels for 35% -> 36%
where the time goes in v3:
time: 156 us; the launch traced here: 155 us
  Pallas kernels  77.5 us (50%)
  starting transfers between devices  27.1 us (17%)
  waiting for transfers between devices  25.9 us (17%)
  local copies, waits for them, and re-layouts  23.5 us (15%)
    unnamed x101, local copies, waits for them, and re-layouts  23.4 us
    pallas_call x2, Pallas kernels, weight_call(): pl.pallas_call(functools.partial(weight_kernel, expert, len(pieces)), gri...  20 us
    pallas_call x1, Pallas kernels, forward_call(): pl.pallas_call(forward_kernel, in_specs=[smem()] + [far()] * 11, out_spec...  18.5 us
    pallas_call x1, Pallas kernels, pair_call(): pl.pallas_call(pair_kernel, in_specs=[smem()] + [far()] * 5, out_specs=[f...  17.2 us
    ppermute x4, waiting for transfers between devices, pass_on(): lax.ppermute(ahead_part, 'dp', ahead)  8.18 us
    pallas_call x1, Pallas kernels, middle_call(): pl.pallas_call(middle_kernel, in_specs=[smem()] * 2 + [vmem()] * 4 + [far...  7.96 us
    all_to_all x1, starting transfers between devices, scatter(): lax.all_to_all(half.reshape(count, rows // count, cols), axes, 0, 0, tile...  6.79 us
    ppermute x6, waiting for transfers between devices, exchange(): lax.ppermute(parts[step], hosts_axes, [(i, i ^ step) for i in range(hosts)])  6.59 us
  transfers between devices with their start and end apart: 19, of which 10 were waited for; matrix products, arithmetic and copies ran while one was open for 1% of the time, Pallas kernels for 36%

profile of v3, /device:TPU:11, one launch (start us, length us, event | category | flops | bytes accessed | tf_op | source)
XLA Modules:
  0.0 155.1 jit_solution(9748924078104242385)
XLA Ops:
  0.7 0.0 copy-start.17
  0.7 18.5 %attention_and_mixing.1 = (bf16[128,512]{1,0:T(8,128)(2,1)}, bf16[128,512]{1,0:T(8,128)(2,1)}, bf16[128,512]{1,0:T(8,128)(2,1)}, bf16[128,512]{1,0:T(8,128)(2,1)...) custom-call(s32[1]{0:T(128)} %bitcast.place, ...), custom_call_target="tpu_custom_call" | custom-call | flops 20000000000 | bytes 20000000 | tf_op jit(solution)/shard_map/attention_and_mixing/pallas_call | solution.py:819
  19.2 0.7 collective-permute-start
  20.0 1.3 collective-permute-start.1
  21.2 0.5 collective-permute-start.2
  21.7 0.9 constant_dynamic-update-slice_fusion.3
  22.6 2.6 %collective-permute-done.1.in2 = bf16[128,512]{1,0:T(8,128)(2,1)S(1)} collective-permute-done((bf16[128,512]{1,0:T(8,128)(2,1)}, bf16[128,512]{1,0:T(8,128)(2,1)S(1)}, u32[]{:S(2)}, u32[]{:S(2)}) %collective-permute-start.1) | collective-permute-done | bytes 131104 | tf_op jit(solution)/shard_map/to_experts/ppermute | solution.py:1063
  25.3 3.0 %collective-permute-done.2.in3 = bf16[128,512]{1,0:T(8,128)(2,1)S(1)} collective-permute-done((bf16[128,512]{1,0:T(8,128)(2,1)}, bf16[128,512]{1,0:T(8,128)(2,1)S(1)}, u32[]{:S(2)}, u32[]{:S(2)}) %collective-permute-start.2) | collective-permute-done | bytes 131104 | tf_op jit(solution)/shard_map/to_experts/ppermute | solution.py:1063
  28.2 0.0 copy-start.13
  28.3 0.2 collective-permute-start.6
  28.5 1.3 collective-permute-start.8
  29.8 0.9 copy-done.12
  30.7 0.0 copy-start.44
  30.7 4.4 %experts.1 = (bf16[128,512]{1,0:T(8,128)(2,1)S(1)}, bf16[128,512]{1,0:T(8,128)(2,1)S(1)}, bf16[128,512]{1,0:T(8,128)(2,1)S(1)}, bf16[128,512]{1,0:T(8,128)(2,1)S(1)}) custom-call(bf16[128,512]{1,0:T(8,128)(2,1)S(1)} %copy-done.12, bf16[128,512]{1,0:T(8,128)(2,1)S(1)} %collective-permute-done.in1, bf16[128,512]{1,0:T(8,128)(2,1)S(1)} %collective-permute-done.1.in2, ...), custom_call_target="tpu_custom_call" | custom-call | flops 5000000000 | bytes 10000000 | tf_op jit(solution)/shard_map/experts/pallas_call | solution.py:852
  35.2 0.9 collective-permute-start.3
  36.0 1.3 collective-permute-start.4
  37.3 0.5 collective-permute-start.5
  37.7 3.9 %collective-permute-done.6.refs_1_ = bf16[512,512]{1,0:T(8,128)(2,1)S(1)} collective-permute-done((bf16[512,512]{1,0:T(8,128)(2,1)S(1)}, bf16[512,512]{1,0:T(8,128)(2,1)S(1)}, u32[]{:S(2)}, u32[]{:S(2)}) %collective-permute-start.6) | collective-permute-done | bytes 524320 | tf_op jit(solution)/shard_map/gather_for_weights/ppermute | solution.py:1068
  41.6 0.2 collective-permute-start.7
  41.8 1.3 collective-permute-start.9
  43.1 1.0 collective-permute-done.5.ret3
  44.2 0.0 copy-start.48
  44.2 8.0 %mixing_backward.1 = (bf16[1024,512]{1,0:T(8,128)(2,1)}, f32[1024,512]{1,0:T(8,128)S(1)}, bf16[8,1024,128]{2,1,0:T(8,128)(2,1)S(1)}, bf16[256,640]{1,0:T(8,128)(2,1)S(1)}, bf16[256,640]{1,0:T(8,128)(2,1)S(1)}) custom-call(s32[1]{0:T(128)} %bitcast.place, s32[1]{0:T(128)} %bitcast.1.near, bf16[128,512]{1,0:T(8,128)(2,1)S(1)} %get-tuple-element.78.ret0, ...), custom_call_target="tpu_custom_call" | custom-call | flops 8000000000 | bytes 15000000 | tf_op jit(solution)/shard_map/mixing_backward/pallas_call | solution.py:874
  52.2 1.3 copy-done.6
  53.5 0.5 collective-permute-done.7.refs_3_
  54.0 0.2 collective-permute-start.10
  54.2 1.3 collective-permute-start.11
  55.5 2.7 %collective-permute-start.12 = (bf16[256,640]{1,0:T(8,128)(2,1)S(1)}, bf16[256,640]{1,0:T(8,128)(2,1)S(1)}, u32[]{:S(2)}, u32[]{:S(2)}) collective-permute-start(bf16[256,640]{1,0:T(8,128)(2,1)S(1)} %get-tuple-element.98), channel_id=1, source_target_pairs={{0,1},{1,0},{2,3},{3,2},{4,5},{5,4},{6,7},{7,6},{8,9},{9,8},{10,11... | collective-permute-start | bytes 983048 | tf_op jit(solution)/shard_map/reduce/ppermute | solution.py:1080
  58.2 17.2 %attention_backward.1 = (bf16[4,1024,384]{2,1,0:T(8,128)(2,1)S(1)}, bf16[256,1536]{1,0:T(8,128)(2,1)S(1)}, bf16[256,1536]{1,0:T(8,128)(2,1)S(1)}) custom-call(s32[1]{0:T(128)} %bitcast.1.near, bf16[8,1024,128]{2,1,0:T(8,128)(2,1)S(1)} %copy-done.45, bf16[8,1024,128]{2,1,0:T(8,128)(2,1)S(1)} %copy-done.46, bf16[8,1024,128]{2,1,0:T(8,128)(2,1)S(1)} %copy-done.47, ...), custom_call_target="tpu_custom_call" | custom-call | flops 20000000000 | bytes 12000000 | tf_op jit(solution)/shard_map/attention_backward/pallas_call | solution.py:899
  75.4 0.1 collective-permute-start.13
  75.5 0.1 collective-permute-start.14
  75.7 1.4 collective-permute-start.15
  77.1 0.7 collective-permute-done.13.swapped
  77.8 1.3 reduce.2
  79.2 3.8 %collective-permute-done.14.refs_7_ = bf16[256,512]{1,0:T(8,128)(2,1)S(1)} collective-permute-done((bf16[256,512]{1,0:T(8,128)(2,1)S(1)}, bf16[256,512]{1,0:T(8,128)(2,1)S(1)}, u32[]{:S(2)}, u32[]{:S(2)}) %collective-permute-start.14) | collective-permute-done | bytes 262176 | tf_op jit(solution)/shard_map/gather_for_weights/ppermute | solution.py:1068
  83.0 0.7 copy-done.37
  83.7 6.8 %all-to-all-start = ((bf16[16,16,2176]{2,1,0:T(8,128)(2,1)}), bf16[16,16,2176]{2,1,0:T(8,128)(2,1)S(1)}, u32[]{:S(2)}, u32[]{:S(2)}) async-start(bf16[16,16,2176]{2,1,0:T(8,128)(2,1)} %bitcast.5), calls=%async_computation | async-start | bytes 2228224 | tf_op jit(solution)/shard_map/reduce/all_to_all | solution.py:1084
  90.5 1.9 %copy-done.5 = bf16[4,1024,384]{2,1,0:T(8,128)(2,1)S(1)} copy-done((bf16[4,1024,384]{2,1,0:T(8,128)(2,1)S(1)}, bf16[4,1024,384]{2,1,0:T(8,128)(2,1)}, u32[]{:S(2)}) %copy-start.5) | copy-done | bytes 3145752
  92.4 1.6 %copy-done.7 = f32[1024,512]{1,0:T(8,128)S(1)} copy-done((f32[1024,512]{1,0:T(8,128)S(1)}, f32[1024,512]{1,0:T(8,128)}, u32[]{:S(2)}) %copy-start.7) | copy-done | bytes 2097176
  94.0 1.2 copy-done.8
  95.2 0.0 copy-start.29
  95.3 4.0 %norm_backward.1 = bf16[1024,512]{1,0:T(8,128)(2,1)} custom-call(bf16[4,1024,384]{2,1,0:T(8,128)(2,1)S(1)} %copy-done.5, bf16[1024,512]{1,0:T(8,128)(2,1)S(1)} %copy-done.8, f32[1024,512]{1,0:T(8,128)S(1)} %copy-done.7, f32[1,512]{1,0:T(1,128)S(1)} %bitcast.14, bf16[512,512]{1,0:T(8,128)(2,1)S(1)} %copy-done, bf16[512,512]{1,0:T(8,128)(2,1)S(1)} %copy-done.1, ...), custom_call_target="tpu_custom_call" | custom-call | flops 2000000000 | bytes 8000000 | tf_op jit(solution)/shard_map/norm_backward/pallas_call | solution.py:956
  99.4 2.2 %copy-done.21 = bf16[2,2048,512]{2,1,0:T(8,128)(2,1)S(1)} copy-done((bf16[2,2048,512]{2,1,0:T(8,128)(2,1)S(1)}, bf16[2,2048,512]{2,1,0:T(8,128)(2,1)}, u32[]{:S(2)}) %copy-start.21) | copy-done | bytes 4194328
  101.6 10.0 %expert_weights.2 = (f32[2,64,2048]{2,1,0:T(8,128)}, f32[2,256,512]{2,1,0:T(8,128)}) custom-call(s32[1]{0:T(128)} %bitcast.6.place, bf16[512,512]{1,0:T(8,128)(2,1)S(1)} %copy-done.14, bf16[512,512]{1,0:T(8,128)(2,1)S(1)} %copy-done.26, bf16[512,512]{1,0:T(8,128)(2,1)S(1)} %copy-done.29, bf16[512,512]{1,0:T(8,128)(2,1)S(1)} %copy-done.32, ...), custom_call_target="tpu_custom_call" | custom-call | flops 10000000000 | bytes 8000000 | tf_op jit(solution)/shard_map/expert_weights/pallas_call | solution.py:923
  111.6 5.0 %all-to-all-done.parts = bf16[16,16,2176]{2,1,0:T(8,128)(2,1)S(1)} async-done(((bf16[16,16,2176]{2,1,0:T(8,128)(2,1)}), bf16[16,16,2176]{2,1,0:T(8,128)(2,1)S(1)}, u32[]{:S(2)}, u32[]{:S(2)}) %all-to-all-start) | async-done | bytes 1114144 | tf_op jit(solution)/shard_map/reduce/all_to_all | solution.py:1084
  116.6 0.2 reduce.3
  116.8 1.0 copy-done.3
  117.8 4.0 %all-to-all-start.1 = ((bf16[16,16,2176]{2,1,0:T(8,128)(2,1)}), bf16[16,16,2176]{2,1,0:T(8,128)(2,1)S(1)}, u32[]{:S(2)}, u32[]{:S(2)}) async-start(bf16[16,16,2176]{2,1,0:T(8,128)(2,1)} %copy-done.3), calls=%async_computation.1 | async-start | bytes 2228224 | tf_op jit(solution)/shard_map/reduce/all_to_all | solution.py:1087
  121.8 1.0 copy-done.11
  122.8 1.0 copy-done.15
  123.9 2.2 %copy-done.19 = bf16[2,512,2048]{2,1,0:T(8,128)(2,1)S(1)} copy-done((bf16[2,512,2048]{2,1,0:T(8,128)(2,1)S(1)}, bf16[2,512,2048]{2,1,0:T(8,128)(2,1)}, u32[]{:S(2)}) %copy-start.19) | copy-done | bytes 4194328
  126.1 2.2 %copy-done.22 = bf16[2,2048,512]{2,1,0:T(8,128)(2,1)S(1)} copy-done((bf16[2,2048,512]{2,1,0:T(8,128)(2,1)S(1)}, bf16[2,2048,512]{2,1,0:T(8,128)(2,1)}, u32[]{:S(2)}) %copy-start.22) | copy-done | bytes 4194328
  128.2 1.0 copy-done.27
  129.3 1.0 copy-done.30
  130.3 1.0 copy-done.33
  131.4 1.0 copy-done.36
  132.4 0.9 copy-done.39
  133.4 10.0 %expert_weights.3 = (f32[2,64,2048]{2,1,0:T(8,128)}, f32[2,256,512]{2,1,0:T(8,128)}) custom-call(s32[1]{0:T(128)} %bitcast.6.place, bf16[512,512]{1,0:T(8,128)(2,1)S(1)} %copy-done.15, bf16[512,512]{1,0:T(8,128)(2,1)S(1)} %copy-done.27, bf16[512,512]{1,0:T(8,128)(2,1)S(1)} %copy-done.30, ...), custom_call_target="tpu_custom_call", output_to_operand_aliasing={{0}: (12, {}), {1}: (13, {})} | custom-call | flops 10000000000 | bytes 8000000 | tf_op jit(solution)/shard_map/expert_weights/pallas_call | solution.py:923
  143.4 4.5 %all-to-all-done.1 = bf16[16,16,2176]{2,1,0:T(8,128)(2,1)S(1)} async-done(((bf16[16,16,2176]{2,1,0:T(8,128)(2,1)}), bf16[16,16,2176]{2,1,0:T(8,128)(2,1)S(1)}, u32[]{:S(2)}, u32[]{:S(2)}) %all-to-all-start.1) | async-done | bytes 1114144 | tf_op jit(solution)/shard_map/reduce/all_to_all | solution.py:1087
  147.9 2.5 %collective-permute-start.16 = (bf16[256,2176]{1,0:T(8,128)(2,1)S(1)}, bf16[256,2176]{1,0:T(8,128)(2,1)S(1)}, u32[]{:S(2)}, u32[]{:S(2)}) collective-permute-start(bf16[256,2176]{1,0:T(8,128)(2,1)S(1)} %bitcast.11), channel_id=1, source_target_pairs={{0,1},{1,0},{2,3},{3,2},{4,5},{5,4},{6,7},{7,6},{8,9},{9,8},{10,11... | collective-permute-start | bytes 3342344 | tf_op jit(solution)/shard_map/reduce/ppermute | solution.py:1080
  150.4 1.5 assemble.3
  151.9 0.9 collective-permute-done.16.both
  152.8 1.5 assemble.4
  154.3 0.7 assemble.5
  (90 shorter events, 0.2 us)
Async XLA Ops:
  0.7 29.1 %copy-start.17 = (bf16[2,512,2048]{2,1,0:T(8,128)(2,1)S(1)}, bf16[2,512,2048]{2,1,0:T(8,128)(2,1)}, u32[]{:S(2)}) copy-start(bf16[2,512,2048]{2,1,0:T(8,128)(2,1)} %refs_9_.3) | copy-start | bytes 12582916
  0.7 29.1 %copy-start.20 = (bf16[2,2048,512]{2,1,0:T(8,128)(2,1)S(1)}, bf16[2,2048,512]{2,1,0:T(8,128)(2,1)}, u32[]{:S(2)}) copy-start(bf16[2,2048,512]{2,1,0:T(8,128)(2,1)} %refs_10_.3) | copy-start | bytes 12582916
  19.2 3.4 %collective-permute-start = (bf16[128,512]{1,0:T(8,128)(2,1)}, bf16[128,512]{1,0:T(8,128)(2,1)S(1)}, u32[]{:S(2)}, u32[]{:S(2)}) collective-permute-start(bf16[128,512]{1,0:T(8,128)(2,1)} %get-tuple-element.75), channel_id=1, source_target_pairs={{0,1},{1,0},{2,3},{3,2},{4,5},{5,4},{6,7},{7,6},{8,9},{9,8},{10,11... | collective-permute-start | bytes 393224 | tf_op jit(solution)/shard_map/to_experts/ppermute | solution.py:1063
  20.0 5.3 %collective-permute-start.1 = (bf16[128,512]{1,0:T(8,128)(2,1)}, bf16[128,512]{1,0:T(8,128)(2,1)S(1)}, u32[]{:S(2)}, u32[]{:S(2)}) collective-permute-start(bf16[128,512]{1,0:T(8,128)(2,1)} %get-tuple-element.76), channel_id=1, source_target_pairs={{0,2},{1,3},{2,0},{3,1},{4,6},{5,7},{6,4},{7,5},{8,10},{9,11},{10,... | collective-permute-start | bytes 393224 | tf_op jit(solution)/shard_map/to_experts/ppermute | solution.py:1063
  21.2 7.0 %collective-permute-start.2 = (bf16[128,512]{1,0:T(8,128)(2,1)}, bf16[128,512]{1,0:T(8,128)(2,1)S(1)}, u32[]{:S(2)}, u32[]{:S(2)}) collective-permute-start(bf16[128,512]{1,0:T(8,128)(2,1)} %get-tuple-element.77), channel_id=1, source_target_pairs={{0,3},{1,2},{2,1},{3,0},{4,7},{5,6},{6,5},{7,4},{8,11},{9,10},{10,... | collective-permute-start | bytes 393224 | tf_op jit(solution)/shard_map/to_experts/ppermute | solution.py:1063
  28.2 15.9 %copy-start.40 = (bf16[512,8]{0,1:T(8,128)(2,1)S(1)}, bf16[512,8]{0,1:T(8,128)(2,1)}, u32[]{:S(2)}) copy-start(bf16[512,8]{0,1:T(8,128)(2,1)} %param.22) | copy-start | bytes 24580
  28.2 15.9 %copy-start.41 = (f32[512]{0:T(512)S(1)}, f32[512]{0:T(512)}, u32[]{:S(2)}) copy-start(f32[512]{0:T(512)} %param.21) | copy-start | bytes 6148
  28.2 6.9 %copy-start.13 = (bf16[512,512]{1,0:T(8,128)(2,1)}, bf16[512,512]{1,0:T(8,128)(2,1)S(1)}, u32[]{:S(2)}) copy-start(bf16[512,512]{1,0:T(8,128)(2,1)S(1)} %constant_dynamic-update-slice_fusion.refs_0_) | copy-start | bytes 1572868
  28.3 13.3 %collective-permute-start.6 = (bf16[512,512]{1,0:T(8,128)(2,1)S(1)}, bf16[512,512]{1,0:T(8,128)(2,1)S(1)}, u32[]{:S(2)}, u32[]{:S(2)}) collective-permute-start(bf16[512,512]{1,0:T(8,128)(2,1)S(1)} %constant_dynamic-update-slice_fusion.refs_0_), channel_id=1, source_target_pairs={{0,8},{8,16},{16,24},{24,28},{28,20},{20,12},{12,4},{4,0},{1,9},{9... | collective-permute-start | bytes 1572872 | tf_op jit(solution)/shard_map/gather_for_weights/ppermute | solution.py:1068
  28.5 13.3 %collective-permute-start.8 = (bf16[512,512]{1,0:T(8,128)(2,1)S(1)}, bf16[512,512]{1,0:T(8,128)(2,1)S(1)}, u32[]{:S(2)}, u32[]{:S(2)}) collective-permute-start(bf16[512,512]{1,0:T(8,128)(2,1)S(1)} %constant_dynamic-update-slice_fusion.refs_0_), channel_id=1, source_target_pairs={{8,0},{16,8},{24,16},{28,24},{20,28},{12,20},{4,12},{0,4},{9,1},{1... | collective-permute-start | bytes 1572872 | tf_op jit(solution)/shard_map/gather_for_weights/ppermute | solution.py:1068
  30.7 13.4 %copy-start.23 = (bf16[1024,512]{1,0:T(8,128)(2,1)S(1)}, bf16[1024,512]{1,0:T(8,128)(2,1)}, u32[]{:S(2)}) copy-start(bf16[1024,512]{1,0:T(8,128)(2,1)} %cot_far.3) | copy-start | bytes 3145732
  30.7 13.4 %copy-start.24 = (bf16[512,512]{1,0:T(8,128)(2,1)S(1)}, bf16[512,512]{1,0:T(8,128)(2,1)}, u32[]{:S(2)}) copy-start(bf16[512,512]{1,0:T(8,128)(2,1)} %w_out_far.3) | copy-start | bytes 1572868
  30.7 13.4 %copy-start.42 = (f32[1024,512]{1,0:T(8,128)S(1)}, f32[1024,512]{1,0:T(8,128)}, u32[]{:S(2)}) copy-start(f32[1024,512]{1,0:T(8,128)} %get-tuple-element.82.hidden_far) | copy-start | bytes 6291460
  30.7 13.4 %copy-start.43 = (f32[1024,256]{1,0:T(8,128)S(1)}, f32[1024,256]{1,0:T(8,128)}, u32[]{:S(2)}) copy-start(f32[1024,256]{1,0:T(8,128)} %get-tuple-element.83.mix_far) | copy-start | bytes 3145732
  30.7 13.4 %copy-start.44 = (bf16[1024,512]{1,0:T(8,128)(2,1)S(1)}, bf16[1024,512]{1,0:T(8,128)(2,1)}, u32[]{:S(2)}) copy-start(bf16[1024,512]{1,0:T(8,128)(2,1)} %get-tuple-element.84.attended_far) | copy-start | bytes 3145732
  35.2 7.9 %collective-permute-start.3 = (bf16[128,512]{1,0:T(8,128)(2,1)S(1)}, bf16[128,512]{1,0:T(8,128)(2,1)S(1)}, u32[]{:S(2)}, u32[]{:S(2)}) collective-permute-start(bf16[128,512]{1,0:T(8,128)(2,1)S(1)} %get-tuple-element.79), channel_id=1, source_target_pairs={{0,1},{1,0},{2,3},{3,2},{4,5},{5,4},{6,7},{7,6},{8,9},{9,8},{10,11... | collective-permute-start | bytes 393224 | tf_op jit(solution)/shard_map/from_experts/ppermute | solution.py:1063
  36.0 7.1 %collective-permute-start.4 = (bf16[128,512]{1,0:T(8,128)(2,1)S(1)}, bf16[128,512]{1,0:T(8,128)(2,1)S(1)}, u32[]{:S(2)}, u32[]{:S(2)}) collective-permute-start(bf16[128,512]{1,0:T(8,128)(2,1)S(1)} %get-tuple-element.80), channel_id=1, source_target_pairs={{0,2},{1,3},{2,0},{3,1},{4,6},{5,7},{6,4},{7,5},{8,10},{9,11},{10,... | collective-permute-start | bytes 393224 | tf_op jit(solution)/shard_map/from_experts/ppermute | solution.py:1063
  37.3 6.8 %collective-permute-start.5 = (bf16[128,512]{1,0:T(8,128)(2,1)S(1)}, bf16[128,512]{1,0:T(8,128)(2,1)S(1)}, u32[]{:S(2)}, u32[]{:S(2)}) collective-permute-start(bf16[128,512]{1,0:T(8,128)(2,1)S(1)} %get-tuple-element.81), channel_id=1, source_target_pairs={{0,3},{1,2},{2,1},{3,0},{4,7},{5,6},{6,5},{7,4},{8,11},{9,10},{10,... | collective-permute-start | bytes 393224 | tf_op jit(solution)/shard_map/from_experts/ppermute | solution.py:1063
  41.6 10.5 %copy-start.25 = (bf16[512,512]{1,0:T(8,128)(2,1)}, bf16[512,512]{1,0:T(8,128)(2,1)S(1)}, u32[]{:S(2)}) copy-start(bf16[512,512]{1,0:T(8,128)(2,1)S(1)} %collective-permute-done.6.refs_1_) | copy-start | bytes 1572868
  41.6 12.4 %collective-permute-start.7 = (bf16[512,512]{1,0:T(8,128)(2,1)S(1)}, bf16[512,512]{1,0:T(8,128)(2,1)S(1)}, u32[]{:S(2)}, u32[]{:S(2)}) collective-permute-start(bf16[512,512]{1,0:T(8,128)(2,1)S(1)} %collective-permute-done.6.refs_1_), channel_id=1, source_target_pairs={{0,8},{8,16},{16,24},{24,28},{28,20},{20,12},{12,4},{4,0},{1,9},{9... | collective-permute-start | bytes 1572872 | tf_op jit(solution)/shard_map/gather_for_weights/ppermute | solution.py:1068
  41.8 10.4 %copy-start.28 = (bf16[512,512]{1,0:T(8,128)(2,1)}, bf16[512,512]{1,0:T(8,128)(2,1)S(1)}, u32[]{:S(2)}) copy-start(bf16[512,512]{1,0:T(8,128)(2,1)S(1)} %collective-permute-done.8.refs_2_) | copy-start | bytes 1572868
  41.8 12.2 %collective-permute-start.9 = (bf16[512,512]{1,0:T(8,128)(2,1)S(1)}, bf16[512,512]{1,0:T(8,128)(2,1)S(1)}, u32[]{:S(2)}, u32[]{:S(2)}) collective-permute-start(bf16[512,512]{1,0:T(8,128)(2,1)S(1)} %collective-permute-done.8.refs_2_), channel_id=1, source_target_pairs={{8,0},{16,8},{24,16},{28,24},{20,28},{12,20},{4,12},{0,4},{9,1},{1... | collective-permute-start | bytes 1572872 | tf_op jit(solution)/shard_map/gather_for_weights/ppermute | solution.py:1068
  44.1 14.0 %copy-start.45 = (bf16[8,1024,128]{2,1,0:T(8,128)(2,1)S(1)}, bf16[8,1024,128]{2,1,0:T(8,128)(2,1)}, u32[]{:S(2)}) copy-start(bf16[8,1024,128]{2,1,0:T(8,128)(2,1)} %get-tuple-element.87.queries_far) | copy-start | bytes 6291460
  44.1 14.0 %copy-start.46 = (bf16[8,1024,128]{2,1,0:T(8,128)(2,1)S(1)}, bf16[8,1024,128]{2,1,0:T(8,128)(2,1)}, u32[]{:S(2)}) copy-start(bf16[8,1024,128]{2,1,0:T(8,128)(2,1)} %get-tuple-element.88.keys_far) | copy-start | bytes 6291460
  44.1 14.0 %copy-start.47 = (bf16[8,1024,128]{2,1,0:T(8,128)(2,1)S(1)}, bf16[8,1024,128]{2,1,0:T(8,128)(2,1)}, u32[]{:S(2)}) copy-start(bf16[8,1024,128]{2,1,0:T(8,128)(2,1)} %get-tuple-element.89.values_far) | copy-start | bytes 6291460
  44.2 14.0 %copy-start.48 = (bf16[1024,512]{1,0:T(8,128)(2,1)S(1)}, bf16[1024,512]{1,0:T(8,128)(2,1)}, u32[]{:S(2)}) copy-start(bf16[1024,512]{1,0:T(8,128)(2,1)} %get-tuple-element.93.normed_far) | copy-start | bytes 3145732
  52.2 1.3 copy-start.6
  54.0 21.4 %copy-start.31 = (bf16[512,512]{1,0:T(8,128)(2,1)}, bf16[512,512]{1,0:T(8,128)(2,1)S(1)}, u32[]{:S(2)}) copy-start(bf16[512,512]{1,0:T(8,128)(2,1)S(1)} %collective-permute-done.7.refs_3_) | copy-start | bytes 1572868
  54.0 21.4 %copy-start.34 = (bf16[512,512]{1,0:T(8,128)(2,1)}, bf16[512,512]{1,0:T(8,128)(2,1)S(1)}, u32[]{:S(2)}) copy-start(bf16[512,512]{1,0:T(8,128)(2,1)S(1)} %collective-permute-done.9.refs_4_) | copy-start | bytes 1572868
  54.0 21.4 %collective-permute-start.10 = (bf16[512,512]{1,0:T(8,128)(2,1)S(1)}, bf16[512,512]{1,0:T(8,128)(2,1)S(1)}, u32[]{:S(2)}, u32[]{:S(2)}) collective-permute-start(bf16[512,512]{1,0:T(8,128)(2,1)S(1)} %collective-permute-done.7.refs_3_), channel_id=1, source_target_pairs={{0,8},{8,16},{16,24},{24,28},{28,20},{20,12},{12,4},{4,0},{1,9},{9... | collective-permute-start | bytes 1572872 | tf_op jit(solution)/shard_map/gather_for_weights/ppermute | solution.py:1068
  54.2 21.2 %collective-permute-start.11 = (bf16[512,512]{1,0:T(8,128)(2,1)S(1)}, bf16[512,512]{1,0:T(8,128)(2,1)S(1)}, u32[]{:S(2)}, u32[]{:S(2)}) collective-permute-start(bf16[512,512]{1,0:T(8,128)(2,1)S(1)} %collective-permute-done.9.refs_4_), channel_id=1, source_target_pairs={{8,0},{16,8},{24,16},{28,24},{20,28},{12,20},{4,12},{0,4},{9,1},{1... | collective-permute-start | bytes 1572872 | tf_op jit(solution)/shard_map/gather_for_weights/ppermute | solution.py:1068
  55.5 19.9 %collective-permute-start.12 = (bf16[256,640]{1,0:T(8,128)(2,1)S(1)}, bf16[256,640]{1,0:T(8,128)(2,1)S(1)}, u32[]{:S(2)}, u32[]{:S(2)}) collective-permute-start(bf16[256,640]{1,0:T(8,128)(2,1)S(1)} %get-tuple-element.98), channel_id=1, source_target_pairs={{0,1},{1,0},{2,3},{3,2},{4,5},{5,4},{6,7},{7,6},{8,9},{9,8},{10,11... | collective-permute-start | bytes 983048 | tf_op jit(solution)/shard_map/reduce/ppermute | solution.py:1080
  75.4 3.8 %copy-start.4 = (bf16[4,1024,384]{2,1,0:T(8,128)(2,1)}, bf16[4,1024,384]{2,1,0:T(8,128)(2,1)S(1)}, u32[]{:S(2)}) copy-start(bf16[4,1024,384]{2,1,0:T(8,128)(2,1)S(1)} %get-tuple-element.110.grads) | copy-start | bytes 9437188
  75.4 3.7 %copy-start.9 = (bf16[512,512]{1,0:T(8,128)(2,1)}, bf16[512,512]{1,0:T(8,128)(2,1)S(1)}, u32[]{:S(2)}) copy-start(bf16[512,512]{1,0:T(8,128)(2,1)S(1)} %collective-permute-done.11.refs_6_) | copy-start | bytes 1572868
  75.4 2.4 %collective-permute-start.13 = (bf16[256,1536]{1,0:T(8,128)(2,1)S(1)}, bf16[256,1536]{1,0:T(8,128)(2,1)S(1)}, u32[]{:S(2)}, u32[]{:S(2)}) collective-permute-start(bf16[256,1536]{1,0:T(8,128)(2,1)S(1)} %get-tuple-element.101), channel_id=1, source_target_pairs={{0,1},{1,0},{2,3},{3,2},{4,5},{5,4},{6,7},{7,6},{8,9},{9,8},{10,11... | collective-permute-start | bytes 2359304 | tf_op jit(solution)/shard_map/reduce/ppermute | solution.py:1080
  75.5 7.4 %collective-permute-start.14 = (bf16[256,512]{1,0:T(8,128)(2,1)S(1)}, bf16[256,512]{1,0:T(8,128)(2,1)S(1)}, u32[]{:S(2)}, u32[]{:S(2)}) collective-permute-start(bf16[256,512]{1,0:T(8,128)(2,1)S(1)} %slice.6), channel_id=1, source_target_pairs={{0,8},{8,16},{16,24},{24,28},{28,20},{20,12},{12,4},{4,0},{1,9},{9... | collective-permute-start | bytes 786440 | tf_op jit(solution)/shard_map/gather_for_weights/ppermute | solution.py:1068
  75.7 7.3 %collective-permute-start.15 = (bf16[256,512]{1,0:T(8,128)(2,1)S(1)}, bf16[256,512]{1,0:T(8,128)(2,1)S(1)}, u32[]{:S(2)}, u32[]{:S(2)}) collective-permute-start(bf16[256,512]{1,0:T(8,128)(2,1)S(1)} %slice.7), channel_id=1, source_target_pairs={{8,0},{16,8},{24,16},{28,24},{20,28},{12,20},{4,12},{0,4},{9,1},{1... | collective-permute-start | bytes 786440 | tf_op jit(solution)/shard_map/gather_for_weights/ppermute | solution.py:1068
  77.8 12.7 %copy-start = (bf16[512,512]{1,0:T(8,128)(2,1)S(1)}, bf16[512,512]{1,0:T(8,128)(2,1)}, u32[]{:S(2)}) copy-start(bf16[512,512]{1,0:T(8,128)(2,1)} %w_query_far.5) | copy-start | bytes 1572868
  77.8 12.7 %copy-start.1 = (bf16[512,512]{1,0:T(8,128)(2,1)S(1)}, bf16[512,512]{1,0:T(8,128)(2,1)}, u32[]{:S(2)}) copy-start(bf16[512,512]{1,0:T(8,128)(2,1)} %w_key_far.5) | copy-start | bytes 1572868
  77.8 12.7 %copy-start.2 = (bf16[512,512]{1,0:T(8,128)(2,1)S(1)}, bf16[512,512]{1,0:T(8,128)(2,1)}, u32[]{:S(2)}) copy-start(bf16[512,512]{1,0:T(8,128)(2,1)} %w_value_far.5) | copy-start | bytes 1572868
  77.8 12.7 %copy-start.16 = (f32[512]{0:T(512)S(1)}, f32[512]{0:T(512)}, u32[]{:S(2)}) copy-start(f32[512]{0:T(512)} %param.16) | copy-start | bytes 6148
  83.7 32.9 %all-to-all-start = ((bf16[16,16,2176]{2,1,0:T(8,128)(2,1)}), bf16[16,16,2176]{2,1,0:T(8,128)(2,1)S(1)}, u32[]{:S(2)}, u32[]{:S(2)}) async-start(bf16[16,16,2176]{2,1,0:T(8,128)(2,1)} %bitcast.5), calls=%async_computation | async-start | bytes 2228224 | tf_op jit(solution)/shard_map/reduce/all_to_all | solution.py:1084
  90.5 1.9 %copy-start.5 = (bf16[4,1024,384]{2,1,0:T(8,128)(2,1)S(1)}, bf16[4,1024,384]{2,1,0:T(8,128)(2,1)}, u32[]{:S(2)}) copy-start(bf16[4,1024,384]{2,1,0:T(8,128)(2,1)} %copy-done.4) | copy-start | bytes 9437188
  92.4 1.6 %copy-start.7 = (f32[1024,512]{1,0:T(8,128)S(1)}, f32[1024,512]{1,0:T(8,128)}, u32[]{:S(2)}) copy-start(f32[1024,512]{1,0:T(8,128)} %copy-done.6) | copy-start | bytes 6291460
  94.0 1.2 copy-start.8
  95.2 4.1 %copy-start.10 = (bf16[512,512]{1,0:T(8,128)(2,1)S(1)}, bf16[512,512]{1,0:T(8,128)(2,1)}, u32[]{:S(2)}) copy-start(bf16[512,512]{1,0:T(8,128)(2,1)} %copy-done.9) | copy-start | bytes 1572868
  95.2 4.1 %copy-start.14 = (bf16[512,512]{1,0:T(8,128)(2,1)S(1)}, bf16[512,512]{1,0:T(8,128)(2,1)}, u32[]{:S(2)}) copy-start(bf16[512,512]{1,0:T(8,128)(2,1)} %copy-done.13) | copy-start | bytes 1572868
  95.2 4.1 %copy-start.18 = (bf16[2,512,2048]{2,1,0:T(8,128)(2,1)S(1)}, bf16[2,512,2048]{2,1,0:T(8,128)(2,1)}, u32[]{:S(2)}) copy-start(bf16[2,512,2048]{2,1,0:T(8,128)(2,1)} %refs_9_.3) | copy-start | bytes 12582916
  95.2 4.1 %copy-start.26 = (bf16[512,512]{1,0:T(8,128)(2,1)S(1)}, bf16[512,512]{1,0:T(8,128)(2,1)}, u32[]{:S(2)}) copy-start(bf16[512,512]{1,0:T(8,128)(2,1)} %copy-done.25) | copy-start | bytes 1572868
  95.2 4.1 %copy-start.29 = (bf16[512,512]{1,0:T(8,128)(2,1)S(1)}, bf16[512,512]{1,0:T(8,128)(2,1)}, u32[]{:S(2)}) copy-start(bf16[512,512]{1,0:T(8,128)(2,1)} %copy-done.28) | copy-start | bytes 1572868
  95.2 4.1 %copy-start.32 = (bf16[512,512]{1,0:T(8,128)(2,1)S(1)}, bf16[512,512]{1,0:T(8,128)(2,1)}, u32[]{:S(2)}) copy-start(bf16[512,512]{1,0:T(8,128)(2,1)} %copy-done.31) | copy-start | bytes 1572868
  95.3 4.1 %copy-start.35 = (bf16[512,512]{1,0:T(8,128)(2,1)S(1)}, bf16[512,512]{1,0:T(8,128)(2,1)}, u32[]{:S(2)}) copy-start(bf16[512,512]{1,0:T(8,128)(2,1)} %copy-done.34) | copy-start | bytes 1572868
  95.3 4.1 %copy-start.38 = (bf16[256,512]{1,0:T(8,128)(2,1)S(1)}, bf16[256,512]{1,0:T(8,128)(2,1)}, u32[]{:S(2)}) copy-start(bf16[256,512]{1,0:T(8,128)(2,1)} %copy-done.37) | copy-start | bytes 786436
  99.4 2.2 %copy-start.21 = (bf16[2,2048,512]{2,1,0:T(8,128)(2,1)S(1)}, bf16[2,2048,512]{2,1,0:T(8,128)(2,1)}, u32[]{:S(2)}) copy-start(bf16[2,2048,512]{2,1,0:T(8,128)(2,1)} %refs_10_.3) | copy-start | bytes 12582916
  117.8 30.1 %all-to-all-start.1 = ((bf16[16,16,2176]{2,1,0:T(8,128)(2,1)}), bf16[16,16,2176]{2,1,0:T(8,128)(2,1)S(1)}, u32[]{:S(2)}, u32[]{:S(2)}) async-start(bf16[16,16,2176]{2,1,0:T(8,128)(2,1)} %copy-done.3), calls=%async_computation.1 | async-start | bytes 2228224 | tf_op jit(solution)/shard_map/reduce/all_to_all | solution.py:1087
  121.8 1.0 copy-start.11
  122.8 1.0 copy-start.15
  123.9 2.2 %copy-start.19 = (bf16[2,512,2048]{2,1,0:T(8,128)(2,1)S(1)}, bf16[2,512,2048]{2,1,0:T(8,128)(2,1)}, u32[]{:S(2)}) copy-start(bf16[2,512,2048]{2,1,0:T(8,128)(2,1)} %refs_9_.3) | copy-start | bytes 12582916
  126.1 2.2 %copy-start.22 = (bf16[2,2048,512]{2,1,0:T(8,128)(2,1)S(1)}, bf16[2,2048,512]{2,1,0:T(8,128)(2,1)}, u32[]{:S(2)}) copy-start(bf16[2,2048,512]{2,1,0:T(8,128)(2,1)} %refs_10_.3) | copy-start | bytes 12582916
  128.2 1.0 copy-start.27
  129.3 1.0 copy-start.30
  130.3 1.0 copy-start.33
  131.4 1.0 copy-start.36
  147.9 4.9 %collective-permute-start.16 = (bf16[256,2176]{1,0:T(8,128)(2,1)S(1)}, bf16[256,2176]{1,0:T(8,128)(2,1)S(1)}, u32[]{:S(2)}, u32[]{:S(2)}) collective-permute-start(bf16[256,2176]{1,0:T(8,128)(2,1)S(1)} %bitcast.11), channel_id=1, source_target_pairs={{0,1},{1,0},{2,3},{3,2},{4,5},{5,4},{6,7},{7,6},{8,9},{9,8},{10,11... | collective-permute-start | bytes 3342344 | tf_op jit(solution)/shard_map/reduce/ppermute | solution.py:1080
  (4 other events, 3.6 us)

commit v4 on v3

--- a/solution.py
+++ b/solution.py
@@ -311,12 +311,12 @@
     mixed_sum = 0.0
     pulled_sum = 0.0
     for rows in blocks:
-        full = spread[rows, :] * scale
-        mix[rows, :] = full
-        low = full.astype(LOW)
+        mix[rows, :] = spread[rows, :] * scale
+    begin(outs[3:])
+    for rows in blocks:
+        low = mix[rows, :].astype(LOW)
         mixed_sum = mixed_sum + product_tn(low, second[rows, :])
         pulled_sum = pulled_sum + product_tn(low, cot[rows, :])
-    begin(outs[3:])
     mixed[...] = mixed_sum.astype(LOW)
     pulled[...] = pulled_sum.astype(LOW)
     share = EXP_DEV * groups

time: 156 us -> 156 us (level)
  no operation moved by 1% of the time
where the time goes in v4:
time: 156 us; the launch traced here: 155 us
  Pallas kernels  77.5 us (50%)
  starting transfers between devices  27.1 us (17%)
  waiting for transfers between devices  25.9 us (17%)
  local copies, waits for them, and re-layouts  23.5 us (15%)
    unnamed x101, local copies, waits for them, and re-layouts  23.4 us
    pallas_call x2, Pallas kernels, weight_call(): pl.pallas_call(functools.partial(weight_kernel, expert, len(pieces)), gri...  20 us
    pallas_call x1, Pallas kernels, forward_call(): pl.pallas_call(forward_kernel, in_specs=[smem()] + [far()] * 11, out_spec...  18.6 us
    pallas_call x1, Pallas kernels, pair_call(): pl.pallas_call(pair_kernel, in_specs=[smem()] + [far()] * 5, out_specs=[f...  17.2 us
    ppermute x4, waiting for transfers between devices, pass_on(): lax.ppermute(ahead_part, 'dp', ahead)  8.17 us
    pallas_call x1, Pallas kernels, middle_call(): pl.pallas_call(middle_kernel, in_specs=[smem()] * 2 + [vmem()] * 4 + [far...  7.96 us
    all_to_all x1, starting transfers between devices, scatter(): lax.all_to_all(half.reshape(count, rows // count, cols), axes, 0, 0, tile...  6.8 us
    ppermute x6, waiting for transfers between devices, exchange(): lax.ppermute(parts[step], hosts_axes, [(i, i ^ step) for i in range(hosts)])  6.59 us
  transfers between devices with their start and end apart: 19, of which 10 were waited for; matrix products, arithmetic and copies ran while one was open for 1% of the time, Pallas kernels for 36%

profile of v4, /device:TPU:11, one launch (start us, length us, event | category | flops | bytes accessed | tf_op | source)
XLA Modules:
  0.0 155.1 jit_solution(677235389813109178)
XLA Ops:
  0.7 0.0 copy-start.17
  0.7 0.0 copy-start.20
  0.7 18.6 %attention_and_mixing.1 = (bf16[128,512]{1,0:T(8,128)(2,1)}, bf16[128,512]{1,0:T(8,128)(2,1)}, bf16[128,512]{1,0:T(8,128)(2,1)}, bf16[128,512]{1,0:T(8,128)(2,1)...) custom-call(s32[1]{0:T(128)} %bitcast.place, ...), custom_call_target="tpu_custom_call" | custom-call | flops 20000000000 | bytes 20000000 | tf_op jit(solution)/shard_map/attention_and_mixing/pallas_call | solution.py:819
  19.3 0.7 collective-permute-start
  20.0 1.3 collective-permute-start.1
  21.2 0.5 collective-permute-start.2
  21.7 0.9 constant_dynamic-update-slice_fusion.3
  22.7 2.6 %collective-permute-done.1.in2 = bf16[128,512]{1,0:T(8,128)(2,1)S(1)} collective-permute-done((bf16[128,512]{1,0:T(8,128)(2,1)}, bf16[128,512]{1,0:T(8,128)(2,1)S(1)}, u32[]{:S(2)}, u32[]{:S(2)}) %collective-permute-start.1) | collective-permute-done | bytes 131104 | tf_op jit(solution)/shard_map/to_experts/ppermute | solution.py:1063
  25.3 3.0 %collective-permute-done.2.in3 = bf16[128,512]{1,0:T(8,128)(2,1)S(1)} collective-permute-done((bf16[128,512]{1,0:T(8,128)(2,1)}, bf16[128,512]{1,0:T(8,128)(2,1)S(1)}, u32[]{:S(2)}, u32[]{:S(2)}) %collective-permute-start.2) | collective-permute-done | bytes 131104 | tf_op jit(solution)/shard_map/to_experts/ppermute | solution.py:1063
  28.3 0.0 copy-start.13
  28.3 0.2 collective-permute-start.6
  28.5 1.3 collective-permute-start.8
  29.8 0.9 copy-done.12
  30.7 0.0 copy-start.44
  30.7 4.4 %experts.1 = (bf16[128,512]{1,0:T(8,128)(2,1)S(1)}, bf16[128,512]{1,0:T(8,128)(2,1)S(1)}, bf16[128,512]{1,0:T(8,128)(2,1)S(1)}, bf16[128,512]{1,0:T(8,128)(2,1)S(1)}) custom-call(bf16[128,512]{1,0:T(8,128)(2,1)S(1)} %copy-done.12, bf16[128,512]{1,0:T(8,128)(2,1)S(1)} %collective-permute-done.in1, bf16[128,512]{1,0:T(8,128)(2,1)S(1)} %collective-permute-done.1.in2, ...), custom_call_target="tpu_custom_call" | custom-call | flops 5000000000 | bytes 10000000 | tf_op jit(solution)/shard_map/experts/pallas_call | solution.py:852
  35.2 0.9 collective-permute-start.3
  36.1 1.3 collective-permute-start.4
  37.3 0.5 collective-permute-start.5
  37.8 3.9 %collective-permute-done.6.refs_1_ = bf16[512,512]{1,0:T(8,128)(2,1)S(1)} collective-permute-done((bf16[512,512]{1,0:T(8,128)(2,1)S(1)}, bf16[512,512]{1,0:T(8,128)(2,1)S(1)}, u32[]{:S(2)}, u32[]{:S(2)}) %collective-permute-start.6) | collective-permute-done | bytes 524320 | tf_op jit(solution)/shard_map/gather_for_weights/ppermute | solution.py:1068
  41.6 0.2 collective-permute-start.7
  41.8 1.3 collective-permute-start.9
  43.1 1.0 collective-permute-done.5.ret3
  44.2 0.0 copy-start.48
  44.2 8.0 %mixing_backward.1 = (bf16[1024,512]{1,0:T(8,128)(2,1)}, f32[1024,512]{1,0:T(8,128)S(1)}, bf16[8,1024,128]{2,1,0:T(8,128)(2,1)S(1)}, bf16[256,640]{1,0:T(8,128)(2,1)S(1)}, bf16[256,640]{1,0:T(8,128)(2,1)S(1)}) custom-call(s32[1]{0:T(128)} %bitcast.place, s32[1]{0:T(128)} %bitcast.1.near, bf16[128,512]{1,0:T(8,128)(2,1)S(1)} %get-tuple-element.78.ret0, ...), custom_call_target="tpu_custom_call" | custom-call | flops 8000000000 | bytes 15000000 | tf_op jit(solution)/shard_map/mixing_backward/pallas_call | solution.py:874
  52.2 1.3 copy-done.6
  53.5 0.5 collective-permute-done.7.refs_3_
  54.0 0.2 collective-permute-start.10
  54.2 1.3 collective-permute-start.11
  55.5 2.7 %collective-permute-start.12 = (bf16[256,640]{1,0:T(8,128)(2,1)S(1)}, bf16[256,640]{1,0:T(8,128)(2,1)S(1)}, u32[]{:S(2)}, u32[]{:S(2)}) collective-permute-start(bf16[256,640]{1,0:T(8,128)(2,1)S(1)} %get-tuple-element.98), channel_id=1, source_target_pairs={{0,1},{1,0},{2,3},{3,2},{4,5},{5,4},{6,7},{7,6},{8,9},{9,8},{10,11... | collective-permute-start | bytes 983048 | tf_op jit(solution)/shard_map/reduce/ppermute | solution.py:1080
  58.2 17.2 %attention_backward.1 = (bf16[4,1024,384]{2,1,0:T(8,128)(2,1)S(1)}, bf16[256,1536]{1,0:T(8,128)(2,1)S(1)}, bf16[256,1536]{1,0:T(8,128)(2,1)S(1)}) custom-call(s32[1]{0:T(128)} %bitcast.1.near, bf16[8,1024,128]{2,1,0:T(8,128)(2,1)S(1)} %copy-done.45, bf16[8,1024,128]{2,1,0:T(8,128)(2,1)S(1)} %copy-done.46, bf16[8,1024,128]{2,1,0:T(8,128)(2,1)S(1)} %copy-done.47, ...), custom_call_target="tpu_custom_call" | custom-call | flops 20000000000 | bytes 12000000 | tf_op jit(solution)/shard_map/attention_backward/pallas_call | solution.py:899
  75.5 0.1 collective-permute-start.13
  75.6 0.1 collective-permute-start.14
  75.7 1.4 collective-permute-start.15
  77.2 0.7 collective-permute-done.13.swapped
  77.8 1.3 reduce.2
  79.2 3.8 %collective-permute-done.14.refs_7_ = bf16[256,512]{1,0:T(8,128)(2,1)S(1)} collective-permute-done((bf16[256,512]{1,0:T(8,128)(2,1)S(1)}, bf16[256,512]{1,0:T(8,128)(2,1)S(1)}, u32[]{:S(2)}, u32[]{:S(2)}) %collective-permute-start.14) | collective-permute-done | bytes 262176 | tf_op jit(solution)/shard_map/gather_for_weights/ppermute | solution.py:1068
  83.0 0.7 copy-done.37
  83.7 6.8 %all-to-all-start = ((bf16[16,16,2176]{2,1,0:T(8,128)(2,1)}), bf16[16,16,2176]{2,1,0:T(8,128)(2,1)S(1)}, u32[]{:S(2)}, u32[]{:S(2)}) async-start(bf16[16,16,2176]{2,1,0:T(8,128)(2,1)} %bitcast.5), calls=%async_computation | async-start | bytes 2228224 | tf_op jit(solution)/shard_map/reduce/all_to_all | solution.py:1084
  90.6 1.9 %copy-done.5 = bf16[4,1024,384]{2,1,0:T(8,128)(2,1)S(1)} copy-done((bf16[4,1024,384]{2,1,0:T(8,128)(2,1)S(1)}, bf16[4,1024,384]{2,1,0:T(8,128)(2,1)}, u32[]{:S(2)}) %copy-start.5) | copy-done | bytes 3145752
  92.4 1.6 %copy-done.7 = f32[1024,512]{1,0:T(8,128)S(1)} copy-done((f32[1024,512]{1,0:T(8,128)S(1)}, f32[1024,512]{1,0:T(8,128)}, u32[]{:S(2)}) %copy-start.7) | copy-done | bytes 2097176
  94.0 1.2 copy-done.8
  95.3 4.0 %norm_backward.1 = bf16[1024,512]{1,0:T(8,128)(2,1)} custom-call(bf16[4,1024,384]{2,1,0:T(8,128)(2,1)S(1)} %copy-done.5, bf16[1024,512]{1,0:T(8,128)(2,1)S(1)} %copy-done.8, f32[1024,512]{1,0:T(8,128)S(1)} %copy-done.7, f32[1,512]{1,0:T(1,128)S(1)} %bitcast.14, bf16[512,512]{1,0:T(8,128)(2,1)S(1)} %copy-done, bf16[512,512]{1,0:T(8,128)(2,1)S(1)} %copy-done.1, ...), custom_call_target="tpu_custom_call" | custom-call | flops 2000000000 | bytes 8000000 | tf_op jit(solution)/shard_map/norm_backward/pallas_call | solution.py:956
  99.4 2.2 %copy-done.21 = bf16[2,2048,512]{2,1,0:T(8,128)(2,1)S(1)} copy-done((bf16[2,2048,512]{2,1,0:T(8,128)(2,1)S(1)}, bf16[2,2048,512]{2,1,0:T(8,128)(2,1)}, u32[]{:S(2)}) %copy-start.21) | copy-done | bytes 4194328
  101.6 10.0 %expert_weights.2 = (f32[2,64,2048]{2,1,0:T(8,128)}, f32[2,256,512]{2,1,0:T(8,128)}) custom-call(s32[1]{0:T(128)} %bitcast.6.place, bf16[512,512]{1,0:T(8,128)(2,1)S(1)} %copy-done.14, bf16[512,512]{1,0:T(8,128)(2,1)S(1)} %copy-done.26, bf16[512,512]{1,0:T(8,128)(2,1)S(1)} %copy-done.29, bf16[512,512]{1,0:T(8,128)(2,1)S(1)} %copy-done.32, ...), custom_call_target="tpu_custom_call" | custom-call | flops 10000000000 | bytes 8000000 | tf_op jit(solution)/shard_map/expert_weights/pallas_call | solution.py:923
  111.6 5.0 %all-to-all-done.parts = bf16[16,16,2176]{2,1,0:T(8,128)(2,1)S(1)} async-done(((bf16[16,16,2176]{2,1,0:T(8,128)(2,1)}), bf16[16,16,2176]{2,1,0:T(8,128)(2,1)S(1)}, u32[]{:S(2)}, u32[]{:S(2)}) %all-to-all-start) | async-done | bytes 1114144 | tf_op jit(solution)/shard_map/reduce/all_to_all | solution.py:1084
  116.7 0.2 reduce.3
  116.8 1.0 copy-done.3
  117.8 4.0 %all-to-all-start.1 = ((bf16[16,16,2176]{2,1,0:T(8,128)(2,1)}), bf16[16,16,2176]{2,1,0:T(8,128)(2,1)S(1)}, u32[]{:S(2)}, u32[]{:S(2)}) async-start(bf16[16,16,2176]{2,1,0:T(8,128)(2,1)} %copy-done.3), calls=%async_computation.1 | async-start | bytes 2228224 | tf_op jit(solution)/shard_map/reduce/all_to_all | solution.py:1087
  121.8 1.0 copy-done.11
  122.9 1.0 copy-done.15
  123.9 2.2 %copy-done.19 = bf16[2,512,2048]{2,1,0:T(8,128)(2,1)S(1)} copy-done((bf16[2,512,2048]{2,1,0:T(8,128)(2,1)S(1)}, bf16[2,512,2048]{2,1,0:T(8,128)(2,1)}, u32[]{:S(2)}) %copy-start.19) | copy-done | bytes 4194328
  126.1 2.2 %copy-done.22 = bf16[2,2048,512]{2,1,0:T(8,128)(2,1)S(1)} copy-done((bf16[2,2048,512]{2,1,0:T(8,128)(2,1)S(1)}, bf16[2,2048,512]{2,1,0:T(8,128)(2,1)}, u32[]{:S(2)}) %copy-start.22) | copy-done | bytes 4194328
  128.3 1.0 copy-done.27
  129.3 1.0 copy-done.30
  130.4 1.0 copy-done.33
  131.4 1.0 copy-done.36
  132.4 0.9 copy-done.39
  133.4 10.0 %expert_weights.3 = (f32[2,64,2048]{2,1,0:T(8,128)}, f32[2,256,512]{2,1,0:T(8,128)}) custom-call(s32[1]{0:T(128)} %bitcast.6.place, bf16[512,512]{1,0:T(8,128)(2,1)S(1)} %copy-done.15, bf16[512,512]{1,0:T(8,128)(2,1)S(1)} %copy-done.27, bf16[512,512]{1,0:T(8,128)(2,1)S(1)} %copy-done.30, ...), custom_call_target="tpu_custom_call", output_to_operand_aliasing={{0}: (12, {}), {1}: (13, {})} | custom-call | flops 10000000000 | bytes 8000000 | tf_op jit(solution)/shard_map/expert_weights/pallas_call | solution.py:923
  143.4 4.5 %all-to-all-done.1 = bf16[16,16,2176]{2,1,0:T(8,128)(2,1)S(1)} async-done(((bf16[16,16,2176]{2,1,0:T(8,128)(2,1)}), bf16[16,16,2176]{2,1,0:T(8,128)(2,1)S(1)}, u32[]{:S(2)}, u32[]{:S(2)}) %all-to-all-start.1) | async-done | bytes 1114144 | tf_op jit(solution)/shard_map/reduce/all_to_all | solution.py:1087
  148.0 2.5 %collective-permute-start.16 = (bf16[256,2176]{1,0:T(8,128)(2,1)S(1)}, bf16[256,2176]{1,0:T(8,128)(2,1)S(1)}, u32[]{:S(2)}, u32[]{:S(2)}) collective-permute-start(bf16[256,2176]{1,0:T(8,128)(2,1)S(1)} %bitcast.11), channel_id=1, source_target_pairs={{0,1},{1,0},{2,3},{3,2},{4,5},{5,4},{6,7},{7,6},{8,9},{9,8},{10,11... | collective-permute-start | bytes 3342344 | tf_op jit(solution)/shard_map/reduce/ppermute | solution.py:1080
  150.5 1.5 assemble.3
  151.9 0.9 collective-permute-done.16.both
  152.8 1.5 assemble.4
  154.4 0.7 assemble.5
  (90 shorter events, 0.2 us)
Async XLA Ops:
  0.7 29.2 %copy-start.17 = (bf16[2,512,2048]{2,1,0:T(8,128)(2,1)S(1)}, bf16[2,512,2048]{2,1,0:T(8,128)(2,1)}, u32[]{:S(2)}) copy-start(bf16[2,512,2048]{2,1,0:T(8,128)(2,1)} %refs_9_.3) | copy-start | bytes 12582916
  0.7 29.1 %copy-start.20 = (bf16[2,2048,512]{2,1,0:T(8,128)(2,1)S(1)}, bf16[2,2048,512]{2,1,0:T(8,128)(2,1)}, u32[]{:S(2)}) copy-start(bf16[2,2048,512]{2,1,0:T(8,128)(2,1)} %refs_10_.3) | copy-start | bytes 12582916
  19.3 3.4 %collective-permute-start = (bf16[128,512]{1,0:T(8,128)(2,1)}, bf16[128,512]{1,0:T(8,128)(2,1)S(1)}, u32[]{:S(2)}, u32[]{:S(2)}) collective-permute-start(bf16[128,512]{1,0:T(8,128)(2,1)} %get-tuple-element.75), channel_id=1, source_target_pairs={{0,1},{1,0},{2,3},{3,2},{4,5},{5,4},{6,7},{7,6},{8,9},{9,8},{10,11... | collective-permute-start | bytes 393224 | tf_op jit(solution)/shard_map/to_experts/ppermute | solution.py:1063
  20.0 5.3 %collective-permute-start.1 = (bf16[128,512]{1,0:T(8,128)(2,1)}, bf16[128,512]{1,0:T(8,128)(2,1)S(1)}, u32[]{:S(2)}, u32[]{:S(2)}) collective-permute-start(bf16[128,512]{1,0:T(8,128)(2,1)} %get-tuple-element.76), channel_id=1, source_target_pairs={{0,2},{1,3},{2,0},{3,1},{4,6},{5,7},{6,4},{7,5},{8,10},{9,11},{10,... | collective-permute-start | bytes 393224 | tf_op jit(solution)/shard_map/to_experts/ppermute | solution.py:1063
  21.2 7.0 %collective-permute-start.2 = (bf16[128,512]{1,0:T(8,128)(2,1)}, bf16[128,512]{1,0:T(8,128)(2,1)S(1)}, u32[]{:S(2)}, u32[]{:S(2)}) collective-permute-start(bf16[128,512]{1,0:T(8,128)(2,1)} %get-tuple-element.77), channel_id=1, source_target_pairs={{0,3},{1,2},{2,1},{3,0},{4,7},{5,6},{6,5},{7,4},{8,11},{9,10},{10,... | collective-permute-start | bytes 393224 | tf_op jit(solution)/shard_map/to_experts/ppermute | solution.py:1063
  28.3 15.9 %copy-start.40 = (bf16[512,8]{0,1:T(8,128)(2,1)S(1)}, bf16[512,8]{0,1:T(8,128)(2,1)}, u32[]{:S(2)}) copy-start(bf16[512,8]{0,1:T(8,128)(2,1)} %param.22) | copy-start | bytes 24580
  28.3 15.9 %copy-start.41 = (f32[512]{0:T(512)S(1)}, f32[512]{0:T(512)}, u32[]{:S(2)}) copy-start(f32[512]{0:T(512)} %param.21) | copy-start | bytes 6148
  28.3 6.9 %copy-start.13 = (bf16[512,512]{1,0:T(8,128)(2,1)}, bf16[512,512]{1,0:T(8,128)(2,1)S(1)}, u32[]{:S(2)}) copy-start(bf16[512,512]{1,0:T(8,128)(2,1)S(1)} %constant_dynamic-update-slice_fusion.refs_0_) | copy-start | bytes 1572868
  28.3 13.3 %collective-permute-start.6 = (bf16[512,512]{1,0:T(8,128)(2,1)S(1)}, bf16[512,512]{1,0:T(8,128)(2,1)S(1)}, u32[]{:S(2)}, u32[]{:S(2)}) collective-permute-start(bf16[512,512]{1,0:T(8,128)(2,1)S(1)} %constant_dynamic-update-slice_fusion.refs_0_), channel_id=1, source_target_pairs={{0,8},{8,16},{16,24},{24,28},{28,20},{20,12},{12,4},{4,0},{1,9},{9... | collective-permute-start | bytes 1572872 | tf_op jit(solution)/shard_map/gather_for_weights/ppermute | solution.py:1068
  28.5 13.3 %collective-permute-start.8 = (bf16[512,512]{1,0:T(8,128)(2,1)S(1)}, bf16[512,512]{1,0:T(8,128)(2,1)S(1)}, u32[]{:S(2)}, u32[]{:S(2)}) collective-permute-start(bf16[512,512]{1,0:T(8,128)(2,1)S(1)} %constant_dynamic-update-slice_fusion.refs_0_), channel_id=1, source_target_pairs={{8,0},{16,8},{24,16},{28,24},{20,28},{12,20},{4,12},{0,4},{9,1},{1... | collective-permute-start | bytes 1572872 | tf_op jit(solution)/shard_map/gather_for_weights/ppermute | solution.py:1068
  30.7 13.4 %copy-start.23 = (bf16[1024,512]{1,0:T(8,128)(2,1)S(1)}, bf16[1024,512]{1,0:T(8,128)(2,1)}, u32[]{:S(2)}) copy-start(bf16[1024,512]{1,0:T(8,128)(2,1)} %cot_far.3) | copy-start | bytes 3145732
  30.7 13.4 %copy-start.24 = (bf16[512,512]{1,0:T(8,128)(2,1)S(1)}, bf16[512,512]{1,0:T(8,128)(2,1)}, u32[]{:S(2)}) copy-start(bf16[512,512]{1,0:T(8,128)(2,1)} %w_out_far.3) | copy-start | bytes 1572868
  30.7 13.4 %copy-start.42 = (f32[1024,512]{1,0:T(8,128)S(1)}, f32[1024,512]{1,0:T(8,128)}, u32[]{:S(2)}) copy-start(f32[1024,512]{1,0:T(8,128)} %get-tuple-element.82.hidden_far) | copy-start | bytes 6291460
  30.7 13.4 %copy-start.43 = (f32[1024,256]{1,0:T(8,128)S(1)}, f32[1024,256]{1,0:T(8,128)}, u32[]{:S(2)}) copy-start(f32[1024,256]{1,0:T(8,128)} %get-tuple-element.83.mix_far) | copy-start | bytes 3145732
  30.7 13.4 %copy-start.44 = (bf16[1024,512]{1,0:T(8,128)(2,1)S(1)}, bf16[1024,512]{1,0:T(8,128)(2,1)}, u32[]{:S(2)}) copy-start(bf16[1024,512]{1,0:T(8,128)(2,1)} %get-tuple-element.84.attended_far) | copy-start | bytes 3145732
  35.2 7.9 %collective-permute-start.3 = (bf16[128,512]{1,0:T(8,128)(2,1)S(1)}, bf16[128,512]{1,0:T(8,128)(2,1)S(1)}, u32[]{:S(2)}, u32[]{:S(2)}) collective-permute-start(bf16[128,512]{1,0:T(8,128)(2,1)S(1)} %get-tuple-element.79), channel_id=1, source_target_pairs={{0,1},{1,0},{2,3},{3,2},{4,5},{5,4},{6,7},{7,6},{8,9},{9,8},{10,11... | collective-permute-start | bytes 393224 | tf_op jit(solution)/shard_map/from_experts/ppermute | solution.py:1063
  36.1 7.0 %collective-permute-start.4 = (bf16[128,512]{1,0:T(8,128)(2,1)S(1)}, bf16[128,512]{1,0:T(8,128)(2,1)S(1)}, u32[]{:S(2)}, u32[]{:S(2)}) collective-permute-start(bf16[128,512]{1,0:T(8,128)(2,1)S(1)} %get-tuple-element.80), channel_id=1, source_target_pairs={{0,2},{1,3},{2,0},{3,1},{4,6},{5,7},{6,4},{7,5},{8,10},{9,11},{10,... | collective-permute-start | bytes 393224 | tf_op jit(solution)/shard_map/from_experts/ppermute | solution.py:1063
  37.3 6.8 %collective-permute-start.5 = (bf16[128,512]{1,0:T(8,128)(2,1)S(1)}, bf16[128,512]{1,0:T(8,128)(2,1)S(1)}, u32[]{:S(2)}, u32[]{:S(2)}) collective-permute-start(bf16[128,512]{1,0:T(8,128)(2,1)S(1)} %get-tuple-element.81), channel_id=1, source_target_pairs={{0,3},{1,2},{2,1},{3,0},{4,7},{5,6},{6,5},{7,4},{8,11},{9,10},{10,... | collective-permute-start | bytes 393224 | tf_op jit(solution)/shard_map/from_experts/ppermute | solution.py:1063
  41.6 10.5 %copy-start.25 = (bf16[512,512]{1,0:T(8,128)(2,1)}, bf16[512,512]{1,0:T(8,128)(2,1)S(1)}, u32[]{:S(2)}) copy-start(bf16[512,512]{1,0:T(8,128)(2,1)S(1)} %collective-permute-done.6.refs_1_) | copy-start | bytes 1572868
  41.6 12.4 %collective-permute-start.7 = (bf16[512,512]{1,0:T(8,128)(2,1)S(1)}, bf16[512,512]{1,0:T(8,128)(2,1)S(1)}, u32[]{:S(2)}, u32[]{:S(2)}) collective-permute-start(bf16[512,512]{1,0:T(8,128)(2,1)S(1)} %collective-permute-done.6.refs_1_), channel_id=1, source_target_pairs={{0,8},{8,16},{16,24},{24,28},{28,20},{20,12},{12,4},{4,0},{1,9},{9... | collective-permute-start | bytes 1572872 | tf_op jit(solution)/shard_map/gather_for_weights/ppermute | solution.py:1068
  41.8 10.4 %copy-start.28 = (bf16[512,512]{1,0:T(8,128)(2,1)}, bf16[512,512]{1,0:T(8,128)(2,1)S(1)}, u32[]{:S(2)}) copy-start(bf16[512,512]{1,0:T(8,128)(2,1)S(1)} %collective-permute-done.8.refs_2_) | copy-start | bytes 1572868
  41.8 12.2 %collective-permute-start.9 = (bf16[512,512]{1,0:T(8,128)(2,1)S(1)}, bf16[512,512]{1,0:T(8,128)(2,1)S(1)}, u32[]{:S(2)}, u32[]{:S(2)}) collective-permute-start(bf16[512,512]{1,0:T(8,128)(2,1)S(1)} %collective-permute-done.8.refs_2_), channel_id=1, source_target_pairs={{8,0},{16,8},{24,16},{28,24},{20,28},{12,20},{4,12},{0,4},{9,1},{1... | collective-permute-start | bytes 1572872 | tf_op jit(solution)/shard_map/gather_for_weights/ppermute | solution.py:1068
  44.2 14.0 %copy-start.45 = (bf16[8,1024,128]{2,1,0:T(8,128)(2,1)S(1)}, bf16[8,1024,128]{2,1,0:T(8,128)(2,1)}, u32[]{:S(2)}) copy-start(bf16[8,1024,128]{2,1,0:T(8,128)(2,1)} %get-tuple-element.87.queries_far) | copy-start | bytes 6291460
  44.2 14.0 %copy-start.46 = (bf16[8,1024,128]{2,1,0:T(8,128)(2,1)S(1)}, bf16[8,1024,128]{2,1,0:T(8,128)(2,1)}, u32[]{:S(2)}) copy-start(bf16[8,1024,128]{2,1,0:T(8,128)(2,1)} %get-tuple-element.88.keys_far) | copy-start | bytes 6291460
  44.2 14.0 %copy-start.47 = (bf16[8,1024,128]{2,1,0:T(8,128)(2,1)S(1)}, bf16[8,1024,128]{2,1,0:T(8,128)(2,1)}, u32[]{:S(2)}) copy-start(bf16[8,1024,128]{2,1,0:T(8,128)(2,1)} %get-tuple-element.89.values_far) | copy-start | bytes 6291460
  44.2 14.0 %copy-start.48 = (bf16[1024,512]{1,0:T(8,128)(2,1)S(1)}, bf16[1024,512]{1,0:T(8,128)(2,1)}, u32[]{:S(2)}) copy-start(bf16[1024,512]{1,0:T(8,128)(2,1)} %get-tuple-element.93.normed_far) | copy-start | bytes 3145732
  52.2 1.3 copy-start.6
  54.0 21.4 %copy-start.31 = (bf16[512,512]{1,0:T(8,128)(2,1)}, bf16[512,512]{1,0:T(8,128)(2,1)S(1)}, u32[]{:S(2)}) copy-start(bf16[512,512]{1,0:T(8,128)(2,1)S(1)} %collective-permute-done.7.refs_3_) | copy-start | bytes 1572868
  54.0 21.4 %copy-start.34 = (bf16[512,512]{1,0:T(8,128)(2,1)}, bf16[512,512]{1,0:T(8,128)(2,1)S(1)}, u32[]{:S(2)}) copy-start(bf16[512,512]{1,0:T(8,128)(2,1)S(1)} %collective-permute-done.9.refs_4_) | copy-start | bytes 1572868
  54.0 21.4 %collective-permute-start.10 = (bf16[512,512]{1,0:T(8,128)(2,1)S(1)}, bf16[512,512]{1,0:T(8,128)(2,1)S(1)}, u32[]{:S(2)}, u32[]{:S(2)}) collective-permute-start(bf16[512,512]{1,0:T(8,128)(2,1)S(1)} %collective-permute-done.7.refs_3_), channel_id=1, source_target_pairs={{0,8},{8,16},{16,24},{24,28},{28,20},{20,12},{12,4},{4,0},{1,9},{9... | collective-permute-start | bytes 1572872 | tf_op jit(solution)/shard_map/gather_for_weights/ppermute | solution.py:1068
  54.2 21.2 %collective-permute-start.11 = (bf16[512,512]{1,0:T(8,128)(2,1)S(1)}, bf16[512,512]{1,0:T(8,128)(2,1)S(1)}, u32[]{:S(2)}, u32[]{:S(2)}) collective-permute-start(bf16[512,512]{1,0:T(8,128)(2,1)S(1)} %collective-permute-done.9.refs_4_), channel_id=1, source_target_pairs={{8,0},{16,8},{24,16},{28,24},{20,28},{12,20},{4,12},{0,4},{9,1},{1... | collective-permute-start | bytes 1572872 | tf_op jit(solution)/shard_map/gather_for_weights/ppermute | solution.py:1068
  55.5 19.9 %collective-permute-start.12 = (bf16[256,640]{1,0:T(8,128)(2,1)S(1)}, bf16[256,640]{1,0:T(8,128)(2,1)S(1)}, u32[]{:S(2)}, u32[]{:S(2)}) collective-permute-start(bf16[256,640]{1,0:T(8,128)(2,1)S(1)} %get-tuple-element.98), channel_id=1, source_target_pairs={{0,1},{1,0},{2,3},{3,2},{4,5},{5,4},{6,7},{7,6},{8,9},{9,8},{10,11... | collective-permute-start | bytes 983048 | tf_op jit(solution)/shard_map/reduce/ppermute | solution.py:1080
  75.4 3.8 %copy-start.4 = (bf16[4,1024,384]{2,1,0:T(8,128)(2,1)}, bf16[4,1024,384]{2,1,0:T(8,128)(2,1)S(1)}, u32[]{:S(2)}) copy-start(bf16[4,1024,384]{2,1,0:T(8,128)(2,1)S(1)} %get-tuple-element.110.grads) | copy-start | bytes 9437188
  75.5 3.7 %copy-start.9 = (bf16[512,512]{1,0:T(8,128)(2,1)}, bf16[512,512]{1,0:T(8,128)(2,1)S(1)}, u32[]{:S(2)}) copy-start(bf16[512,512]{1,0:T(8,128)(2,1)S(1)} %collective-permute-done.11.refs_6_) | copy-start | bytes 1572868
  75.5 2.4 %collective-permute-start.13 = (bf16[256,1536]{1,0:T(8,128)(2,1)S(1)}, bf16[256,1536]{1,0:T(8,128)(2,1)S(1)}, u32[]{:S(2)}, u32[]{:S(2)}) collective-permute-start(bf16[256,1536]{1,0:T(8,128)(2,1)S(1)} %get-tuple-element.101), channel_id=1, source_target_pairs={{0,1},{1,0},{2,3},{3,2},{4,5},{5,4},{6,7},{7,6},{8,9},{9,8},{10,11... | collective-permute-start | bytes 2359304 | tf_op jit(solution)/shard_map/reduce/ppermute | solution.py:1080
  75.6 7.4 %collective-permute-start.14 = (bf16[256,512]{1,0:T(8,128)(2,1)S(1)}, bf16[256,512]{1,0:T(8,128)(2,1)S(1)}, u32[]{:S(2)}, u32[]{:S(2)}) collective-permute-start(bf16[256,512]{1,0:T(8,128)(2,1)S(1)} %slice.6), channel_id=1, source_target_pairs={{0,8},{8,16},{16,24},{24,28},{28,20},{20,12},{12,4},{4,0},{1,9},{9... | collective-permute-start | bytes 786440 | tf_op jit(solution)/shard_map/gather_for_weights/ppermute | solution.py:1068
  75.7 7.3 %collective-permute-start.15 = (bf16[256,512]{1,0:T(8,128)(2,1)S(1)}, bf16[256,512]{1,0:T(8,128)(2,1)S(1)}, u32[]{:S(2)}, u32[]{:S(2)}) collective-permute-start(bf16[256,512]{1,0:T(8,128)(2,1)S(1)} %slice.7), channel_id=1, source_target_pairs={{8,0},{16,8},{24,16},{28,24},{20,28},{12,20},{4,12},{0,4},{9,1},{1... | collective-permute-start | bytes 786440 | tf_op jit(solution)/shard_map/gather_for_weights/ppermute | solution.py:1068
  77.8 12.7 %copy-start = (bf16[512,512]{1,0:T(8,128)(2,1)S(1)}, bf16[512,512]{1,0:T(8,128)(2,1)}, u32[]{:S(2)}) copy-start(bf16[512,512]{1,0:T(8,128)(2,1)} %w_query_far.5) | copy-start | bytes 1572868
  77.8 12.7 %copy-start.1 = (bf16[512,512]{1,0:T(8,128)(2,1)S(1)}, bf16[512,512]{1,0:T(8,128)(2,1)}, u32[]{:S(2)}) copy-start(bf16[512,512]{1,0:T(8,128)(2,1)} %w_key_far.5) | copy-start | bytes 1572868
  77.8 12.7 %copy-start.2 = (bf16[512,512]{1,0:T(8,128)(2,1)S(1)}, bf16[512,512]{1,0:T(8,128)(2,1)}, u32[]{:S(2)}) copy-start(bf16[512,512]{1,0:T(8,128)(2,1)} %w_value_far.5) | copy-start | bytes 1572868
  77.8 12.7 %copy-start.16 = (f32[512]{0:T(512)S(1)}, f32[512]{0:T(512)}, u32[]{:S(2)}) copy-start(f32[512]{0:T(512)} %param.16) | copy-start | bytes 6148
  83.7 32.9 %all-to-all-start = ((bf16[16,16,2176]{2,1,0:T(8,128)(2,1)}), bf16[16,16,2176]{2,1,0:T(8,128)(2,1)S(1)}, u32[]{:S(2)}, u32[]{:S(2)}) async-start(bf16[16,16,2176]{2,1,0:T(8,128)(2,1)} %bitcast.5), calls=%async_computation | async-start | bytes 2228224 | tf_op jit(solution)/shard_map/reduce/all_to_all | solution.py:1084
  90.6 1.9 %copy-start.5 = (bf16[4,1024,384]{2,1,0:T(8,128)(2,1)S(1)}, bf16[4,1024,384]{2,1,0:T(8,128)(2,1)}, u32[]{:S(2)}) copy-start(bf16[4,1024,384]{2,1,0:T(8,128)(2,1)} %copy-done.4) | copy-start | bytes 9437188
  92.4 1.6 %copy-start.7 = (f32[1024,512]{1,0:T(8,128)S(1)}, f32[1024,512]{1,0:T(8,128)}, u32[]{:S(2)}) copy-start(f32[1024,512]{1,0:T(8,128)} %copy-done.6) | copy-start | bytes 6291460
  94.0 1.2 copy-start.8
  95.3 4.1 %copy-start.10 = (bf16[512,512]{1,0:T(8,128)(2,1)S(1)}, bf16[512,512]{1,0:T(8,128)(2,1)}, u32[]{:S(2)}) copy-start(bf16[512,512]{1,0:T(8,128)(2,1)} %copy-done.9) | copy-start | bytes 1572868
  95.3 4.1 %copy-start.14 = (bf16[512,512]{1,0:T(8,128)(2,1)S(1)}, bf16[512,512]{1,0:T(8,128)(2,1)}, u32[]{:S(2)}) copy-start(bf16[512,512]{1,0:T(8,128)(2,1)} %copy-done.13) | copy-start | bytes 1572868
  95.3 4.1 %copy-start.18 = (bf16[2,512,2048]{2,1,0:T(8,128)(2,1)S(1)}, bf16[2,512,2048]{2,1,0:T(8,128)(2,1)}, u32[]{:S(2)}) copy-start(bf16[2,512,2048]{2,1,0:T(8,128)(2,1)} %refs_9_.3) | copy-start | bytes 12582916
  95.3 4.1 %copy-start.26 = (bf16[512,512]{1,0:T(8,128)(2,1)S(1)}, bf16[512,512]{1,0:T(8,128)(2,1)}, u32[]{:S(2)}) copy-start(bf16[512,512]{1,0:T(8,128)(2,1)} %copy-done.25) | copy-start | bytes 1572868
  95.3 4.1 %copy-start.29 = (bf16[512,512]{1,0:T(8,128)(2,1)S(1)}, bf16[512,512]{1,0:T(8,128)(2,1)}, u32[]{:S(2)}) copy-start(bf16[512,512]{1,0:T(8,128)(2,1)} %copy-done.28) | copy-start | bytes 1572868
  95.3 4.1 %copy-start.32 = (bf16[512,512]{1,0:T(8,128)(2,1)S(1)}, bf16[512,512]{1,0:T(8,128)(2,1)}, u32[]{:S(2)}) copy-start(bf16[512,512]{1,0:T(8,128)(2,1)} %copy-done.31) | copy-start | bytes 1572868
  95.3 4.1 %copy-start.35 = (bf16[512,512]{1,0:T(8,128)(2,1)S(1)}, bf16[512,512]{1,0:T(8,128)(2,1)}, u32[]{:S(2)}) copy-start(bf16[512,512]{1,0:T(8,128)(2,1)} %copy-done.34) | copy-start | bytes 1572868
  95.3 4.1 %copy-start.38 = (bf16[256,512]{1,0:T(8,128)(2,1)S(1)}, bf16[256,512]{1,0:T(8,128)(2,1)}, u32[]{:S(2)}) copy-start(bf16[256,512]{1,0:T(8,128)(2,1)} %copy-done.37) | copy-start | bytes 786436
  99.4 2.2 %copy-start.21 = (bf16[2,2048,512]{2,1,0:T(8,128)(2,1)S(1)}, bf16[2,2048,512]{2,1,0:T(8,128)(2,1)}, u32[]{:S(2)}) copy-start(bf16[2,2048,512]{2,1,0:T(8,128)(2,1)} %refs_10_.3) | copy-start | bytes 12582916
  117.8 30.1 %all-to-all-start.1 = ((bf16[16,16,2176]{2,1,0:T(8,128)(2,1)}), bf16[16,16,2176]{2,1,0:T(8,128)(2,1)S(1)}, u32[]{:S(2)}, u32[]{:S(2)}) async-start(bf16[16,16,2176]{2,1,0:T(8,128)(2,1)} %copy-done.3), calls=%async_computation.1 | async-start | bytes 2228224 | tf_op jit(solution)/shard_map/reduce/all_to_all | solution.py:1087
  121.8 1.0 copy-start.11
  122.9 1.0 copy-start.15
  123.9 2.2 %copy-start.19 = (bf16[2,512,2048]{2,1,0:T(8,128)(2,1)S(1)}, bf16[2,512,2048]{2,1,0:T(8,128)(2,1)}, u32[]{:S(2)}) copy-start(bf16[2,512,2048]{2,1,0:T(8,128)(2,1)} %refs_9_.3) | copy-start | bytes 12582916
  126.1 2.2 %copy-start.22 = (bf16[2,2048,512]{2,1,0:T(8,128)(2,1)S(1)}, bf16[2,2048,512]{2,1,0:T(8,128)(2,1)}, u32[]{:S(2)}) copy-start(bf16[2,2048,512]{2,1,0:T(8,128)(2,1)} %refs_10_.3) | copy-start | bytes 12582916
  128.3 1.0 copy-start.27
  129.3 1.0 copy-start.30
  130.4 1.0 copy-start.33
  131.4 1.0 copy-start.36
  148.0 4.9 %collective-permute-start.16 = (bf16[256,2176]{1,0:T(8,128)(2,1)S(1)}, bf16[256,2176]{1,0:T(8,128)(2,1)S(1)}, u32[]{:S(2)}, u32[]{:S(2)}) collective-permute-start(bf16[256,2176]{1,0:T(8,128)(2,1)S(1)} %bitcast.11), channel_id=1, source_target_pairs={{0,1},{1,0},{2,3},{3,2},{4,5},{5,4},{6,7},{7,6},{8,9},{9,8},{10,11... | collective-permute-start | bytes 3342344 | tf_op jit(solution)/shard_map/reduce/ppermute | solution.py:1080
  (4 other events, 3.6 us)
